TPU v7x, 32 devices: a whole 2x2x4 slice. The times are simulated.
32 devices in a mesh: dom: 8 (over z, x), row: 4 (over y, core).
Axes of the slice: x: 2, y: 2, z: 4, core: 2. Of those that a mesh axis runs over, the one named last changes fastest.
Arguments:
- features: bfloat16 [16384, 2048], P(('dom', 'row')), may hold values from -6 to 6
- adjacency: bfloat16 [16384, 2048], P(('dom', 'row')), as said below
- tile_values: bfloat16 [2048, 128, 128], P(('dom', 'row')), as said below
- tile_block: int32 [2048], P(('dom', 'row')), may hold values from 0 to 3
- tile_slot: int32 [2048], P(('dom', 'row')), may hold values from 0 to 7, as said below
- tile_count: int32 [32], P(('dom', 'row')), may hold values from 16 to 64
- send_block: int32 [32, 8], P(('dom', 'row')), may hold values from -1 to 3, as said below
- node_mask: int32 [16384], P(('dom', 'row')), may hold values from 0 to 1, as said below
- weight: float32 [2048, 2048], P('row')
- params: float32 [3, 2048], replicated
- weight_first: float32 [2048, 2048], P('row')
- weight_second: float32 [2048, 2048], P('row'), as said below
- params_first: float32 [3, 2048], replicated
- params_second: float32 [3, 2048], replicated, as said below
- cotangent: bfloat16 [16384, 2048], P(('dom', 'row')), may hold values from -6 to 6
Outputs:
- output: bfloat16 [16384, 2048], P(('dom', 'row'))
- grad_features: bfloat16 [16384, 2048], P(('dom', 'row'))
- weight_new: float32 [2048, 2048], P('row')
- weight_low: bfloat16 [2048, 2048], P('row')
- weight_first_new: float32 [2048, 2048], P('row')
- weight_second_new: float32 [2048, 2048], P('row')
- params_new: float32 [3, 2048], replicated
- params_first_new: float32 [3, 2048], replicated
- params_second_new: float32 [3, 2048], replicated
- norms: float32 [4, 2], replicated
Inputs may be any that keep to these rules, and one draw needn't show every extreme that they name: The adjacency entries are nonnegative; the entry of a node against itself is positive. `tile_values`: the tile entries are nonnegative. `send_block`: entry (p, q) names a row block of device p, or is -1; it is -1 where q is p's own dom index. `tile_slot`: A tile of device (q, r) reads from a dom index d whose device (d, r) sends a block to q. `node_mask`: the first node of every device counts. `weight_second`: second moments are positive. `params_second`: second moments are positive.
All inputs are finite; a program needn't handle non-finite values.
Results may differ from a plain program's by a relative error of at most 0.0081.
Values may be sent and summed in bfloat16 or wider, within the bound.
No kernel may reach another device: no remote copies, remote signals or barrier semaphores. Data moves between devices by JAX's collectives and lax.ppermute only.
A program may use at most 384 MiB of HBM per device.

v0:
```python
import jax
import jax.numpy as jnp
from jax import lax
from jax.sharding import PartitionSpec as P

STEP = 5


SELF_LOOP = 1.0
NORM_EPS = 1e-05
DECAY_FIRST = 0.5
DECAY_SECOND = 0.5
ADAM_EPS = 1e-06
WEIGHT_DECAY = 0.01
LEARN_RATE = 0.5
TRUST_EPS = 1e-06
PRECISE = lax.Precision.HIGHEST


def lamb_step(value, grad, first, second, decay):
    first_new = DECAY_FIRST * first + (1.0 - DECAY_FIRST) * grad
    second_new = DECAY_SECOND * second + (1.0 - DECAY_SECOND) * grad * grad
    update = (
        first_new
        / (1.0 - DECAY_FIRST**STEP)
        / (jnp.sqrt(second_new / (1.0 - DECAY_SECOND**STEP)) + ADAM_EPS)
        + decay * value
    )
    return (first_new, second_new, update)


def on_device(
    features,
    adjacency,
    tile_values,
    tile_block,
    tile_slot,
    tile_count,
    send_block,
    node_mask,
    weight,
    params,
    weight_first,
    weight_second,
    params_first,
    params_second,
    cotangent,
):
    row_count, feat_width = features.shape
    tile_total = tile_values.shape[0]
    block_rows = tile_values.shape[1]
    blocks = row_count // block_rows
    peer_count = lax.axis_size("dom")
    member = lax.axis_index("row")
    shard_rows = weight.shape[0]
    full_weight = lax.all_gather(weight.astype(jnp.bfloat16), "row", axis=0, tiled=True)
    columns = adjacency
    intra = jnp.dot(
        columns,
        lax.all_gather(features, "row", axis=0, tiled=True),
        preferred_element_type=jnp.float32,
    )
    own_columns = lax.dynamic_slice_in_dim(adjacency, member * row_count, row_count, 1)
    self_weight = SELF_LOOP * jnp.diagonal(own_columns).astype(jnp.float32)
    chooser = (send_block[0][:, None] == jnp.arange(blocks, dtype=jnp.int32)[None, :]).astype(
        jnp.bfloat16
    )
    feature_blocks = features.reshape(blocks, block_rows, feat_width)
    outgoing = jnp.einsum(
        "qb,bkf->qkf", chooser, feature_blocks, preferred_element_type=jnp.float32
    ).astype(jnp.bfloat16)
    incoming = lax.all_to_all(
        outgoing.reshape(peer_count * block_rows, feat_width),
        "dom",
        split_axis=0,
        concat_axis=0,
        tiled=True,
    ).reshape(peer_count, block_rows, feat_width)
    live_flags = (jnp.arange(tile_total, dtype=jnp.int32) < tile_count[0]).astype(jnp.float32)
    slot_table = (tile_slot[:, None] == jnp.arange(peer_count, dtype=jnp.int32)[None, :]).astype(
        jnp.float32
    )
    block_table = (tile_block[:, None] == jnp.arange(blocks, dtype=jnp.int32)[None, :]).astype(
        jnp.float32
    )
    slot_pick = slot_table.astype(jnp.bfloat16)
    block_pick = block_table.astype(jnp.bfloat16)
    live_slots = slot_table * live_flags[:, None]
    live_blocks = block_table * live_flags[:, None]
    picked = jnp.einsum(
        "td,dkf->tkf", slot_pick, incoming, preferred_element_type=jnp.float32
    ).astype(jnp.bfloat16)
    products = jnp.einsum("tij,tjf->tif", tile_values, picked, preferred_element_type=jnp.float32)
    halo_sum = jnp.einsum("tb,tif->bif", live_blocks, products, precision=PRECISE).reshape(
        row_count, feat_width
    )
    hidden = (intra + self_weight[:, None] * features.astype(jnp.float32) + halo_sum).astype(
        jnp.bfloat16
    )
    preact = jnp.dot(hidden, full_weight, preferred_element_type=jnp.float32) + params[0]
    activated = jax.nn.gelu(preact)
    mask_col = node_mask.astype(jnp.float32)[:, None]
    node_count, first_sum = lax.psum(
        (jnp.sum(mask_col), jnp.sum(mask_col * activated, axis=0)), ("dom", "row")
    )
    mean_act = first_sum / node_count
    centred = activated - mean_act
    variance = lax.psum(jnp.sum(mask_col * centred * centred, axis=0), ("dom", "row")) / node_count
    inverse = lax.rsqrt(variance + NORM_EPS)
    normed = centred * inverse
    output = (mask_col * (params[1] * normed + params[2])).astype(jnp.bfloat16)
    grad_out = mask_col * cotangent.astype(jnp.float32)
    shift_grad, scale_grad = lax.psum(
        (jnp.sum(grad_out, axis=0), jnp.sum(grad_out * normed, axis=0)), ("dom", "row")
    )
    grad_act = (
        mask_col
        * (params[1] * inverse)
        * (grad_out - (shift_grad + normed * scale_grad) / node_count)
    )
    gelu_back = jax.vjp(jax.nn.gelu, preact)[1]
    grad_pre = gelu_back(grad_act)[0].astype(jnp.bfloat16)
    bias_local = jnp.sum(grad_pre.astype(jnp.float32), axis=0)
    weight_local = jnp.einsum("rf,rg->fg", hidden, grad_pre, preferred_element_type=jnp.float32)
    grad_hidden = jnp.einsum(
        "rg,fg->rf", grad_pre, full_weight, preferred_element_type=jnp.float32
    ).astype(jnp.bfloat16)
    columns = adjacency
    grad_intra = lax.psum_scatter(
        jnp.einsum("rp,rf->pf", columns, grad_hidden, preferred_element_type=jnp.float32),
        "row",
        scatter_dimension=0,
        tiled=True,
    )
    hidden_rows = jnp.einsum(
        "tb,bkf->tkf",
        block_pick,
        grad_hidden.reshape(blocks, block_rows, feat_width),
        preferred_element_type=jnp.float32,
    ).astype(jnp.bfloat16)
    back_terms = jnp.einsum(
        "tij,tif->tjf", tile_values, hidden_rows, preferred_element_type=jnp.float32
    )
    slot_grads = jnp.einsum("td,tjf->djf", live_slots, back_terms, precision=PRECISE).astype(
        jnp.bfloat16
    )
    returned = lax.all_to_all(
        slot_grads.reshape(peer_count * block_rows, feat_width),
        "dom",
        split_axis=0,
        concat_axis=0,
        tiled=True,
    ).reshape(peer_count, block_rows, feat_width)
    grad_halo = jnp.einsum(
        "qb,qkf->bkf", chooser, returned, preferred_element_type=jnp.float32
    ).reshape(row_count, feat_width)
    grad_features = (
        grad_intra + self_weight[:, None] * grad_hidden.astype(jnp.float32) + grad_halo
    ).astype(jnp.bfloat16)
    weight_total, bias_grad = lax.psum((weight_local, bias_local), ("dom", "row"))
    weight_grad = lax.dynamic_slice_in_dim(weight_total, member * shard_rows, shard_rows, 0)
    weight_first_new, weight_second_new, weight_update = lamb_step(
        weight, weight_grad, weight_first, weight_second, WEIGHT_DECAY
    )
    squares = jnp.stack([jnp.sum(weight * weight), jnp.sum(weight_update * weight_update)])
    squares = lax.psum(squares, "row")
    weight_norms = jnp.sqrt(squares)
    weight_new = (
        weight - LEARN_RATE * (weight_norms[0] / (weight_norms[1] + TRUST_EPS)) * weight_update
    )
    param_grads = jnp.stack([bias_grad, scale_grad, shift_grad])
    params_first_new, params_second_new, param_update = lamb_step(
        params, param_grads, params_first, params_second, 0.0
    )
    param_norms = jnp.sqrt(jnp.sum(params * params, axis=1, keepdims=True))
    update_norms = jnp.sqrt(jnp.sum(param_update * param_update, axis=1, keepdims=True))
    params_new = params - LEARN_RATE * (param_norms / (update_norms + TRUST_EPS)) * param_update
    norms = jnp.concatenate(
        [weight_norms[None, :], jnp.concatenate([param_norms, update_norms], axis=1)], axis=0
    )
    return (
        output,
        grad_features,
        weight_new,
        weight_new.astype(jnp.bfloat16),
        weight_first_new,
        weight_second_new,
        params_new,
        params_first_new,
        params_second_new,
        norms,
    )


def solution(mesh):
    in_specs = (
        P(("dom", "row"), None),
        P(("dom", "row"), None),
        P(("dom", "row"), None, None),
        P(("dom", "row")),
        P(("dom", "row")),
        P(("dom", "row")),
        P(("dom", "row"), None),
        P(("dom", "row")),
        P("row", None),
        P(),
        P("row", None),
        P("row", None),
        P(),
        P(),
        P(("dom", "row"), None),
    )
    out_specs = (
        P(("dom", "row"), None),
        P(("dom", "row"), None),
        P("row", None),
        P("row", None),
        P("row", None),
        P("row", None),
        P(),
        P(),
        P(),
        P(),
    )
    return jax.shard_map(
        on_device, mesh=mesh, in_specs=in_specs, out_specs=out_specs, check_vma=False
    )
```

profile of v0, /device:TPU:0, one launch (start us, length us, event | category | flops | bytes accessed | tf_op | source)
XLA Modules:
  0.0 984.2 jit_solution(7578531470991578254)
XLA Ops:
  16.0 7.3 all-to-all-start
  34.9 81.6 %all-to-all-done = bf16[8,128,2048]{2,1,0:T(8,128)(2,1)} async-done(((bf16[8,128,2048]{2,1,0:T(8,128)(2,1)}), bf16[8,128,2048]{2,1,0:T(8,128)(2,1)}, u32[]{:S(2)}, u32[]{:S(2)}) %all-to-all-start) | async-done | bytes 4194336 | tf_op jit(solution)/shard_map/all_to_all | solution.py:72
  116.6 16.2 %convolution_convert_fusion = bf16[64,128,2048]{2,0,1:T(8,128)(2,1)} fusion(bf16[8,128,2048]{2,1,0:T(8,128)(2,1)} %all-to-all-done, s32[64]{0:T(128)S(1)} %copy-done.13), kind=kOutput, calls=%fused_computation.7 | convolution fusion | flops 285214208 | bytes 37748992 | tf_op jit(solution)/shard_map/td,dkf->tkf/dot_general | solution.py:90
  132.8 59.0 %fusion.4 = f32[64,128,2048]{1,2,0:T(8,128)} fusion(bf16[64,128,128]{2,1,0:T(8,128)(2,1)S(1)} %copy-done, bf16[64,128,2048]{2,0,1:T(8,128)(2,1)} %convolution_convert_fusion), kind=kOutput, calls=%fused_computation.5 | convolution fusion | flops 4294967296 | bytes 102760448 | tf_op jit(solution)/shard_map/tij,tjf->tif/dot_general | solution.py:93
  191.8 71.3 %copy.49 = f32[64,128,2048]{2,0,1:T(8,128)} copy(f32[64,128,2048]{1,2,0:T(8,128)} %fusion.4) | data formatting | bytes 134217728 | tf_op jit(solution)/shard_map/tij,tjf->tif/dot_general | solution.py:93
  263.1 36.1 %fusion.32 = f32[4,128,2048]{2,0,1:T(4,128)S(1)} fusion(f32[64,128,2048]{2,0,1:T(8,128)} %copy.49, f32[64]{0:T(128)S(1)} %compare_convert_fusion, s32[64]{0:T(128)S(1)} %copy-done.12), kind=kOutput, calls=%fused_computation.63 | convolution fusion | flops 805306880 | bytes 71303680 | tf_op jit(solution)/shard_map/tb,tif->bif/dot_general | solution.py:94
  303.6 11.6 %fusion.20 = bf16[512,2048]{1,0:T(8,128)(2,1)} fusion(f32[4,128,2048]{2,1,0:T(8,128)} %copy.50, bf16[512,2048]{1,0:T(8,128)(2,1)} %param.15, bf16[512,2048]{1,0:T(8,128)(2,1)} %param.16, bf16[2048,2048]{1,0:T(8,128)(2,1)} %all-gather.3.cloned.1.call-done, f32[512]{0:T(512)S(1)} %convert_element_type.76), kind=kOutput, calls=%fused_computation.27 | convolution fusion | flops 4300210176 | bytes 18876416 | tf_op jit(solution)/shard_map/dot_general | solution.py:58
  315.3 11.6 %multiply_reduce_fusion.3 = (f32[2048]{0:T(1024)S(1)}, f32[512,2048]{1,0:T(8,128)}) fusion(f32[512]{0:T(512)S(1)} %convert_element_type.75, f32[2048]{0:T(1024)S(1)} %bitcast.74, bf16[512,2048]{1,0:T(8,128)(2,1)} %fusion.20, bf16[2048,2048]{1,0:T(8,128)(2,1)} %all-gather.5.cloned.1.call-done), kind=kOutput, calls=%fused_computation.40 | convolution fusion | flops 4306499584 | bytes 14698496 | tf_op jit(solution)/shard_map/dot_general | solution.py:100
  326.8 38.0 %all-reduce.1 = (f32[2048]{0:T(1024)S(1)}, f32[]{:T(128)}) all-reduce(f32[2048]{0:T(1024)S(1)} %get-tuple-element.42, f32[]{:T(128)} %convert_reduce_fusion.1), channel_id=1, replica_groups=mesh['dom'=8,'row'=4] {'dom','row'}, use_global_device_ids=true, to_apply=%region_1.2 | all-reduce | flops 2049 | bytes 16392 | tf_op jit(solution)/shard_map/psum | solution.py:103
  369.1 42.1 %psum.58 = f32[2048]{0:T(1024)S(1)} all-reduce(f32[2048]{0:T(1024)S(1)} %fusion.18), channel_id=1, replica_groups=mesh['dom'=8,'row'=4] {'dom','row'}, use_global_device_ids=true, to_apply=%region_5.6 | all-reduce | flops 2048 | bytes 16384 | tf_op jit(solution)/shard_map/psum | solution.py:108
  416.3 39.5 %all-reduce = (f32[2048]{0:T(1024)S(1)}, f32[2048]{0:T(1024)S(1)}) all-reduce(f32[2048]{0:T(1024)S(1)} %get-tuple-element.13, f32[2048]{0:T(1024)S(1)} %get-tuple-element.12), channel_id=1, replica_groups=mesh['dom'=8,'row'=4] {'dom','row'}, use_global_device_ids=true, to_apply=%region_9.10 | all-reduce | flops 4096 | bytes 32768 | tf_op jit(solution)/shard_map/psum | solution.py:113
  455.8 8.7 convert_reduce_fusion
  465.8 8.1 fusion.60
  474.0 8.7 convolution_convert_fusion.4
  484.0 8.5 convolution_bitcast_fusion
  492.5 15.9 %convolution_convert_fusion.1 = bf16[64,128,2048]{2,0,1:T(8,128)(2,1)} fusion(bf16[4,128,2048]{2,1,0:T(8,128)(2,1)} %bitcast.72, s32[64]{0:T(128)S(1)} %copy-done.12), kind=kOutput, calls=%fused_computation.8 | convolution fusion | flops 150995712 | bytes 35651840 | tf_op jit(solution)/shard_map/tb,bkf->tkf/dot_general | solution.py:135
  508.4 58.8 %fusion.7 = f32[64,128,2048]{1,2,0:T(8,128)} fusion(bf16[64,128,128]{2,1,0:T(8,128)(2,1)S(1)} %copy-done, bf16[64,128,2048]{2,0,1:T(8,128)(2,1)} %convolution_convert_fusion.1), kind=kOutput, calls=%fused_computation.6 | convolution fusion | flops 4294967296 | bytes 102760448 | tf_op jit(solution)/shard_map/tij,tif->tjf/dot_general | solution.py:141
  567.2 72.0 %copy.54 = f32[64,128,2048]{2,0,1:T(8,128)} copy(f32[64,128,2048]{1,2,0:T(8,128)} %fusion.7) | data formatting | bytes 134217728 | tf_op jit(solution)/shard_map/tij,tif->tjf/dot_general | solution.py:141
  639.2 37.6 %convolution_convert_fusion.2 = bf16[8,128,2048]{2,0,1:T(8,128)(2,1)S(1)} fusion(f32[64,128,2048]{2,0,1:T(8,128)} %copy.54, f32[64]{0:T(128)S(1)} %compare_convert_fusion, s32[64]{0:T(128)S(1)} %copy-done.14), kind=kOutput, calls=%fused_computation.43 | convolution fusion | flops 1612710912 | bytes 71303680 | tf_op jit(solution)/shard_map/td,tjf->djf/dot_general | solution.py:144
  686.4 158.0 %psum.63 = f32[1,2048]{1,0:T(1,128)S(1)} all-reduce(f32[1,2048]{1,0:T(1,128)S(1)} %bitcast.82), channel_id=1, replica_groups=mesh['dom'=8,'row'=4] {'dom','row'}, use_global_device_ids=true, to_apply=%region_17.18 | all-reduce | flops 2048 | bytes 16384 | tf_op jit(solution)/shard_map/psum | solution.py:160
  846.0 7.8 fusion.21
  853.8 15.5 %multiply_reduce_fusion.1 = (f32[]{:T(128)}, f32[]{:T(128)}, f32[512,2048]{1,0:T(8,128)}, f32[512,2048]{1,0:T(8,128)}) fusion(f32[512,2048]{1,0:T(8,128)} %param.23, f32[2048,2048]{1,0:T(8,128)} %all-reduce.4.cloned.1.call-done, s32[]{:T(128)S(6)} %select_n.8, f32[512,2048]{1,0:T(8,128)} %param.25, f32[512,2048]{1,0:T(8,128)} %param.26), kind=kLoop, calls=%fused_computation.35 | loop fusion | flops 16777214 | bytes 25165836 | tf_op jit(solution)/shard_map/reduce_sum | solution.py:165
  884.1 9.9 %fusion.55 = (bf16[512,2048]{1,0:T(8,128)(2,1)}, f32[512,2048]{1,0:T(8,128)}) fusion(f32[512,2048]{1,0:T(8,128)} %param.23, f32[512,2048]{1,0:T(8,128)} %get-tuple-element.27, f32[512,2048]{1,0:T(8,128)} %get-tuple-element.26, f32[]{:T(128)} %bitcast.20), kind=kLoop, calls=%fused_computation.94 | loop fusion | flops 9437184 | bytes 18874372 | tf_op jit(solution)/shard_map/convert_element_type | solution.py:185
  894.0 76.8 %reduce-scatter.2.cloned.1.call-done = f32[512,2048]{1,0:T(8,128)} async-done(((f32[2048,2048]{1,0:T(8,128)}), f32[512,2048]{1,0:T(8,128)}) %reduce-scatter.2.cloned.1.call-update) | async-done | bytes 4194320 | tf_op jit(solution)/shard_map/reduce_scatter | solution.py:129
  (75 shorter events, 67.6 us)
Async XLA Ops:
  7.2 125.6 %copy-start = (bf16[64,128,128]{2,1,0:T(8,128)(2,1)S(1)}, bf16[64,128,128]{2,1,0:T(8,128)(2,1)}, u32[]{:S(2)}) copy-start(bf16[64,128,128]{2,1,0:T(8,128)(2,1)} %param.17) | copy-start | bytes 6291460
  7.2 296.4 %all-gather.3.cloned.1.call-start = ((), (), s32[]{:S(2)}) async-start(), calls=%async_computation.3 | async-start | bytes 10485760 | tf_op jit(solution)/shard_map/all_gather | solution.py:60
  16.0 100.5 %all-to-all-start = ((bf16[8,128,2048]{2,1,0:T(8,128)(2,1)}), bf16[8,128,2048]{2,1,0:T(8,128)(2,1)}, u32[]{:S(2)}, u32[]{:S(2)}) async-start(bf16[8,128,2048]{2,1,0:T(8,128)(2,1)} %copy.46), calls=%async_computation | async-start | bytes 8388608 | tf_op jit(solution)/shard_map/all_to_all | solution.py:72
  23.3 4.4 copy-start.9
  23.3 11.6 %copy-start.4 = (f32[3,2048]{1,0:T(4,128)S(1)}, f32[3,2048]{1,0:T(4,128)}, u32[]{:S(2)}) copy-start(f32[3,2048]{1,0:T(4,128)} %param.24) | copy-start | bytes 73732
  23.3 93.3 %copy-start.13 = (s32[64]{0:T(128)S(1)}, s32[64]{0:T(128)}, u32[]{:S(2)}) copy-start(s32[64]{0:T(128)} %param.19) | copy-start | bytes 772
  23.3 292.0 %all-gather.5.cloned.1.call-start = ((), (), s32[]{:S(2)}) async-start(), calls=%async_computation.4 | async-start | bytes 10485760 | tf_op jit(solution)/shard_map/all_gather | solution.py:56
  27.6 826.2 %all-reduce.4.cloned.1.call-start = ((), (), s32[]{:S(2)}) async-start(), calls=%async_computation.6 | async-start | bytes 33554432 | tf_op jit(solution)/shard_map/psum | solution.py:160
  34.3 269.4 %copy-start.10 = (f32[512]{0:T(512)}, f32[512]{0:T(512)S(1)}, u32[]{:S(2)}) copy-start(f32[512]{0:T(512)S(1)} %convert_element_type.76) | copy-start | bytes 6148
  191.8 71.3 %copy-start.12 = (s32[64]{0:T(128)S(1)}, s32[64]{0:T(128)}, u32[]{:S(2)}) copy-start(s32[64]{0:T(128)} %param.18) | copy-start | bytes 772
  455.8 10.0 %copy-start.16 = (bf16[512,2048]{1,0:T(8,128)(2,1)S(1)}, bf16[512,2048]{1,0:T(8,128)(2,1)}, u32[]{:S(2)}) copy-start(bf16[512,2048]{1,0:T(8,128)(2,1)} %fusion.20) | copy-start | bytes 6291460
  464.5 1.3 copy-start.3
  473.9 496.8 %reduce-scatter.2.cloned.1.call-start = ((), (), s32[]{:S(2)}) async-start(), calls=%async_computation.5 | async-start | bytes 20971520 | tf_op jit(solution)/shard_map/reduce_scatter | solution.py:129
  474.0 10.0 %copy-start.6 = (bf16[512,2048]{1,0:T(8,128)(2,1)S(1)}, bf16[512,2048]{1,0:T(8,128)(2,1)}, u32[]{:S(2)}) copy-start(bf16[512,2048]{1,0:T(8,128)(2,1)} %param.16) | copy-start | bytes 6291460
  482.7 1.3 copy-start.2
  567.2 72.0 %copy-start.14 = (s32[64]{0:T(128)S(1)}, s32[64]{0:T(128)}, u32[]{:S(2)}) copy-start(s32[64]{0:T(128)} %param.19) | copy-start | bytes 772
  681.1 163.3 %copy-start.5 = (f32[3,2048]{1,0:T(4,128)S(1)}, f32[3,2048]{1,0:T(4,128)}, u32[]{:S(2)}) copy-start(f32[3,2048]{1,0:T(4,128)} %param.24) | copy-start | bytes 73732
  681.1 163.3 %copy-start.7 = (f32[3,2048]{1,0:T(4,128)S(1)}, f32[3,2048]{1,0:T(4,128)}, u32[]{:S(2)}) copy-start(f32[3,2048]{1,0:T(4,128)} %param.27) | copy-start | bytes 73732
  681.1 163.3 %copy-start.8 = (f32[3,2048]{1,0:T(4,128)S(1)}, f32[3,2048]{1,0:T(4,128)}, u32[]{:S(2)}) copy-start(f32[3,2048]{1,0:T(4,128)} %param.28) | copy-start | bytes 73732
  681.1 164.9 %copy-start.15 = (s32[1,8]{1,0:T(1,128)S(1)}, s32[1,8]{1,0:T(1,128)}, u32[]{:S(2)}) copy-start(s32[1,8]{1,0:T(1,128)} %param.21) | copy-start | bytes 100
  681.1 164.9 %all-to-all-start.1 = ((bf16[8,128,2048]{2,1,0:T(8,128)(2,1)}), bf16[8,128,2048]{2,1,0:T(8,128)(2,1)}, u32[]{:S(2)}, u32[]{:S(2)}) async-start(bf16[8,128,2048]{2,1,0:T(8,128)(2,1)} %copy.55), calls=%async_computation.2 | async-start | bytes 8388608 | tf_op jit(solution)/shard_map/all_to_all | solution.py:147
  853.7 16.9 %copy-start.1 = (f32[4,128,2048]{2,0,1:T(4,128)S(1)}, f32[4,128,2048]{2,0,1:T(4,128)}, u32[]{:S(2)}) copy-start(f32[4,128,2048]{2,0,1:T(4,128)} %fusion.21) | copy-start | bytes 12582916
  884.1 86.7 %copy-start.11 = (f32[512]{0:T(512)S(1)}, f32[512]{0:T(512)}, u32[]{:S(2)}) copy-start(f32[512]{0:T(512)} %copy-done.10) | copy-start | bytes 6148
Sparse Core Ops, SparseCore 0:
  9.6 60.9 all-gather.2
  72.7 58.2 all-gather.4
  474.1 368.0 all-reduce.3
  844.6 126.1 reduce-scatter.1
where the time goes:
time: 993 us; the launch traced here: 984 us
  matrix products  284 us (29%)
  blocking collectives  284 us (29%)
  local copies, waits for them, and re-layouts  170 us (17%)
  waiting for transfers between devices  159 us (16%)
  other arithmetic  58.6 us (6%)
  between operations  16.2 us (2%)
  starting transfers between devices  12.8 us (1%)
    psum x1, blocking collectives, on_device(): lax.psum((weight_local, bias_local), ('dom', 'row'))  158 us
    all_to_all x1, waiting for transfers between devices, on_device(): lax.all_to_all(outgoing.reshape(peer_count * block_rows, feat_width), 'do...  81.6 us
    reduce_scatter x1, waiting for transfers between devices, on_device(): lax.psum_scatter(jnp.einsum('rp,rf->pf', columns, grad_hidden, preferred_...  76.8 us
    dot_general x1, local copies, waits for them, and re-layouts, on_device(): jnp.einsum('tij,tif->tjf', tile_values, hidden_rows, preferred_element_ty...  72 us
    dot_general x1, local copies, waits for them, and re-layouts, on_device(): jnp.einsum('tij,tjf->tif', tile_values, picked, preferred_element_type=jn...  71.3 us
    dot_general x1, matrix products, on_device(): jnp.einsum('tij,tjf->tif', tile_values, picked, preferred_element_type=jn...  59 us
    dot_general x1, matrix products, on_device(): jnp.einsum('tij,tif->tjf', tile_values, hidden_rows, preferred_element_ty...  58.8 us
    psum x1, blocking collectives, on_device(): lax.psum(jnp.sum(mask_col * centred * centred, axis=0), ('dom', 'row'))  42.1 us
  transfers between devices with their start and end apart: 6, of which 2 were waited for; matrix products, arithmetic and copies ran while one was open for 47% of the time, Pallas kernels for 0%

commit v1 on v0

v1 whole, which is shorter than its diff:
```python
import math

import jax
import jax.numpy as jnp
from jax import lax
from jax.experimental import pallas as pl
from jax.experimental.pallas import tpu as pltpu
from jax.sharding import PartitionSpec as P

STEP = 5


SELF_LOOP = 1.0
NORM_EPS = 1e-05
DECAY_FIRST = 0.5
DECAY_SECOND = 0.5
ADAM_EPS = 1e-06
WEIGHT_DECAY = 0.01
LEARN_RATE = 0.5
TRUST_EPS = 1e-06

AXES = ("dom", "row")
GELU_ROOT = math.sqrt(2.0 / math.pi)
GELU_CUBE = 0.044715
STAT_ROWS = 8
GROUP = 8
WEIGHT_PARTS = 2

ANY_ROWS = (((1,), (0,)), ((), ()))
BOTH_LAST = (((1,), (1,)), ((), ()))


def dot(left, right, dims=ANY_ROWS):
    return lax.dot_general(left, right, dims, preferred_element_type=jnp.float32)


def swap(value, dom_flip, row_flip):
    dom_count, row_count = lax.axis_size("dom"), lax.axis_size("row")
    pairs = [
        (d * row_count + r, (d ^ dom_flip) * row_count + (r ^ row_flip))
        for d in range(dom_count)
        for r in range(row_count)
    ]
    return lax.ppermute(value, AXES, pairs)


def call(kernel, *, flops, nbytes, vmem_mb, **kw):
    return pl.pallas_call(
        kernel,
        cost_estimate=pl.CostEstimate(
            flops=int(flops), bytes_accessed=int(nbytes), transcendentals=0
        ),
        compiler_params=pltpu.CompilerParams(vmem_limit_bytes=vmem_mb << 20),
        **kw,
    )


def spread_rows(value):
    near = swap(value, 0, 1)
    far = swap(value, 0, 2)
    return [value, near, far, swap(far, 0, 1)]


def prepare_kernel(
    me, block_ref, slot_ref, count_ref, adj_ref, tile_ref, wide, flip, halo, halo_flip, total
):
    rows = adj_ref.shape[0]
    row_count = adj_ref.shape[1] // rows
    blocks, peers, side = total.shape[0], total.shape[1], total.shape[2]
    for j in range(row_count):
        start = pl.multiple_of((me[1] ^ j) * rows, rows)
        piece = adj_ref[:, pl.ds(start, rows)]
        if j == 0:
            at_row = lax.broadcasted_iota(jnp.int32, (rows, rows), 0)
            at_col = lax.broadcasted_iota(jnp.int32, (rows, rows), 1)
            wide_piece = piece.astype(jnp.float32)
            piece = jnp.where(at_row == at_col, (1.0 + SELF_LOOP) * wide_piece, wide_piece).astype(
                jnp.bfloat16
            )
        wide[:, j * rows : (j + 1) * rows] = piece
        flip[j * rows : (j + 1) * rows, :] = piece.T
    total[...] = jnp.zeros(total.shape, total.dtype)

    def add(t, carry):
        b = block_ref[t]
        k = slot_ref[t] ^ me[0]
        total[b, k] = total[b, k] + tile_ref[t].astype(jnp.float32)
        return carry

    lax.fori_loop(0, count_ref[0], add, 0)
    for b in range(blocks):
        for k in range(peers):
            piece = total[b, k].astype(jnp.bfloat16)
            halo[b * side : (b + 1) * side, k * side : (k + 1) * side] = piece
            halo_flip[k * side : (k + 1) * side, b * side : (b + 1) * side] = piece.T


def prepare(me, tile_block, tile_slot, tile_count, adjacency, tiles, peers):
    rows, part = adjacency.shape
    side = tiles.shape[1]
    smem = pl.BlockSpec(memory_space=pltpu.SMEM)
    vmem = pl.BlockSpec(memory_space=pltpu.VMEM)
    halo_bytes = rows * peers * side * 2
    bf = jnp.bfloat16
    return call(
        prepare_kernel,
        flops=tiles.size,
        nbytes=2 * (adjacency.size * 6 + tiles.size) + 2 * halo_bytes,
        vmem_mb=20 + (4 * halo_bytes >> 20),
        in_specs=[smem] * 4 + [vmem] * 2,
        out_specs=[vmem] * 4,
        out_shape=[
            jax.ShapeDtypeStruct((rows, part), bf),
            jax.ShapeDtypeStruct((part, rows), bf),
            jax.ShapeDtypeStruct((rows, peers * side), bf),
            jax.ShapeDtypeStruct((peers * side, rows), bf),
        ],
        scratch_shapes=[pltpu.VMEM((rows // side, peers, side, side), jnp.float32)],
        name="prepare",
    )(me, tile_block, tile_slot, tile_count, adjacency, tiles)


def gather_kernel(me, wide, halo, *refs):
    hidden, hidden_flip = refs[-2:]
    near = refs[:-2]
    row_count = wide.shape[1] // wide.shape[0]
    side = near[row_count].shape[0]
    total = dot(wide[...], jnp.concatenate([ref[...] for ref in near[:row_count]], axis=0))
    total += dot(halo[:, side:], jnp.concatenate([ref[...] for ref in near[row_count:]], axis=0))
    low = total.astype(jnp.bfloat16)
    hidden[...] = low
    hidden_flip[...] = low.T


def gather(me, wide, halo, own, arrived):
    rows, width = own[0].shape
    row_count = len(own)
    side = arrived[0].shape[0]
    cols = 256
    per = rows // cols

    def place(i, me):
        return ((i // per) ^ me[1]) * per + i % per

    def place_flip(i, me):
        j = (i // per) ^ me[1]
        return ((j % 2) * (row_count // 2) + j // 2) * per + i % per

    whole = lambda shape: pl.BlockSpec(shape, lambda i, me: (0, 0))
    return call(
        gather_kernel,
        flops=2 * rows * width * (row_count * rows + halo.shape[1]),
        nbytes=2 * (wide.size + halo.size + (row_count + 2) * own[0].size + len(arrived) * side * width),
        vmem_mb=24 + (2 * halo.size * 2 + 2 * len(arrived) * side * cols * 4 >> 20),
        grid_spec=pltpu.PrefetchScalarGridSpec(
            num_scalar_prefetch=1,
            grid=(width // cols,),
            in_specs=[whole(wide.shape), whole(halo.shape)]
            + [pl.BlockSpec((rows, cols), lambda i, me: (0, i))] * row_count
            + [pl.BlockSpec((side, cols), lambda i, me: (0, i))] * len(arrived),
            out_specs=[
                pl.BlockSpec((rows, cols), lambda i, me: (0, place(i, me))),
                pl.BlockSpec((cols, rows), lambda i, me: (place_flip(i, me), 0)),
            ],
        ),
        out_shape=[
            jax.ShapeDtypeStruct((rows, width), jnp.bfloat16),
            jax.ShapeDtypeStruct((width, rows), jnp.bfloat16),
        ],
        name="gather",
    )(me, wide, halo, *own, *arrived)


def gelu_parts(v):
    inner = GELU_ROOT * (v + GELU_CUBE * (v * v * v))
    return jnp.tanh(inner)


def linear_kernel(hidden, params, mask_ref, cot_ref, *refs):
    weights, (preact, stats) = refs[:-2], refs[-2:]
    v = dot(hidden[...], jnp.concatenate([ref[...] for ref in weights], axis=0)) + params[0:1, :]
    preact[...] = v
    act = 0.5 * v * (1.0 + gelu_parts(v))
    mask = mask_ref[...]
    count = jnp.sum(mask)
    mean = jnp.sum(mask * act, axis=0, keepdims=True) / count
    centred = act - mean
    grad = mask * cot_ref[...].astype(jnp.float32)
    stats[0:1, :] = mean
    stats[1:2, :] = jnp.sum(mask * centred * centred, axis=0, keepdims=True)
    stats[2:3, :] = jnp.sum(grad, axis=0, keepdims=True)
    stats[3:4, :] = jnp.sum(grad * centred, axis=0, keepdims=True)
    stats[4:8, :] = jnp.full((4, mean.shape[1]), count, jnp.float32)


def linear(hidden, params, mask, cotangent, weights):
    rows, width = hidden.shape
    cols = 256
    wide = pl.BlockSpec((rows, cols), lambda i: (0, i))
    return call(
        linear_kernel,
        flops=2 * rows * width * width,
        nbytes=2 * width * width + 10 * rows * width,
        vmem_mb=28,
        grid=(width // cols,),
        in_specs=[
            pl.BlockSpec((rows, width), lambda i: (0, 0)),
            pl.BlockSpec((3, cols), lambda i: (0, i)),
            pl.BlockSpec((rows, 1), lambda i: (0, 0)),
            wide,
        ]
        + [pl.BlockSpec((w.shape[0], cols), lambda i: (0, i)) for w in weights],
        out_specs=[wide, pl.BlockSpec((STAT_ROWS, cols), lambda i: (0, i))],
        out_shape=[
            jax.ShapeDtypeStruct((rows, width), jnp.float32),
            jax.ShapeDtypeStruct((STAT_ROWS, width), jnp.float32),
        ],
        name="linear",
    )(hidden, params, mask, cotangent, *weights)


def merged(mine, refs, ordered):
    for i, ref in enumerate(refs):
        ordered[mine ^ i] = ref[...]
    parts = [ordered[i] for i in range(len(refs))]
    count = sum(p[4:5] for p in parts)
    mean = sum(p[4:5] * p[0:1] for p in parts) / count
    spread = sum(p[1:2] + p[4:5] * (p[0:1] - mean) * (p[0:1] - mean) for p in parts)
    shift = sum(p[2:3] for p in parts)
    scale = sum(p[3:4] + (p[0:1] - mean) * p[2:3] for p in parts)
    return mean, spread, shift, scale, count


def merge_kernel(mine, *refs):
    out, ordered = refs[-2:]
    for i, row in enumerate(merged(mine[0], refs[:-2], ordered)):
        out[i : i + 1, :] = row
    out[5:8, :] = jnp.zeros((3, out.shape[1]), jnp.float32)


def merge(mine, parts):
    vmem = pl.BlockSpec(memory_space=pltpu.VMEM)
    return call(
        merge_kernel,
        flops=20 * parts[0].size * len(parts),
        nbytes=4 * parts[0].size * len(parts),
        vmem_mb=8,
        in_specs=[pl.BlockSpec(memory_space=pltpu.SMEM)] + [vmem] * len(parts),
        out_specs=vmem,
        out_shape=jax.ShapeDtypeStruct(parts[0].shape, jnp.float32),
        scratch_shapes=[pltpu.VMEM((len(parts),) + parts[0].shape, jnp.float32)],
        name="merge",
    )(mine[None], *parts)


def exchange_stats(stats, dom_at, row_at, dom_count, row_count):
    stats = merge(row_at, [stats] + [swap(stats, 0, j) for j in range(1, row_count)])
    size, step = dom_count, 1
    while size > GROUP:
        parts = [stats] + [swap(stats, step * j, 0) for j in range(1, GROUP)]
        stats = merge((dom_at // step) % GROUP, parts)
        size, step = size // GROUP, step * GROUP
    parts = [stats] + [swap(stats, step * j, 0) for j in range(1, size)]
    return (dom_at // step) % size, parts


def backward_kernel(me, params, mask_ref, cot_ref, pre_ref, *refs, row_count):
    weights = refs[:row_count]
    output, grad_pre, grad_hidden, sums, ordered, total = refs[-6:]
    parts = refs[row_count:-6]
    at = pl.program_id(0)
    rows = weights[0].shape[0]
    mean, spread, shift_grad, scale_sum, count = merged(me[2], parts, ordered)
    inverse = lax.rsqrt(spread / count + NORM_EPS)
    scale_grad = scale_sum * inverse
    v = pre_ref[...]
    mask = mask_ref[...]
    bend = gelu_parts(v)
    act = 0.5 * v * (1.0 + bend)
    normed = (act - mean) * inverse
    scale = params[1:2, :]
    output[...] = (mask * (scale * normed + params[2:3, :])).astype(jnp.bfloat16)
    grad_out = mask * cot_ref[...].astype(jnp.float32)
    grad_act = (
        mask * (scale * inverse) * (grad_out - shift_grad / count - normed * (scale_grad / count))
    )
    slope = 0.5 * (1.0 + bend) + 0.5 * v * (1.0 - bend * bend) * (
        GELU_ROOT * (1.0 + 3.0 * GELU_CUBE * (v * v))
    )
    low = (grad_act * slope).astype(jnp.bfloat16)
    grad_pre[...] = low
    sums[0:1, :] = jnp.sum(low.astype(jnp.float32), axis=0, keepdims=True)
    sums[1:2, :] = scale_grad
    sums[2:3, :] = shift_grad
    sums[3:8, :] = jnp.zeros((5, scale_grad.shape[1]), jnp.float32)

    for j in range(row_count):
        term = dot(low, weights[j][...], BOTH_LAST)

        @pl.when(at == 0)
        def _():
            total[j] = term

        @pl.when(at > 0)
        def _():
            total[j] = total[j] + term

    @pl.when(at == pl.num_programs(0) - 1)
    def _():
        for j in range(row_count):
            start = pl.multiple_of((me[1] ^ j) * rows, rows)
            grad_hidden[:, pl.ds(start, rows)] = total[j].astype(jnp.bfloat16)


def backward(me, params, mask, cotangent, preact, weights, parts):
    rows, width = preact.shape
    row_count = len(weights)
    cols = 512
    wide = pl.BlockSpec((rows, cols), lambda i, me: (0, i))
    narrow = pl.BlockSpec((STAT_ROWS, cols), lambda i, me: (0, i))

    def kernel(*refs):
        backward_kernel(*refs, row_count=row_count)

    return call(
        kernel,
        flops=2 * rows * width * width,
        nbytes=2 * width * width + 12 * rows * width,
        vmem_mb=40,
        grid_spec=pltpu.PrefetchScalarGridSpec(
            num_scalar_prefetch=1,
            grid=(width // cols,),
            in_specs=[
                pl.BlockSpec((3, cols), lambda i, me: (0, i)),
                pl.BlockSpec((rows, 1), lambda i, me: (0, 0)),
                wide,
                wide,
            ]
            + [pl.BlockSpec((w.shape[0], cols), lambda i, me: (0, i)) for w in weights]
            + [narrow] * len(parts),
            out_specs=[
                wide,
                wide,
                pl.BlockSpec((rows, width), lambda i, me: (0, 0)),
                narrow,
            ],
            scratch_shapes=[
                pltpu.VMEM((len(parts), STAT_ROWS, cols), jnp.float32),
                pltpu.VMEM((row_count, rows, rows), jnp.float32),
            ],
        ),
        out_shape=[
            jax.ShapeDtypeStruct((rows, width), jnp.bfloat16),
            jax.ShapeDtypeStruct((rows, width), jnp.bfloat16),
            jax.ShapeDtypeStruct((rows, width), jnp.bfloat16),
            jax.ShapeDtypeStruct((STAT_ROWS, width), jnp.float32),
        ],
        name="backward",
    )(me, params, mask, cotangent, preact, *weights, *parts)


def slots_kernel(flip, grads, *outs):
    side = outs[0].shape[0]
    total = dot(flip[side:, :], grads[...]).astype(jnp.bfloat16)
    for k, out in enumerate(outs):
        out[...] = total[k * side : (k + 1) * side]


def slots(flip, grads, side):
    rows, width = grads.shape
    count = flip.shape[0] // side - 1
    cols = 256
    return call(
        slots_kernel,
        flops=2 * flip.size * width,
        nbytes=2 * (flip.size + grads.size + count * side * width),
        vmem_mb=16 + (2 * flip.size * 2 + 6 * count * side * cols * 2 >> 20),
        grid=(width // cols,),
        in_specs=[
            pl.BlockSpec(flip.shape, lambda i: (0, 0)),
            pl.BlockSpec((rows, cols), lambda i: (0, i)),
        ],
        out_specs=[pl.BlockSpec((side, cols), lambda i: (0, i))] * count,
        out_shape=[jax.ShapeDtypeStruct((side, width), jnp.bfloat16)] * count,
        name="slots",
    )(flip, grads)


def outer_kernel(hidden_flip, grads, keep, send):
    half = keep.shape[0]
    low = dot(hidden_flip[...], grads[...]).astype(jnp.bfloat16)
    keep[...] = low[:half]
    send[...] = low[half:]


def outer(hidden_flip, grads, part, parts):
    width, rows = hidden_flip.shape
    span = width // parts
    cols = 256
    first = part * span // cols
    out = pl.BlockSpec((width // 2, cols), lambda i: (0, i))
    return call(
        outer_kernel,
        flops=2 * rows * width * span,
        nbytes=2 * (hidden_flip.size + rows * span + width * span),
        vmem_mb=24,
        grid=(span // cols,),
        in_specs=[
            pl.BlockSpec(hidden_flip.shape, lambda i: (0, 0)),
            pl.BlockSpec((rows, cols), lambda i: (0, i + first)),
        ],
        out_specs=[out, out],
        out_shape=[jax.ShapeDtypeStruct((width // 2, span), jnp.bfloat16)] * 2,
        name="outer",
    )(hidden_flip, grads)


def return_kernel(picks, flips_and_grads, returned, out, total):
    flips, grads = flips_and_grads
    blocks, side = total.shape[0], total.shape[1]
    result = dot(flips[0][...], grads[0][...])
    for flip, grad in zip(flips[1:], grads[1:]):
        result += dot(flip[...], grad[...])
    for b in range(blocks):
        total[b] = result[b * side : (b + 1) * side]
    for k, ref in enumerate(returned):
        b = picks[k]

        @pl.when(b >= 0)
        def _():
            total[b] = total[b] + ref[...].astype(jnp.float32)

    for b in range(blocks):
        out[b * side : (b + 1) * side, :] = total[b].astype(jnp.bfloat16)


def give_back(picks, flips, grads, returned):
    rows, width = grads[0].shape
    side = returned[0].shape[0]
    row_count = len(flips)
    cols = 256

    def kernel(picks, *refs):
        flip_refs, rest = refs[:row_count], refs[row_count:]
        return_kernel(
            picks, (flip_refs, rest[:row_count]), rest[row_count:-2], rest[-2], rest[-1]
        )

    return call(
        kernel,
        flops=2 * rows * rows * row_count * width,
        nbytes=2 * (row_count * (rows * rows + rows * width) + (len(returned) * side + rows) * width),
        vmem_mb=20 + (6 * len(returned) * side * cols * 2 >> 20),
        grid_spec=pltpu.PrefetchScalarGridSpec(
            num_scalar_prefetch=1,
            grid=(width // cols,),
            in_specs=[pl.BlockSpec((rows, rows), lambda i, p: (0, 0))] * row_count
            + [pl.BlockSpec((rows, cols), lambda i, p: (0, i))] * row_count
            + [pl.BlockSpec((side, cols), lambda i, p: (0, i))] * len(returned),
            out_specs=pl.BlockSpec((rows, cols), lambda i, p: (0, i)),
            scratch_shapes=[pltpu.VMEM((rows // side, side, cols), jnp.float32)],
        ),
        out_shape=jax.ShapeDtypeStruct((rows, width), jnp.bfloat16),
        name="give_back",
    )(picks, *flips, *grads, *returned)


def lamb_step(value, grad, first, second, decay):
    first_new = DECAY_FIRST * first + (1.0 - DECAY_FIRST) * grad
    second_new = DECAY_SECOND * second + (1.0 - DECAY_SECOND) * grad * grad
    update = (
        first_new
        / (1.0 - DECAY_FIRST**STEP)
        / (jnp.sqrt(second_new / (1.0 - DECAY_SECOND**STEP)) + ADAM_EPS)
        + decay * value
    )
    return (first_new, second_new, update)


def sum_all(value, dom_count, row_count):
    step = 1
    while step < row_count:
        value = value + swap(value, 0, step)
        step *= 2
    step = 1
    while step < dom_count:
        value = value + swap(value, step, 0)
        step *= 2
    return value


def reduce_weight(keep, send, dom_at, dom_count):
    half = keep.shape[0] // 2
    f32, bf = jnp.float32, jnp.bfloat16
    near = swap(send, 0, 1)
    cross = (keep[half:].astype(f32) + near[half:].astype(f32)).astype(bf)
    far = swap(cross, 0, 2)
    total = (keep[:half].astype(f32) + near[:half].astype(f32) + far.astype(f32)).astype(bf)
    step, rows = 1, half
    while step < dom_count:
        rows //= 2
        bit = (dom_at // step) % 2
        other = lax.dynamic_slice_in_dim(total, (1 - bit) * rows, rows, 0)
        mine = lax.dynamic_slice_in_dim(total, bit * rows, rows, 0)
        total = (mine.astype(f32) + swap(other, step, 0).astype(f32)).astype(bf)
        step *= 2
    return total


def collect_weight(total, dom_at, dom_count):
    step = dom_count // 2
    while step >= 1:
        bit = (dom_at // step) % 2
        other = swap(total, step, 0)
        total = jnp.where(
            bit == 0,
            jnp.concatenate([total, other], axis=0),
            jnp.concatenate([other, total], axis=0),
        )
        step //= 2
    return total


def on_device(
    features,
    adjacency,
    tile_values,
    tile_block,
    tile_slot,
    tile_count,
    send_block,
    node_mask,
    weight,
    params,
    weight_first,
    weight_second,
    params_first,
    params_second,
    cotangent,
):
    dom_count, row_count = lax.axis_size("dom"), lax.axis_size("row")
    dom_at, row_at = lax.axis_index("dom"), lax.axis_index("row")
    rows = features.shape[0]
    side = tile_values.shape[1]
    me = jnp.stack([dom_at, row_at]).astype(jnp.int32)
    sends = send_block[0]
    picks = jnp.stack([sends[dom_at ^ k] for k in range(1, dom_count)])
    mask = node_mask.astype(jnp.float32)[:, None]

    arrived = []
    for k in reversed(range(1, dom_count)):
        block = jnp.maximum(picks[k - 1], 0)
        arrived.append(
            swap(lax.dynamic_slice_in_dim(features, block * side, side, 0), k, 0)
        )
    arrived = arrived[::-1]
    near_features = spread_rows(features)
    near_weights = spread_rows(weight.astype(jnp.bfloat16))

    wide, flip, halo, halo_flip = prepare(
        me, tile_block, tile_slot, tile_count, adjacency, tile_values, dom_count
    )
    flips = [flip[:rows]] + [
        swap(flip[j * rows : (j + 1) * rows], 0, j) for j in range(1, row_count)
    ]
    hidden, hidden_flip = gather(me, wide, halo, near_features, arrived)
    preact, stats = linear(hidden, params, mask, cotangent, near_weights)
    stat_at, parts = exchange_stats(stats, dom_at, row_at, dom_count, row_count)
    me = jnp.concatenate([me, stat_at[None]])
    output, grad_pre, grad_hidden, sums = backward(
        me, params, mask, cotangent, preact, near_weights, parts
    )

    returned = [
        swap(piece, k + 1, 0) for k, piece in enumerate(slots(halo_flip, grad_hidden, side))
    ]
    near_grads = spread_rows(grad_hidden)

    pieces = []
    for part in range(WEIGHT_PARTS):
        keep, send = outer(hidden_flip, grad_pre, part, WEIGHT_PARTS)
        pieces.append(reduce_weight(keep, send, dom_at, dom_count))
    piece = jnp.concatenate(pieces, axis=1).astype(jnp.float32)
    piece_rows = piece.shape[0]
    start = 0
    step, span = 1, rows
    while step < dom_count:
        span //= 2
        start = start + ((dom_at // step) % 2) * span
        step *= 2
    cut = lambda v: lax.dynamic_slice_in_dim(v, start, piece_rows, 0)
    weight_piece = cut(weight)
    update_piece = lamb_step(
        weight_piece, piece, cut(weight_first), cut(weight_second), WEIGHT_DECAY
    )[2]
    squares = jnp.stack([jnp.sum(weight_piece * weight_piece), jnp.sum(update_piece * update_piece)])
    squares = sum_all(jnp.pad(squares[None], ((0, 7), (0, 126))), dom_count, row_count)
    weight_norms = jnp.sqrt(squares[0, :2])
    weight_grad = jnp.concatenate(
        [collect_weight(p, dom_at, dom_count) for p in pieces], axis=1
    ).astype(jnp.float32)
    weight_first_new, weight_second_new, weight_update = lamb_step(
        weight, weight_grad, weight_first, weight_second, WEIGHT_DECAY
    )
    weight_new = (
        weight - LEARN_RATE * (weight_norms[0] / (weight_norms[1] + TRUST_EPS)) * weight_update
    )

    grad_features = give_back(picks, flips, near_grads, returned)

    bias_grad = sum_all(sums, dom_count, row_count)[0:1]
    param_grads = jnp.concatenate([bias_grad, sums[1:3]], axis=0)
    params_first_new, params_second_new, param_update = lamb_step(
        params, param_grads, params_first, params_second, 0.0
    )
    param_norms = jnp.sqrt(jnp.sum(params * params, axis=1, keepdims=True))
    update_norms = jnp.sqrt(jnp.sum(param_update * param_update, axis=1, keepdims=True))
    params_new = params - LEARN_RATE * (param_norms / (update_norms + TRUST_EPS)) * param_update
    norms = jnp.concatenate(
        [weight_norms[None, :], jnp.concatenate([param_norms, update_norms], axis=1)], axis=0
    )
    return (
        output,
        grad_features,
        weight_new,
        weight_new.astype(jnp.bfloat16),
        weight_first_new,
        weight_second_new,
        params_new,
        params_first_new,
        params_second_new,
        norms,
    )


def solution(mesh):
    in_specs = (
        P(("dom", "row"), None),
        P(("dom", "row"), None),
        P(("dom", "row"), None, None),
        P(("dom", "row")),
        P(("dom", "row")),
        P(("dom", "row")),
        P(("dom", "row"), None),
        P(("dom", "row")),
        P("row", None),
        P(),
        P("row", None),
        P("row", None),
        P(),
        P(),
        P(("dom", "row"), None),
    )
    out_specs = (
        P(("dom", "row"), None),
        P(("dom", "row"), None),
        P("row", None),
        P("row", None),
        P("row", None),
        P("row", None),
        P(),
        P(),
        P(),
        P(),
    )
    return jax.shard_map(
        on_device, mesh=mesh, in_specs=in_specs, out_specs=out_specs, check_vma=False
    )
```

time: 993 us -> 508 us (0.51)
  matrix products: 284 us -> 0 us
  blocking collectives: 284 us -> 0 us
  local copies, waits for them, and re-layouts: 170 us -> 35.8 us
  waiting for transfers between devices: 159 us -> 269 us
  starting transfers between devices: 12.8 us -> 93.5 us
  Pallas kernels: 0 us -> 64.3 us
  other arithmetic: 58.6 us -> 30.9 us
    psum x5 -> x0, blocking collectives: 284 us -> none  [the longest x1 158 us: on_device(): lax.psum((weight_local, bias_local), ('dom', 'row'))]
    dot_general x13 -> x0, matrix products: 284 us -> none  [the longest x1 59 us: on_device(): jnp.einsum('tij,tjf->tif', tile_values, picked, preferred_element_type=jn...]
    ppermute x0 -> x62, waiting for transfers between devices: none -> 269 us  [swap(): return lax.ppermute(value, AXES, pairs)]
    dot_general x4 -> x0, local copies, waits for them, and re-layouts: 152 us -> none  [the longest x1 72 us: on_device(): jnp.einsum('tij,tif->tjf', tile_values, hidden_rows, preferred_element_ty...]
    ppermute x0 -> x62, starting transfers between devices: none -> 93.5 us  [swap(): return lax.ppermute(value, AXES, pairs)]
    all_to_all x2 -> x0, waiting for transfers between devices: 81.6 us -> none  [the longest x1 81.6 us: on_device(): lax.all_to_all(outgoing.reshape(peer_count * block_rows, feat_width), 'do...]
    reduce_scatter x1 -> x0, waiting for transfers between devices: 76.8 us -> none  [on_device(): lax.psum_scatter(jnp.einsum('rp,rf->pf', columns, grad_hidden, preferred_...]
    pallas_call x0 -> x9, Pallas kernels: none -> 64.3 us  [the longest x1 16.6 us: backward(): call(kernel, flops=2 * rows * width * width, nbytes=2 * width * width + 1...]
  transfers between devices with their start and end apart: 6 -> 62, of which waited for: 2 -> 29; matrix products, arithmetic and copies ran while one was open for 47% -> 7% of each run, Pallas kernels for 0% -> 7%
where the time goes in v1:
time: 508 us; the launch traced here: 501 us
  waiting for transfers between devices  269 us (53%)
  starting transfers between devices  93.5 us (18%)
  Pallas kernels  64.3 us (13%)
  local copies, waits for them, and re-layouts  35.8 us (7%)
  other arithmetic  30.9 us (6%)
  between operations  7.89 us (2%)
    ppermute x62, waiting for transfers between devices, swap(): return lax.ppermute(value, AXES, pairs)  269 us
    ppermute x62, starting transfers between devices, swap(): return lax.ppermute(value, AXES, pairs)  93.5 us
    unnamed x114, local copies, waits for them, and re-layouts  25.5 us
    pallas_call x1, Pallas kernels, backward(): call(kernel, flops=2 * rows * width * width, nbytes=2 * width * width + 1...  16.6 us
    pallas_call x1, Pallas kernels, gather(): call(gather_kernel, flops=2 * rows * width * (row_count * rows + halo.sha...  11.5 us
    pallas_call x1, Pallas kernels, give_back(): call(kernel, flops=2 * rows * rows * row_count * width, nbytes=2 * (row_c...  11.1 us
    pallas_call x1, Pallas kernels, linear(): call(linear_kernel, flops=2 * rows * width * width, nbytes=2 * width * wi...  10.3 us
  transfers between devices with their start and end apart: 62, of which 29 were waited for; matrix products, arithmetic and copies ran while one was open for 7% of the time, Pallas kernels for 7%

profile of v1, /device:TPU:0, one launch (start us, length us, event | category | flops | bytes accessed | tf_op | source)
XLA Modules:
  0.0 501.0 jit_solution(4240843492197853954)
XLA Ops:
  17.5 10.5 %collective-permute-done.3.refs_4_ = bf16[128,2048]{1,0:T(8,128)(2,1)S(1)} collective-permute-done((bf16[128,2048]{1,0:T(8,128)(2,1)S(1)}, bf16[128,2048]{1,0:T(8,128)(2,1)S(1)}, u32[]{:S(2)}, u32[]{:S(2)}) %collective-permute-start.3) | collective-permute-done | bytes 524320 | tf_op jit(solution)/shard_map/ppermute | solution.py:44
  28.0 22.5 %collective-permute-done.1.refs_2_ = bf16[512,2048]{1,0:T(8,128)(2,1)} collective-permute-done((bf16[512,2048]{1,0:T(8,128)(2,1)}, bf16[512,2048]{1,0:T(8,128)(2,1)}, u32[]{:S(2)}, u32[]{:S(2)}) %collective-permute-start.1) | collective-permute-done | bytes 2097184 | tf_op jit(solution)/shard_map/ppermute | solution.py:44
  56.5 33.2 %collective-permute-done.6.refs_7_ = bf16[128,2048]{1,0:T(8,128)(2,1)S(1)} collective-permute-done((bf16[128,2048]{1,0:T(8,128)(2,1)S(1)}, bf16[128,2048]{1,0:T(8,128)(2,1)S(1)}, u32[]{:S(2)}, u32[]{:S(2)}) %collective-permute-start.6) | collective-permute-done | bytes 524320 | tf_op jit(solution)/shard_map/ppermute | solution.py:44
  94.6 7.1 %collective-permute-done.7.refs_8_ = bf16[128,2048]{1,0:T(8,128)(2,1)S(1)} collective-permute-done((bf16[128,2048]{1,0:T(8,128)(2,1)S(1)}, bf16[128,2048]{1,0:T(8,128)(2,1)S(1)}, u32[]{:S(2)}, u32[]{:S(2)}) %collective-permute-start.7) | collective-permute-done | bytes 524320 | tf_op jit(solution)/shard_map/ppermute | solution.py:44
  106.0 12.3 %collective-permute-done.8.refs_9_ = bf16[128,2048]{1,0:T(8,128)(2,1)S(1)} collective-permute-done((bf16[128,2048]{1,0:T(8,128)(2,1)S(1)}, bf16[128,2048]{1,0:T(8,128)(2,1)S(1)}, u32[]{:S(2)}, u32[]{:S(2)}) %collective-permute-start.8) | collective-permute-done | bytes 524320 | tf_op jit(solution)/shard_map/ppermute | solution.py:44
  136.9 11.5 %gather.1 = (bf16[512,2048]{1,0:T(8,128)(2,1)S(1)}, bf16[2048,512]{1,0:T(8,128)(2,1)S(1)}) custom-call(s32[2]{0:T(128)S(1)} %pad_add_fusion.2.me, bf16[512,2048]{1,0:T(8,128)(2,1)S(1)} %get-tuple-element.33.wide, bf16[512,1024]{1,0:T(8,128)(2,1)S(1)} %get-tuple-element.34.halo, bf16[512,2048]{1,0:T(8,128)(2,1)S(1)} %copy-done, ...), custom_call_target="tpu_custom_call" | custom-call | flops 6442450944 | bytes 19398656 | tf_op jit(solution)/shard_map/gather/pallas_call | solution.py:150
  149.8 10.3 %linear.1 = (f32[512,2048]{1,0:T(8,128)S(1)}, f32[8,2048]{1,0:T(8,128)S(1)}) custom-call(bf16[512,2048]{1,0:T(8,128)(2,1)S(1)} %get-tuple-element.35.hidden, f32[3,2048]{1,0:T(4,128)S(1)} %copy-done.20, f32[512,1]{1,0:T(8,128)S(1)} %copy.27.mask_ref.refs_2_, bf16[512,2048]{1,0:T(8,128)(2,1)S(1)} %copy-done.23, ...), custom_call_target="tpu_custom_call" | custom-call | flops 4294967296 | bytes 18874368 | tf_op jit(solution)/shard_map/linear/pallas_call | solution.py:200
  168.6 19.4 %collective-permute-start.17 = (f32[8,2048]{1,0:T(8,128)S(1)}, f32[8,2048]{1,0:T(8,128)S(1)}, u32[]{:S(2)}, u32[]{:S(2)}) collective-permute-start(f32[8,2048]{1,0:T(8,128)S(1)} %merge.1.refs_9_), channel_id=1, source_target_pairs={{0,8},{1,9},{2,10},{3,11},{4,12},{5,13},{6,14},{7,15},{8,0},{9,1},... | collective-permute-start | bytes 196616 | tf_op jit(solution)/shard_map/ppermute | solution.py:44
  203.2 16.6 %backward.1 = (bf16[512,2048]{1,0:T(8,128)(2,1)}, bf16[512,2048]{1,0:T(8,128)(2,1)S(1)}, bf16[512,2048]{1,0:T(8,128)(2,1)S(1)}, f32[8,2048]{1,0:T(8,128)S(1)}) custom-call(s32[3]{0:T(128)S(1)} %pad_add_fusion.1.refs_0_, f32[3,2048]{1,0:T(4,128)S(1)} %copy-done.20, f32[512,1]{1,0:T(8,128)S(1)} %copy.27.mask_ref.refs_2_, bf16[512,2048]{1,0:T(8,128)(2,1)S(1)} %copy-done.24, ...), custom_call_target="tpu_custom_call" | custom-call | flops 4294967296 | bytes 20971520 | tf_op jit(solution)/shard_map/backward/pallas_call | solution.py:325
  235.7 18.6 %collective-permute-done.42 = bf16[512,1024]{1,0:T(8,128)(2,1)} collective-permute-done((bf16[512,1024]{1,0:T(8,128)(2,1)S(1)}, bf16[512,1024]{1,0:T(8,128)(2,1)}, u32[]{:S(2)}, u32[]{:S(2)}) %collective-permute-start.42) | collective-permute-done | bytes 1048608 | tf_op jit(solution)/shard_map/ppermute | solution.py:44
  257.8 18.1 %collective-permute-done.37 = bf16[512,1024]{1,0:T(8,128)(2,1)} collective-permute-done((bf16[512,1024]{1,0:T(8,128)(2,1)}, bf16[512,1024]{1,0:T(8,128)(2,1)}, u32[]{:S(2)}, u32[]{:S(2)}) %collective-permute-start.37) | collective-permute-done | bytes 1048608 | tf_op jit(solution)/shard_map/ppermute | solution.py:44
  286.2 5.8 %collective-permute-done.38 = bf16[256,1024]{1,0:T(8,128)(2,1)} collective-permute-done((bf16[256,1024]{1,0:T(8,128)(2,1)}, bf16[256,1024]{1,0:T(8,128)(2,1)}, u32[]{:S(2)}, u32[]{:S(2)}) %collective-permute-start.38) | collective-permute-done | bytes 524320 | tf_op jit(solution)/shard_map/ppermute | solution.py:44
  296.4 7.2 %collective-permute-done.39 = bf16[128,1024]{1,0:T(8,128)(2,1)S(1)} collective-permute-done((bf16[128,1024]{1,0:T(8,128)(2,1)S(1)}, bf16[128,1024]{1,0:T(8,128)(2,1)S(1)}, u32[]{:S(2)}, u32[]{:S(2)}) %collective-permute-start.39) | collective-permute-done | bytes 262176 | tf_op jit(solution)/shard_map/ppermute | solution.py:44
  304.8 6.3 %collective-permute-done.40 = bf16[64,1024]{1,0:T(8,128)(2,1)S(1)} collective-permute-done((bf16[64,1024]{1,0:T(8,128)(2,1)S(1)}, bf16[64,1024]{1,0:T(8,128)(2,1)S(1)}, u32[]{:S(2)}, u32[]{:S(2)}) %collective-permute-start.40) | collective-permute-done | bytes 131104 | tf_op jit(solution)/shard_map/ppermute | solution.py:44
  318.1 10.7 %collective-permute-done.58 = f32[8,2048]{1,0:T(8,128)S(1)} collective-permute-done((f32[8,2048]{1,0:T(8,128)S(1)}, f32[8,2048]{1,0:T(8,128)S(1)}, u32[]{:S(2)}, u32[]{:S(2)}) %collective-permute-start.58) | collective-permute-done | bytes 65568 | tf_op jit(solution)/shard_map/ppermute | solution.py:44
  361.7 8.7 %collective-permute-done.25.refs_3_ = bf16[512,512]{1,0:T(8,128)(2,1)S(1)} collective-permute-done((bf16[512,512]{1,0:T(8,128)(2,1)S(1)}, bf16[512,512]{1,0:T(8,128)(2,1)S(1)}, u32[]{:S(2)}, u32[]{:S(2)}) %collective-permute-start.25) | collective-permute-done | bytes 524320 | tf_op jit(solution)/shard_map/ppermute | solution.py:44
  384.8 15.1 %collective-permute-done.31.refs_10_ = bf16[128,2048]{1,0:T(8,128)(2,1)S(1)} collective-permute-done((bf16[128,2048]{1,0:T(8,128)(2,1)S(1)}, bf16[128,2048]{1,0:T(8,128)(2,1)S(1)}, u32[]{:S(2)}, u32[]{:S(2)}) %collective-permute-start.31) | collective-permute-done | bytes 524320 | tf_op jit(solution)/shard_map/ppermute | solution.py:44
  400.6 21.2 %collective-permute-done.32.refs_11_ = bf16[128,2048]{1,0:T(8,128)(2,1)S(1)} collective-permute-done((bf16[128,2048]{1,0:T(8,128)(2,1)S(1)}, bf16[128,2048]{1,0:T(8,128)(2,1)S(1)}, u32[]{:S(2)}, u32[]{:S(2)}) %collective-permute-start.32) | collective-permute-done | bytes 524320 | tf_op jit(solution)/shard_map/ppermute | solution.py:44
  422.7 10.7 %collective-permute-done.33.refs_12_ = bf16[128,2048]{1,0:T(8,128)(2,1)S(1)} collective-permute-done((bf16[128,2048]{1,0:T(8,128)(2,1)S(1)}, bf16[128,2048]{1,0:T(8,128)(2,1)S(1)}, u32[]{:S(2)}, u32[]{:S(2)}) %collective-permute-start.33) | collective-permute-done | bytes 524320 | tf_op jit(solution)/shard_map/ppermute | solution.py:44
  436.1 16.6 %collective-permute-done.51 = bf16[64,1024]{1,0:T(8,128)(2,1)S(1)} collective-permute-done((bf16[64,1024]{1,0:T(8,128)(2,1)S(1)}, bf16[64,1024]{1,0:T(8,128)(2,1)S(1)}, u32[]{:S(2)}, u32[]{:S(2)}) %collective-permute-start.51) | collective-permute-done | bytes 131104 | tf_op jit(solution)/shard_map/ppermute | solution.py:44
  461.7 6.3 %collective-permute-done.52 = bf16[128,1024]{1,0:T(8,128)(2,1)S(1)} collective-permute-done((bf16[128,1024]{1,0:T(8,128)(2,1)}, bf16[128,1024]{1,0:T(8,128)(2,1)S(1)}, u32[]{:S(2)}, u32[]{:S(2)}) %collective-permute-start.52) | collective-permute-done | bytes 262176 | tf_op jit(solution)/shard_map/ppermute | solution.py:44
  474.6 11.1 %give_back.1 = bf16[512,2048]{1,0:T(8,128)(2,1)} custom-call(s32[7]{0:T(128)S(1)} %stack.24.picks, bf16[512,512]{1,0:T(8,128)(2,1)S(1)} %get-tuple-element.69.refs_0_, bf16[512,512]{1,0:T(8,128)(2,1)S(1)} %collective-permute-done.23.refs_1_, bf16[512,512]{1,0:T(8,128)(2,1)} %collective-permute-done.24.refs_2_, bf16[512,512]{1,0:T(8,128)(2,1)S(1)} %copy-done.9, ...), custom_call_target="tpu_custom_call" | custom-call | flops 4294967296 | bytes 16252928 | tf_op jit(solution)/shard_map/give_back/pallas_call | solution.py:449
  486.2 8.0 %collective-permute-done.53 = bf16[256,1024]{1,0:T(8,128)(2,1)S(1)} collective-permute-done((bf16[256,1024]{1,0:T(8,128)(2,1)S(1)}, bf16[256,1024]{1,0:T(8,128)(2,1)S(1)}, u32[]{:S(2)}, u32[]{:S(2)}) %collective-permute-start.53) | collective-permute-done | bytes 524320 | tf_op jit(solution)/shard_map/ppermute | solution.py:44
  494.8 6.3 %fusion.13 = (bf16[512,2048]{1,0:T(8,128)(2,1)}, f32[512,2048]{1,0:T(8,128)}, f32[512,2048]{1,0:T(8,128)}, f32[512,2048]{1,0:T(8,128)}) fusion(f32[512,2048]{1,0:T(8,128)S(1)} %copy-done.42, f32[]{:T(128)} %bitcast.21, bf16[512,1024]{1,0:T(8,128)(2,1)S(1)} %maximum_select_fusion.1, bf16[512,1024]{1,0:T(8,128)(2,1)S(1)} %maximum_select_fusion, ...), kind=kLoop, calls=%fused_computation.72 | loop fusion | flops 19922944 | bytes 29360132 | tf_op jit(solution)/shard_map/convert_element_type | solution.py:626
  (276 shorter events, 179.2 us)
Async XLA Ops:
  0.7 49.8 %collective-permute-start.1 = (bf16[512,2048]{1,0:T(8,128)(2,1)}, bf16[512,2048]{1,0:T(8,128)(2,1)}, u32[]{:S(2)}, u32[]{:S(2)}) collective-permute-start(bf16[512,2048]{1,0:T(8,128)(2,1)} %refs_0_.1), channel_id=1, source_target_pairs={{0,2},{1,3},{2,0},{3,1},{4,6},{5,7},{6,4},{7,5},{8,10},{9,11},{10,... | collective-permute-start | bytes 6291464 | tf_op jit(solution)/shard_map/ppermute | solution.py:44
  7.5 87.1 %collective-permute-start.11 = (bf16[512,2048]{1,0:T(8,128)(2,1)}, bf16[512,2048]{1,0:T(8,128)(2,1)}, u32[]{:S(2)}, u32[]{:S(2)}) collective-permute-start(bf16[512,2048]{1,0:T(8,128)(2,1)} %convert_element_type.114.refs_0_.refs_5_), channel_id=1, source_target_pairs={{0,2},{1,3},{2,0},{3,1},{4,6},{5,7},{6,4},{7,5},{8,10},{9,11},{10,... | collective-permute-start | bytes 6291464 | tf_op jit(solution)/shard_map/ppermute | solution.py:44
  16.0 34.5 %collective-permute-start.4 = (bf16[128,2048]{1,0:T(8,128)(2,1)S(1)}, bf16[128,2048]{1,0:T(8,128)(2,1)S(1)}, u32[]{:S(2)}, u32[]{:S(2)}) collective-permute-start(bf16[128,2048]{1,0:T(8,128)(2,1)S(1)} %get-tuple-element.75), channel_id=1, source_target_pairs={{0,8},{1,9},{2,10},{3,11},{4,12},{5,13},{6,14},{7,15},{8,0},{9,1},... | collective-permute-start | bytes 1572872 | tf_op jit(solution)/shard_map/ppermute | solution.py:44
  17.5 36.9 %collective-permute-start.5 = (bf16[128,2048]{1,0:T(8,128)(2,1)S(1)}, bf16[128,2048]{1,0:T(8,128)(2,1)S(1)}, u32[]{:S(2)}, u32[]{:S(2)}) collective-permute-start(bf16[128,2048]{1,0:T(8,128)(2,1)S(1)} %get-tuple-element.74), channel_id=1, source_target_pairs={{0,12},{1,13},{2,14},{3,15},{4,8},{5,9},{6,10},{7,11},{8,4},{9,5},... | collective-permute-start | bytes 1572872 | tf_op jit(solution)/shard_map/ppermute | solution.py:44
  28.0 107.8 %collective-permute-start = (bf16[512,2048]{1,0:T(8,128)(2,1)S(1)}, bf16[512,2048]{1,0:T(8,128)(2,1)}, u32[]{:S(2)}, u32[]{:S(2)}) collective-permute-start(bf16[512,2048]{1,0:T(8,128)(2,1)S(1)} %copy-done), channel_id=1, source_target_pairs={{0,1},{1,0},{2,3},{3,2},{4,5},{5,4},{6,7},{7,6},{8,9},{9,8},{10,11... | collective-permute-start | bytes 6291464 | tf_op jit(solution)/shard_map/ppermute | solution.py:44
  50.5 85.3 %collective-permute-start.2 = (bf16[512,2048]{1,0:T(8,128)(2,1)}, bf16[512,2048]{1,0:T(8,128)(2,1)}, u32[]{:S(2)}, u32[]{:S(2)}) collective-permute-start(bf16[512,2048]{1,0:T(8,128)(2,1)} %collective-permute-done.1.refs_2_), channel_id=1, source_target_pairs={{0,1},{1,0},{2,3},{3,2},{4,5},{5,4},{6,7},{7,6},{8,9},{9,8},{10,11... | collective-permute-start | bytes 6291464 | tf_op jit(solution)/shard_map/ppermute | solution.py:44
  51.3 38.4 %collective-permute-start.6 = (bf16[128,2048]{1,0:T(8,128)(2,1)S(1)}, bf16[128,2048]{1,0:T(8,128)(2,1)S(1)}, u32[]{:S(2)}, u32[]{:S(2)}) collective-permute-start(bf16[128,2048]{1,0:T(8,128)(2,1)S(1)} %get-tuple-element.73), channel_id=1, source_target_pairs={{0,16},{1,17},{2,18},{3,19},{4,20},{5,21},{6,22},{7,23},{8,24},{9,... | collective-permute-start | bytes 1572872 | tf_op jit(solution)/shard_map/ppermute | solution.py:44
  55.2 46.5 %collective-permute-start.7 = (bf16[128,2048]{1,0:T(8,128)(2,1)S(1)}, bf16[128,2048]{1,0:T(8,128)(2,1)S(1)}, u32[]{:S(2)}, u32[]{:S(2)}) collective-permute-start(bf16[128,2048]{1,0:T(8,128)(2,1)S(1)} %get-tuple-element.72), channel_id=1, source_target_pairs={{0,20},{1,21},{2,22},{3,23},{4,16},{5,17},{6,18},{7,19},{8,28},{9,... | collective-permute-start | bytes 1572872 | tf_op jit(solution)/shard_map/ppermute | solution.py:44
  90.4 59.3 %collective-permute-start.10 = (bf16[512,2048]{1,0:T(8,128)(2,1)}, bf16[512,2048]{1,0:T(8,128)(2,1)}, u32[]{:S(2)}, u32[]{:S(2)}) collective-permute-start(bf16[512,2048]{1,0:T(8,128)(2,1)} %convert_element_type.114.refs_0_.refs_5_), channel_id=1, source_target_pairs={{0,1},{1,0},{2,3},{3,2},{4,5},{5,4},{6,7},{7,6},{8,9},{9,8},{10,11... | collective-permute-start | bytes 6291464 | tf_op jit(solution)/shard_map/ppermute | solution.py:44
  94.6 55.2 %collective-permute-start.12 = (bf16[512,2048]{1,0:T(8,128)(2,1)}, bf16[512,2048]{1,0:T(8,128)(2,1)}, u32[]{:S(2)}, u32[]{:S(2)}) collective-permute-start(bf16[512,2048]{1,0:T(8,128)(2,1)} %collective-permute-done.11.refs_2_.refs_7_), channel_id=1, source_target_pairs={{0,1},{1,0},{2,3},{3,2},{4,5},{5,4},{6,7},{7,6},{8,9},{9,8},{10,11... | collective-permute-start | bytes 6291464 | tf_op jit(solution)/shard_map/ppermute | solution.py:44
  168.6 24.8 %collective-permute-start.17 = (f32[8,2048]{1,0:T(8,128)S(1)}, f32[8,2048]{1,0:T(8,128)S(1)}, u32[]{:S(2)}, u32[]{:S(2)}) collective-permute-start(f32[8,2048]{1,0:T(8,128)S(1)} %merge.1.refs_9_), channel_id=1, source_target_pairs={{0,8},{1,9},{2,10},{3,11},{4,12},{5,13},{6,14},{7,15},{8,0},{9,1},... | collective-permute-start | bytes 196616 | tf_op jit(solution)/shard_map/ppermute | solution.py:44
  228.1 26.2 %collective-permute-start.42 = (bf16[512,1024]{1,0:T(8,128)(2,1)S(1)}, bf16[512,1024]{1,0:T(8,128)(2,1)}, u32[]{:S(2)}, u32[]{:S(2)}) collective-permute-start(bf16[512,1024]{1,0:T(8,128)(2,1)S(1)} %add_convert_fusion.1), channel_id=1, source_target_pairs={{0,2},{1,3},{2,0},{3,1},{4,6},{5,7},{6,4},{7,5},{8,10},{9,11},{10,... | collective-permute-start | bytes 3145736 | tf_op jit(solution)/shard_map/ppermute | solution.py:44
  234.2 41.7 %collective-permute-start.37 = (bf16[512,1024]{1,0:T(8,128)(2,1)}, bf16[512,1024]{1,0:T(8,128)(2,1)}, u32[]{:S(2)}, u32[]{:S(2)}) collective-permute-start(bf16[512,1024]{1,0:T(8,128)(2,1)} %add_convert_fusion.3), channel_id=1, source_target_pairs={{0,2},{1,3},{2,0},{3,1},{4,6},{5,7},{6,4},{7,5},{8,10},{9,11},{10,... | collective-permute-start | bytes 3145736 | tf_op jit(solution)/shard_map/ppermute | solution.py:44
  278.9 79.9 %collective-permute-start.27 = (bf16[512,2048]{1,0:T(8,128)(2,1)S(1)}, bf16[512,2048]{1,0:T(8,128)(2,1)}, u32[]{:S(2)}, u32[]{:S(2)}) collective-permute-start(bf16[512,2048]{1,0:T(8,128)(2,1)S(1)} %get-tuple-element.40.grads.refs_4_), channel_id=1, source_target_pairs={{0,2},{1,3},{2,0},{3,1},{4,6},{5,7},{6,4},{7,5},{8,10},{9,11},{10,... | collective-permute-start | bytes 6291464 | tf_op jit(solution)/shard_map/ppermute | solution.py:44
  280.4 48.4 %collective-permute-start.58 = (f32[8,2048]{1,0:T(8,128)S(1)}, f32[8,2048]{1,0:T(8,128)S(1)}, u32[]{:S(2)}, u32[]{:S(2)}) collective-permute-start(f32[8,2048]{1,0:T(8,128)S(1)} %add.286), channel_id=1, source_target_pairs={{0,2},{1,3},{2,0},{3,1},{4,6},{5,7},{6,4},{7,5},{8,10},{9,11},{10,... | collective-permute-start | bytes 196616 | tf_op jit(solution)/shard_map/ppermute | solution.py:44
  316.1 40.0 %collective-permute-start.23 = (bf16[512,512]{1,0:T(8,128)(2,1)}, bf16[512,512]{1,0:T(8,128)(2,1)S(1)}, u32[]{:S(2)}, u32[]{:S(2)}) collective-permute-start(bf16[512,512]{1,0:T(8,128)(2,1)} %get-tuple-element.68), channel_id=1, source_target_pairs={{0,1},{1,0},{2,3},{3,2},{4,5},{5,4},{6,7},{7,6},{8,9},{9,8},{10,11... | collective-permute-start | bytes 1572872 | tf_op jit(solution)/shard_map/ppermute | solution.py:44
  316.5 39.9 %collective-permute-start.24 = (bf16[512,512]{1,0:T(8,128)(2,1)}, bf16[512,512]{1,0:T(8,128)(2,1)}, u32[]{:S(2)}, u32[]{:S(2)}) collective-permute-start(bf16[512,512]{1,0:T(8,128)(2,1)} %get-tuple-element.67), channel_id=1, source_target_pairs={{0,2},{1,3},{2,0},{3,1},{4,6},{5,7},{6,4},{7,5},{8,10},{9,11},{10,... | collective-permute-start | bytes 1572872 | tf_op jit(solution)/shard_map/ppermute | solution.py:44
  356.4 116.0 %collective-permute-start.26 = (bf16[512,2048]{1,0:T(8,128)(2,1)S(1)}, bf16[512,2048]{1,0:T(8,128)(2,1)}, u32[]{:S(2)}, u32[]{:S(2)}) collective-permute-start(bf16[512,2048]{1,0:T(8,128)(2,1)S(1)} %get-tuple-element.40.grads.refs_4_), channel_id=1, source_target_pairs={{0,1},{1,0},{2,3},{3,2},{4,5},{5,4},{6,7},{7,6},{8,9},{9,8},{10,11... | collective-permute-start | bytes 6291464 | tf_op jit(solution)/shard_map/ppermute | solution.py:44
  360.8 111.7 %collective-permute-start.28 = (bf16[512,2048]{1,0:T(8,128)(2,1)}, bf16[512,2048]{1,0:T(8,128)(2,1)}, u32[]{:S(2)}, u32[]{:S(2)}) collective-permute-start(bf16[512,2048]{1,0:T(8,128)(2,1)} %collective-permute-done.27.refs_6_), channel_id=1, source_target_pairs={{0,1},{1,0},{2,3},{3,2},{4,5},{5,4},{6,7},{7,6},{8,9},{9,8},{10,11... | collective-permute-start | bytes 6291464 | tf_op jit(solution)/shard_map/ppermute | solution.py:44
  380.8 41.0 %collective-permute-start.32 = (bf16[128,2048]{1,0:T(8,128)(2,1)S(1)}, bf16[128,2048]{1,0:T(8,128)(2,1)S(1)}, u32[]{:S(2)}, u32[]{:S(2)}) collective-permute-start(bf16[128,2048]{1,0:T(8,128)(2,1)S(1)} %get-tuple-element.45), channel_id=1, source_target_pairs={{0,16},{1,17},{2,18},{3,19},{4,20},{5,21},{6,22},{7,23},{8,24},{9,... | collective-permute-start | bytes 1572872 | tf_op jit(solution)/shard_map/ppermute | solution.py:44
  380.8 52.6 %collective-permute-start.33 = (bf16[128,2048]{1,0:T(8,128)(2,1)S(1)}, bf16[128,2048]{1,0:T(8,128)(2,1)S(1)}, u32[]{:S(2)}, u32[]{:S(2)}) collective-permute-start(bf16[128,2048]{1,0:T(8,128)(2,1)S(1)} %get-tuple-element.46), channel_id=1, source_target_pairs={{0,20},{1,21},{2,22},{3,23},{4,16},{5,17},{6,18},{7,19},{8,28},{9,... | collective-permute-start | bytes 1572872 | tf_op jit(solution)/shard_map/ppermute | solution.py:44
  400.6 52.1 %collective-permute-start.51 = (bf16[64,1024]{1,0:T(8,128)(2,1)S(1)}, bf16[64,1024]{1,0:T(8,128)(2,1)S(1)}, u32[]{:S(2)}, u32[]{:S(2)}) collective-permute-start(bf16[64,1024]{1,0:T(8,128)(2,1)S(1)} %add_convert_fusion.9), channel_id=1, source_target_pairs={{0,16},{1,17},{2,18},{3,19},{4,20},{5,21},{6,22},{7,23},{8,24},{9,... | collective-permute-start | bytes 393224 | tf_op jit(solution)/shard_map/ppermute | solution.py:44
  422.7 34.1 %collective-permute-start.55 = (bf16[128,1024]{1,0:T(8,128)(2,1)S(1)}, bf16[128,1024]{1,0:T(8,128)(2,1)S(1)}, u32[]{:S(2)}, u32[]{:S(2)}) collective-permute-start(bf16[128,1024]{1,0:T(8,128)(2,1)S(1)} %maximum_select_fusion.5), channel_id=1, source_target_pairs={{0,8},{1,9},{2,10},{3,11},{4,12},{5,13},{6,14},{7,15},{8,0},{9,1},... | collective-permute-start | bytes 786440 | tf_op jit(solution)/shard_map/ppermute | solution.py:44
  434.2 38.1 %collective-permute-start.34 = (bf16[128,2048]{1,0:T(8,128)(2,1)}, bf16[128,2048]{1,0:T(8,128)(2,1)}, u32[]{:S(2)}, u32[]{:S(2)}) collective-permute-start(bf16[128,2048]{1,0:T(8,128)(2,1)} %get-tuple-element.47), channel_id=1, source_target_pairs={{0,24},{1,25},{2,26},{3,27},{4,28},{5,29},{6,30},{7,31},{8,16},{9,... | collective-permute-start | bytes 1572872 | tf_op jit(solution)/shard_map/ppermute | solution.py:44
  (95 other events, 1257.4 us)

commit v2 on v0

v2 whole, which is shorter than its diff:
```python
import math

import jax
import jax.numpy as jnp
from jax import lax
from jax.experimental import pallas as pl
from jax.experimental.pallas import tpu as pltpu
from jax.sharding import PartitionSpec as P

STEP = 5


SELF_LOOP = 1.0
NORM_EPS = 1e-05
DECAY_FIRST = 0.5
DECAY_SECOND = 0.5
ADAM_EPS = 1e-06
WEIGHT_DECAY = 0.01
LEARN_RATE = 0.5
TRUST_EPS = 1e-06

AXES = ("dom", "row")
GELU_ROOT = math.sqrt(2.0 / math.pi)
GELU_CUBE = 0.044715
STAT_ROWS = 8
LANES = 128
COLS = 256
WHOLE_HALO = 2048
SLOT_GROUP = 7

ANY_ROWS = (((1,), (0,)), ((), ()))
BOTH_LAST = (((1,), (1,)), ((), ()))
SMEM = pl.BlockSpec(memory_space=pltpu.SMEM)
VMEM = pl.BlockSpec(memory_space=pltpu.VMEM)
ANY = pl.BlockSpec(memory_space=pl.ANY)
SDS = jax.ShapeDtypeStruct


def dot(left, right, dims=ANY_ROWS):
    return lax.dot_general(left, right, dims, preferred_element_type=jnp.float32)


def swap(value, dom_flip, row_flip):
    dom_count, row_count = lax.axis_size("dom"), lax.axis_size("row")
    pairs = [
        (d * row_count + r, (d ^ dom_flip) * row_count + (r ^ row_flip))
        for d in range(dom_count)
        for r in range(row_count)
    ]
    return lax.ppermute(value, AXES, pairs)


def hold(value, *others):
    return lax.optimization_barrier((value, *others))[0]


def call(kernel, *, flops, vmem_mb=56, **kw):
    return pl.pallas_call(
        kernel,
        cost_estimate=pl.CostEstimate(flops=int(flops), bytes_accessed=0, transcendentals=0),
        compiler_params=pltpu.CompilerParams(vmem_limit_bytes=vmem_mb << 20),
        **kw,
    )


def columns(width, blocked):
    if not blocked:
        return {}, lambda height: VMEM, lambda shape: VMEM
    grid = {"grid": (width // COLS,)}
    block = lambda height: pl.BlockSpec((height, COLS), lambda i: (0, i))
    whole = lambda shape: pl.BlockSpec(shape, lambda i: (0,) * len(shape))
    return grid, block, whole


def turns(dom_count):
    half = dom_count // 2
    far = sorted(range(half, dom_count), key=lambda k: (k % 2, k))
    near = sorted(range(1, half), key=lambda k: (k % 2 == 0, k))
    cut = lambda order, n, of: order[n * len(order) // of : (n + 1) * len(order) // of]
    return [cut(far, n, 4) for n in range(4)], [cut(near, n, 3) for n in range(3)]


def send_in_turn(piece, order, arrived, *first):
    for key in order:
        value = hold(piece(key), *first) if first else piece(key)
        arrived[key] = swap(value, key[0], 0)
        first = (arrived[key],)
    return first[0]


def prepare_kernel(
    me, sends, block_ref, slot_ref, count_ref, adj_ref, tile_ref, *refs
):
    wide, flip, halo, halo_flip, chooser, total = refs
    rows = adj_ref.shape[0]
    row_count = adj_ref.shape[1] // rows
    blocks, peers, side = total.shape[0], total.shape[1], total.shape[2]
    for j in range(row_count):
        start = pl.multiple_of((me[1] ^ j) * rows, rows)
        piece = adj_ref[:, pl.ds(start, rows)]
        if j == 0:
            at_row = lax.broadcasted_iota(jnp.int32, (rows, rows), 0)
            at_col = lax.broadcasted_iota(jnp.int32, (rows, rows), 1)
            wide_piece = piece.astype(jnp.float32)
            piece = jnp.where(at_row == at_col, (1.0 + SELF_LOOP) * wide_piece, wide_piece).astype(
                jnp.bfloat16
            )
        wide[:, j * rows : (j + 1) * rows] = piece
        flip[j * rows : (j + 1) * rows, :] = piece.T
    total[...] = jnp.zeros(total.shape, total.dtype)

    def add(t, carry):
        b = block_ref[t]
        k = slot_ref[t] ^ me[0]
        total[b, k] = total[b, k] + tile_ref[t].astype(jnp.float32)
        return carry

    lax.fori_loop(0, count_ref[0], add, 0)
    for b in range(blocks):
        for k in range(peers):
            piece = total[b, k].astype(jnp.bfloat16)
            halo[b * side : (b + 1) * side, k * side : (k + 1) * side] = piece
            halo_flip[k * side : (k + 1) * side, b * side : (b + 1) * side] = piece.T
    same = lax.broadcasted_iota(jnp.int32, (side, side), 0) == lax.broadcasted_iota(
        jnp.int32, (side, side), 1
    )
    for k in range(peers - 1):
        for b in range(blocks):
            chooser[b * side : (b + 1) * side, k * side : (k + 1) * side] = jnp.where(
                jnp.logical_and(same, sends[me[0] ^ (k + 1)] == b), 1.0, 0.0
            ).astype(jnp.bfloat16)


def prepare(me, sends, tile_block, tile_slot, tile_count, adjacency, tiles, peers):
    rows, part = adjacency.shape
    side = tiles.shape[1]
    bf = jnp.bfloat16
    return call(
        prepare_kernel,
        flops=tiles.size,
        vmem_mb=20 + (10 * rows * peers * side >> 20),
        in_specs=[SMEM] * 5 + [VMEM] * 2,
        out_specs=[VMEM] * 5,
        out_shape=[
            SDS((rows, part), bf),
            SDS((part, rows), bf),
            SDS((rows, peers * side), bf),
            SDS((peers * side, rows), bf),
            SDS((rows, (peers - 1) * side), bf),
        ],
        scratch_shapes=[pltpu.VMEM((rows // side, peers, side, side), jnp.float32)],
        name="prepare",
    )(me, sends, tile_block, tile_slot, tile_count, adjacency, tiles)


def outgoing_kernel(me, sends, source, *targets):
    halves, blocks = targets[:2], targets[2:]
    rows, side = halves[0].shape[0], blocks[0].shape[0]
    for n, target in enumerate(halves):
        target[...] = source[n * rows : (n + 1) * rows, :]
    for k, target in enumerate(blocks):
        block = jnp.maximum(sends[me[0] ^ (k + 1)], 0)
        target[...] = source[pl.ds(pl.multiple_of(block * side, side), side), :]


def outgoing(me, sends, features, side):
    rows, width = features.shape
    count = sends.shape[0] - 1
    low = features.dtype
    first, second, *blocks = call(
        outgoing_kernel,
        flops=0,
        vmem_mb=12 + (count * side * width >> 19),
        in_specs=[SMEM, SMEM, VMEM],
        out_specs=[VMEM] * (2 + count),
        out_shape=[SDS((rows // 2, width), low)] * 2 + [SDS((side, width), low)] * count,
        name="outgoing",
    )(me, sends, features)
    return first, second, blocks


def near_kernel(wide, *refs):
    sources, out = refs[:-1], refs[-1]
    for c in range(out.shape[1] // COLS):
        cs = slice(c * COLS, (c + 1) * COLS)
        total, done = 0.0, 0
        for ref in sources:
            total += dot(wide[:, done : done + ref.shape[0]], ref[:, cs])
            done += ref.shape[0]
        out[:, cs] = total


def near(wide, sources):
    rows, width = sources[0].shape
    return call(
        near_kernel,
        flops=2 * wide.size * width,
        vmem_mb=16,
        in_specs=[VMEM] * (1 + len(sources)),
        out_specs=VMEM,
        out_shape=SDS((rows, width), jnp.float32),
        name="near",
    )(wide, *sources)


def halo_kernel(me, base, halo, *refs, row_count, blocked):
    arrived, (hidden, hidden_flip) = refs[:-2], refs[-2:]
    rows, side = hidden.shape[0], arrived[0].shape[0]
    per = rows // COLS
    count = base.shape[1] // COLS
    for c in range(count):
        cs = slice(c * COLS, (c + 1) * COLS)
        at = c + (pl.program_id(0) * count if blocked else 0)
        pieces = jnp.concatenate([ref[:, cs] for ref in arrived], axis=0)
        low = (base[:, cs] + dot(halo[:, side:], pieces)).astype(jnp.bfloat16)
        hidden[:, pl.ds(pl.multiple_of(at * COLS, COLS), COLS)] = low
        j = (at // per) ^ me[1]
        start = pl.multiple_of(j // 2 * rows + at % per * COLS, COLS)
        hidden_flip[j % 2, pl.ds(start, COLS), :] = low.T


def add_halo(me, base, halo, arrived, row_count):
    rows, width = base.shape
    blocked = halo.shape[1] > WHOLE_HALO
    grid, block, whole = columns(width, blocked)

    def kernel(*refs):
        halo_kernel(*refs, row_count=row_count, blocked=blocked)

    return call(
        kernel,
        flops=2 * halo.size * width,
        vmem_mb=56 if blocked else 16,
        in_specs=[SMEM, block(rows), whole(halo.shape)]
        + [block(a.shape[0]) for a in arrived],
        out_specs=[whole((rows, width)), whole((2, width // 2, rows))],
        out_shape=[SDS((rows, width), jnp.bfloat16), SDS((2, width // 2, rows), jnp.bfloat16)],
        name="add_halo",
        **grid,
    )(me, base, halo, *arrived)


def gelu_parts(v):
    inner = GELU_ROOT * (v + GELU_CUBE * (v * v * v))
    return jnp.tanh(inner)


def weight_starts(me, rows):
    half = rows // 2
    starts = [me[1] * rows, (me[1] ^ 1) * rows]
    for j in (2, 3):
        starts += [(me[1] ^ j) * rows, (me[1] ^ j) * rows + half]
    return [pl.multiple_of(start, half) for start in starts]


def linear_kernel(me, hidden, params, mask_ref, cot_ref, *refs):
    weights, (pre_first, pre_second, stats, act_ref) = refs[:-4], refs[-4:]
    rows, width = hidden.shape
    starts = weight_starts(me, rows)
    mask = mask_ref[...]
    count = jnp.sum(mask[:, 0:1])
    stats[4:8, :] = jnp.full((4, width), count, jnp.float32)
    for c in range(width // COLS):
        cs = slice(c * COLS, (c + 1) * COLS)
        v = params[0:1, cs] + sum(
            dot(hidden[:, pl.ds(start, ref.shape[0])], ref[:, cs])
            for start, ref in zip(starts, weights)
        )
        span = width // 2
        preact = pre_second if c * COLS >= span else pre_first
        preact[:, c * COLS % span : c * COLS % span + COLS] = v
        act_ref[...] = 0.5 * v * (1.0 + gelu_parts(v))
        for part in range(COLS // LANES):
            here = slice(part * LANES, (part + 1) * LANES)
            there = slice(c * COLS + part * LANES, c * COLS + (part + 1) * LANES)
            act = act_ref[:, here]
            mean = jnp.sum(mask * act, axis=0, keepdims=True) / count
            centred = act - mean
            grad = mask * cot_ref[:, there].astype(jnp.float32)
            stats[0:1, there] = mean
            stats[1:2, there] = jnp.sum(mask * centred * centred, axis=0, keepdims=True)
            stats[2:3, there] = jnp.sum(grad, axis=0, keepdims=True)
            stats[3:4, there] = jnp.sum(grad * centred, axis=0, keepdims=True)


def linear(me, hidden, params, mask, cotangent, weights):
    rows, width = hidden.shape
    return call(
        linear_kernel,
        flops=2 * rows * width * width,
        vmem_mb=16,
        in_specs=[SMEM] + [VMEM] * (4 + len(weights)),
        out_specs=[VMEM] * 3,
        out_shape=[SDS((rows, width // 2), jnp.float32)] * 2
        + [SDS((STAT_ROWS, width), jnp.float32)],
        scratch_shapes=[pltpu.VMEM((rows, COLS), jnp.float32)],
        name="linear",
    )(me, hidden, params, mask, cotangent, *weights)


def merged(mine, refs, ordered):
    for i, ref in enumerate(refs):
        ordered[mine ^ i] = ref[...]
    parts = [ordered[i] for i in range(len(refs))]
    count = sum(p[4:5] for p in parts)
    mean = sum(p[4:5] * p[0:1] for p in parts) / count
    spread = sum(p[1:2] + p[4:5] * (p[0:1] - mean) * (p[0:1] - mean) for p in parts)
    shift = sum(p[2:3] for p in parts)
    scale = sum(p[3:4] + (p[0:1] - mean) * p[2:3] for p in parts)
    return mean, spread, shift, scale, count


def merge_kernel(mine, *refs):
    out, ordered = refs[-2:]
    for i, row in enumerate(merged(mine[0], refs[:-2], ordered)):
        out[i : i + 1, :] = row
    out[5:8, :] = jnp.zeros((3, out.shape[1]), jnp.float32)


def merge(mine, parts):
    return call(
        merge_kernel,
        flops=20 * parts[0].size * len(parts),
        vmem_mb=8,
        in_specs=[SMEM] + [VMEM] * len(parts),
        out_specs=VMEM,
        out_shape=SDS(parts[0].shape, jnp.float32),
        scratch_shapes=[pltpu.VMEM((len(parts),) + parts[0].shape, jnp.float32)],
        name="merge",
    )(mine[None], *parts)


def groups(dom_count, row_count):
    flips = [(0, 1 << i) for i in range(row_count.bit_length() - 1)]
    flips += [(1 << i, 0) for i in range(dom_count.bit_length() - 1)]
    return [flips[:1]] + [flips[i : i + 2] for i in range(1, len(flips), 2)]


def exchange(value, group):
    parts = [value]
    for i in range(1, 1 << len(group)):
        picked = [flip for j, flip in enumerate(group) if i >> j & 1]
        parts.append(swap(value, sum(f[0] for f in picked), sum(f[1] for f in picked)))
    return parts


def exchange_stats(stats, dom_at, row_at, dom_count, row_count):
    rounds = groups(dom_count, row_count)
    for n, group in enumerate(rounds):
        mine = jnp.int32(0)
        for i, (d, r) in enumerate(group):
            bit = (row_at & r) != 0 if r else (dom_at & d) != 0
            mine = mine + (bit.astype(jnp.int32) << i)
        parts = exchange(stats, group)
        if n < len(rounds) - 1:
            stats = merge(mine, parts)
    return mine, parts


def pair_sum(value, group, *others):
    parts = exchange(hold(value, *others) if others else value, group)
    while len(parts) > 1:
        parts = [a + b for a, b in zip(parts[::2], parts[1::2])]
    return parts[0]


def backward_kernel(mine, params, mask_ref, cot_in, pre_in, *refs, first, part_count):
    parts = refs[:part_count]
    grad_pre, sums, output, ordered, cot_ref, pre_ref, out_ref, sems, out_sems = refs[-9:]
    rows, span = grad_pre.shape
    step = rows // 4
    there = pl.ds(first, span)
    copies, sent = [], []
    for n in range(4):
        here = pl.ds(n * step, step)
        copies += [
            pltpu.make_async_copy(pre_in.at[here, :], pre_ref.at[here, :], sems.at[0, n]),
            pltpu.make_async_copy(cot_in.at[here, there], cot_ref.at[here, :], sems.at[1, n]),
        ]
    for copy in copies:
        copy.start()
    mean, spread, shift_grad, scale_sum, count = merged(mine[0], parts, ordered)
    inverse = lax.rsqrt(spread / count + NORM_EPS)
    scale_grad = scale_sum * inverse
    scale, shift = params[1:2, :], params[2:3, :]
    gain = scale * inverse
    shift_mean, scale_mean = shift_grad / count, scale_grad / count
    for i, row in enumerate((scale_grad, shift_grad)):
        sums[i + 1 : i + 2, :] = row[:, first : first + span]
    sums[3:8, :] = jnp.zeros((5, span), jnp.float32)
    for n in range(4):
        for copy in copies[2 * n : 2 * n + 2]:
            copy.wait()
        at = slice(n * step, (n + 1) * step)
        mask = mask_ref[at, :]
        for part in range(span // LANES):
            here = slice(part * LANES, (part + 1) * LANES)
            of = slice(first + part * LANES, first + (part + 1) * LANES)
            v = pre_ref[at, here]
            bend = gelu_parts(v)
            act = 0.5 * v * (1.0 + bend)
            normed = (act - mean[:, of]) * inverse[:, of]
            out_ref[at, here] = (mask * (scale[:, of] * normed + shift[:, of])).astype(jnp.bfloat16)
            grad_out = mask * cot_ref[at, here].astype(jnp.float32)
            grad_act = (
                mask * gain[:, of] * (grad_out - shift_mean[:, of] - normed * scale_mean[:, of])
            )
            slope = 0.5 * (1.0 + bend) + 0.5 * v * (1.0 - bend * bend) * (
                GELU_ROOT * (1.0 + 3.0 * GELU_CUBE * (v * v))
            )
            low = (grad_act * slope).astype(jnp.bfloat16)
            grad_pre[at, here] = low
            total = jnp.sum(low.astype(jnp.float32), axis=0, keepdims=True)
            sums[0:1, here] = total if n == 0 else sums[0:1, here] + total
        here = pl.ds(n * step, step)
        sent.append(
            pltpu.make_async_copy(out_ref.at[here, :], output.at[here, there], out_sems.at[n])
        )
        sent[-1].start()
    for copy in sent:
        copy.wait()


def backward(mine, params, mask, cotangent, preact, parts, part, output):
    rows, span = preact.shape
    width = cotangent.shape[1]
    before = [] if output is None else [output]

    def kernel(*refs):
        backward_kernel(*refs, first=part * span, part_count=len(parts))

    return call(
        kernel,
        flops=50 * rows * span,
        vmem_mb=56,
        in_specs=[SMEM, VMEM, VMEM, ANY, ANY] + [VMEM] * len(parts) + [ANY] * len(before),
        out_specs=[VMEM, VMEM, ANY],
        out_shape=[
            SDS((rows, span), jnp.bfloat16),
            SDS((STAT_ROWS, span), jnp.float32),
            SDS((rows, width), jnp.bfloat16),
        ],
        scratch_shapes=[
            pltpu.VMEM((len(parts), STAT_ROWS, width), jnp.float32),
            pltpu.VMEM((rows, span), jnp.bfloat16),
            pltpu.VMEM((rows, span), jnp.float32),
            pltpu.VMEM((rows, span), jnp.bfloat16),
            pltpu.SemaphoreType.DMA((2, 4)),
            pltpu.SemaphoreType.DMA((4,)),
        ],
        input_output_aliases={5 + len(parts): 2} if before else {},
        name="backward",
    )(mine[None], params, mask, cotangent, preact, *parts, *before)


def outers_kernel(me, *refs):
    inputs, outputs, buffers = list(refs[:6]), refs[6:10], refs[10:16]
    low_ref, sems, out_sems = refs[16:]
    inputs[0] = inputs[0].at[0]
    copies = [
        pltpu.make_async_copy(source, buffer, sems.at[n])
        for n, (source, buffer) in enumerate(zip(inputs, buffers))
    ]
    for copy in copies:
        copy.start()
    own_flip, near_flip = buffers[:2]
    rows, span = buffers[2].shape
    half = rows // 2
    sent = []
    for part in range(2):
        for n in ((0, 1, 2, 3), (4, 5))[part]:
            copies[n].wait()
        grad, near_grad = buffers[2 + 2 * part : 4 + 2 * part]
        for c in range(span // COLS):
            cs = slice(c * COLS, (c + 1) * COLS)
            total = dot(own_flip[...], grad[:, cs]) + dot(near_flip[...], near_grad[:, cs])
            low_ref[part, :, cs] = total.astype(jnp.bfloat16)
        for n in range(2):
            here = pl.ds(n * half, half)
            if part:
                kept, given = (
                    pl.multiple_of(n * rows + flag * half, half) for flag in (me[2], 1 - me[2])
                )
            else:
                kept, given = n * half, rows + n * half
            for m, start in enumerate((kept, given)):
                sent.append(
                    pltpu.make_async_copy(
                        low_ref.at[part, pl.ds(start, half), :],
                        outputs[2 * part + m].at[here, :],
                        out_sems.at[part, m, n],
                    )
                )
                sent[-1].start()
    for copy in sent:
        copy.wait()


def outers(me, hidden_flip, near_flip, grads, near_grads):
    rows, span = grads[0].shape
    low = jnp.bfloat16
    inputs = [hidden_flip, near_flip, grads[0], near_grads[0], grads[1], near_grads[1]]
    return call(
        outers_kernel,
        flops=0,
        vmem_mb=56,
        in_specs=[SMEM] + [ANY] * 6,
        out_specs=[ANY] * 4,
        out_shape=[SDS((rows, span), low)] * 4,
        scratch_shapes=[pltpu.VMEM(v.shape[-2:], low) for v in inputs]
        + [
            pltpu.VMEM((2, 2 * rows, span), low),
            pltpu.SemaphoreType.DMA((6,)),
            pltpu.SemaphoreType.DMA((2, 2, 2)),
        ],
        name="outers",
    )(me, *inputs)


def hidden_kernel(me, *refs, piece_total, slot_total, halved):
    inputs, refs = refs[: 3 + piece_total], refs[3 + piece_total :]
    outputs, refs = refs[: 1 + slot_total], refs[1 + slot_total :]
    buffers, refs = refs[: 3 + piece_total], refs[3 + piece_total :]
    grad_hidden, slots, sems, out_sem, slot_sems = refs
    grads, weights, halo_flip = buffers[:2], buffers[2:-1], buffers[-1]
    copies = [
        pltpu.make_async_copy(source, buffer, sems.at[n])
        for n, (source, buffer) in enumerate(zip(inputs, buffers))
    ]
    for copy in copies:
        copy.start()
    rows, width = grad_hidden.shape
    span = grads[0].shape[1]
    for copy in copies[:2]:
        copy.wait()
    for start, ref, copy in zip(weight_starts(me, rows), weights, copies[2:]):
        copy.wait()
        for c in range(ref.shape[0] // COLS):
            total = sum(
                dot(
                    grad[...],
                    ref[c * COLS : (c + 1) * COLS, p * span : (p + 1) * span],
                    BOTH_LAST,
                )
                for p, grad in enumerate(grads)
            )
            at = pl.multiple_of(start + c * COLS, COLS)
            grad_hidden[:, pl.ds(at, COLS)] = total.astype(jnp.bfloat16)
    out_copy = pltpu.make_async_copy(grad_hidden, outputs[0], out_sem)
    out_copy.start()
    copies[-1].wait()
    side = slots.shape[1] // SLOT_GROUP
    count = halo_flip.shape[0] // side - 1
    targets = list(outputs[1:])
    pending = {}
    for first in range(0, count, SLOT_GROUP):
        taken = min(SLOT_GROUP, count - first)
        buffer = first // SLOT_GROUP % 2
        for copy in pending.pop(buffer, ()):
            copy.wait()
        for c in range(width // COLS):
            cs = slice(c * COLS, (c + 1) * COLS)
            picked = halo_flip[(first + 1) * side : (first + 1 + taken) * side, :]
            slots[buffer, : taken * side, cs] = dot(picked, grad_hidden[:, cs]).astype(jnp.bfloat16)
        pending[buffer] = []
        for n in range(taken):
            for part in range(2 if first + n + 1 in halved else 1):
                target = targets.pop(0)
                height = target.shape[0]
                pending[buffer].append(
                    pltpu.make_async_copy(
                        slots.at[buffer, pl.ds(n * side + part * height, height), :],
                        target,
                        slot_sems.at[buffer, n, part],
                    )
                )
                pending[buffer][-1].start()
    for copy in sum(pending.values(), [out_copy]):
        copy.wait()


def hidden_grads(me, grads, weights, halo_flip, side, halved):
    rows, span = grads[0].shape
    width = 2 * span
    count = halo_flip.shape[0] // side - 1
    low = jnp.bfloat16
    shapes = []
    for k in range(1, count + 1):
        shapes += [SDS((side // 2, width), low)] * 2 if k in halved else [SDS((side, width), low)]
    inputs = [*grads, *weights, halo_flip]

    def kernel(*refs):
        hidden_kernel(*refs, piece_total=len(weights), slot_total=len(shapes), halved=halved)

    grad_hidden, *outs = call(
        kernel,
        flops=0,
        vmem_mb=56,
        in_specs=[SMEM] + [ANY] * len(inputs),
        out_specs=[ANY] * (1 + len(shapes)),
        out_shape=[SDS((rows, width), low)] + shapes,
        scratch_shapes=[pltpu.VMEM(v.shape, low) for v in inputs]
        + [
            pltpu.VMEM((rows, width), low),
            pltpu.VMEM((2 if count > SLOT_GROUP else 1, SLOT_GROUP * side, width), low),
            pltpu.SemaphoreType.DMA((len(inputs),)),
            pltpu.SemaphoreType.DMA,
            pltpu.SemaphoreType.DMA((2, SLOT_GROUP, 2)),
        ],
        name="hidden_grads",
    )(me, *inputs)
    slots = {}
    for k in range(1, count + 1):
        for part in range(2 if k in halved else 1):
            slots[k, part] = outs.pop(0)
    return grad_hidden, slots


def near_back_kernel(*refs, row_count):
    flips, grads, out = refs[:row_count], refs[row_count:-1], refs[-1]
    rows = flips[0].shape[0]
    for c in range(out.shape[1] // COLS):
        cs = slice(c * COLS, (c + 1) * COLS)
        total, done = 0.0, 0
        for grad in grads:
            depth = grad.shape[0]
            total += dot(flips[done // rows][:, done % rows : done % rows + depth], grad[:, cs])
            done += depth
        out[:, cs] = total


def near_back(flips, grads):
    rows, width = grads[0].shape

    def kernel(*refs):
        near_back_kernel(*refs, row_count=len(flips))

    return call(
        kernel,
        flops=2 * rows * rows * len(flips) * width,
        vmem_mb=56,
        in_specs=[VMEM] * (len(flips) + len(grads)),
        out_specs=VMEM,
        out_shape=SDS((rows, width), jnp.float32),
        name="near_back",
    )(*flips, *grads)


def return_kernel(chooser, base, *refs):
    returned, out = refs[:-1], refs[-1]
    for c in range(out.shape[1] // COLS):
        cs = slice(c * COLS, (c + 1) * COLS)
        pieces = jnp.concatenate([ref[:, cs] for ref in returned], axis=0)
        out[:, cs] = (base[:, cs] + dot(chooser[...], pieces)).astype(jnp.bfloat16)


def give_back(chooser, base, returned):
    rows, width = base.shape
    blocked = chooser.shape[1] > WHOLE_HALO
    grid, block, whole = columns(width, blocked)
    return call(
        return_kernel,
        flops=2 * rows * chooser.shape[1] * width,
        vmem_mb=56,
        in_specs=[whole(chooser.shape), block(rows)]
        + [block(r.shape[0]) for r in returned],
        out_specs=block(rows),
        out_shape=SDS((rows, width), jnp.bfloat16),
        name="give_back",
        **grid,
    )(chooser, base, *returned)


def lamb_step(value, grad, first, second, decay):
    first_new = DECAY_FIRST * first + (1.0 - DECAY_FIRST) * grad
    second_new = DECAY_SECOND * second + (1.0 - DECAY_SECOND) * grad * grad
    update = (
        first_new
        / (1.0 - DECAY_FIRST**STEP)
        / (jnp.sqrt(second_new / (1.0 - DECAY_SECOND**STEP)) + ADAM_EPS)
        + decay * value
    )
    return (first_new, second_new, update)


def first_sums_kernel(me, keep_a, came_a, keep_b, came_b, kept_a, sent_a, kept_b, sent_b):
    half = kept_a.shape[0]
    for flag, out in ((me[2], kept_a), (1 - me[2], sent_a)):
        rows = pl.ds(pl.multiple_of(flag * half, half), half)
        out[...] = (keep_a[rows, :].astype(jnp.float32) + came_a[rows, :].astype(jnp.float32)).astype(out.dtype)
    for n, out in enumerate((kept_b, sent_b)):
        rows = slice(n * half, (n + 1) * half)
        out[...] = (keep_b[rows, :].astype(jnp.float32) + came_b[rows, :].astype(jnp.float32)).astype(out.dtype)


def first_sums(me, keep_a, came_a, keep_b, came_b):
    rows, span = keep_a.shape
    kept, sent = SDS((rows // 2, span), jnp.float32), SDS((rows // 2, span), jnp.bfloat16)
    return call(
        first_sums_kernel,
        flops=0,
        vmem_mb=56,
        in_specs=[SMEM] + [VMEM] * 4,
        out_specs=[VMEM] * 4,
        out_shape=[kept, sent, kept, sent],
        name="first_sums",
    )(me, keep_a, came_a, keep_b, came_b)


def joined_kernel(flag, kept_a, came_a, kept_b, came_b, kept, sent):
    half, span = kept.shape[0], kept_a.shape[1]
    for n, (keep, came) in enumerate(((kept_a, came_a), (kept_b, came_b))):
        cs = slice(n * span, (n + 1) * span)
        for bit, out in ((flag[0], kept), (1 - flag[0], sent)):
            rows = pl.ds(pl.multiple_of(bit * half, half), half)
            out[:, cs] = (keep[rows, :] + came[rows, :].astype(jnp.float32)).astype(out.dtype)


def joined(flag, kept_a, came_a, kept_b, came_b):
    rows, span = kept_a.shape
    return call(
        joined_kernel,
        flops=0,
        vmem_mb=56,
        in_specs=[SMEM] + [VMEM] * 4,
        out_specs=[VMEM] * 2,
        out_shape=[
            SDS((rows // 2, 2 * span), jnp.float32),
            SDS((rows // 2, 2 * span), jnp.bfloat16),
        ],
        name="joined",
    )(flag[None], kept_a, came_a, kept_b, came_b)


def halved_kernel(flag, keep, came, kept, sent):
    half = kept.shape[0]
    for bit, out in ((flag[0], kept), (1 - flag[0], sent)):
        rows = pl.ds(pl.multiple_of(bit * half, half), half)
        out[...] = (keep[rows, :] + came[rows, :].astype(jnp.float32)).astype(out.dtype)


def halved_sums(flag, keep, came):
    rows, width = keep.shape
    return call(
        halved_kernel,
        flops=0,
        vmem_mb=56,
        in_specs=[SMEM] + [VMEM] * 2,
        out_specs=[VMEM] * 2,
        out_shape=[SDS((rows // 2, width), jnp.float32), SDS((rows // 2, width), jnp.bfloat16)],
        name="halved_sums",
    )(flag[None], keep, came)


def piece_kernel(start, kept, came, sums, value_in, first_in, second_in, piece, totals, value, first, second, sems):
    rows = piece.shape[0]
    here = pl.ds(pl.multiple_of(start[0], rows), rows)
    copies = [
        pltpu.make_async_copy(source.at[here, :], target, sems.at[n])
        for n, (source, target) in enumerate(
            zip((value_in, first_in, second_in), (value, first, second))
        )
    ]
    for copy in copies:
        copy.start()
    low = (kept[...] + came[...].astype(jnp.float32)).astype(jnp.bfloat16)
    piece[...] = low
    for copy in copies:
        copy.wait()
    update = lamb_step(
        value[...], low.astype(jnp.float32), first[...], second[...], WEIGHT_DECAY
    )[2]
    totals[0:1, :] = sums[0:1, :]
    totals[1:2, :] = jnp.sum(value[...] * value[...], axis=0, keepdims=True)
    totals[2:3, :] = jnp.sum(update * update, axis=0, keepdims=True)
    totals[3:8, :] = jnp.zeros((5, totals.shape[1]), jnp.float32)


def piece_totals(start, kept, came, sums, weight, first, second):
    rows, width = kept.shape
    return call(
        piece_kernel,
        flops=0,
        vmem_mb=56,
        in_specs=[SMEM, VMEM, VMEM, VMEM, ANY, ANY, ANY],
        out_specs=[VMEM, VMEM],
        out_shape=[SDS((rows, width), jnp.bfloat16), SDS((STAT_ROWS, width), jnp.float32)],
        scratch_shapes=[pltpu.VMEM((rows, width), jnp.float32)] * 3
        + [pltpu.SemaphoreType.DMA((3,))],
        name="piece_totals",
    )(start[None], kept, came, sums, weight, first, second)


def by_bit(flag, own, came):
    rows, width = own.shape
    mine = (jnp.arange(2, dtype=jnp.int32) == flag)[:, None, None]
    return jnp.where(mine, own[None], came[None]).reshape(2 * rows, width)


def on_device(
    features,
    adjacency,
    tile_values,
    tile_block,
    tile_slot,
    tile_count,
    send_block,
    node_mask,
    weight,
    params,
    weight_first,
    weight_second,
    params_first,
    params_second,
    cotangent,
):
    dom_count, row_count = lax.axis_size("dom"), lax.axis_size("row")
    dom_at, row_at = lax.axis_index("dom"), lax.axis_index("row")
    rows, width = features.shape
    side = tile_values.shape[1]
    side_bit = dom_at % 2
    me = jnp.stack([dom_at, row_at, side_bit]).astype(jnp.int32)
    sends = send_block[0]
    mask = jnp.broadcast_to(node_mask.astype(jnp.float32)[:, None], (rows, LANES))

    half = rows // 2
    low_weight = weight.astype(jnp.bfloat16)
    first_half, second_half, blocks = outgoing(me, sends, features, side)
    wide, flip, halo, halo_flip, chooser = prepare(
        me, sends, tile_block, tile_slot, tile_count, adjacency, tile_values, dom_count
    )

    far, light = turns(dom_count)
    arrived = {}
    whole = lambda order: [(k, 0) for k in order]
    out = lambda key: blocks[key[0] - 1]
    far_first = swap(first_half, 0, 2)
    near_features = swap(features, 0, 1)
    turn = [
        far_first,
        near_features,
        send_in_turn(out, whole(far[0]), arrived),
        send_in_turn(out, whole(light[0]), arrived),
    ]
    far_second = swap(hold(second_half, *turn), 0, 2)
    cross = [swap(hold(far_first, *turn), 0, 1)]
    turn = [
        far_second,
        cross[0],
        send_in_turn(out, whole(far[1]), arrived, *turn),
        send_in_turn(out, whole(light[1]), arrived, *turn),
    ]
    over_y = swap(hold(low_weight[:half], *turn), 0, 2)
    cross.append(swap(hold(far_second, *turn), 0, 1))
    near_weight = swap(hold(low_weight, *turn), 0, 1)
    turn = [
        over_y,
        cross[1],
        near_weight,
        send_in_turn(out, whole(far[2]), arrived, *turn),
        send_in_turn(out, whole(light[2]), arrived, *turn),
    ]
    over_y_too = swap(hold(low_weight[half:], *turn), 0, 2)
    send_in_turn(out, whole(far[3]), arrived, *turn)
    base = near(wide, [features, near_features, far_first, far_second] + cross)
    weights = [
        low_weight,
        near_weight,
        over_y,
        over_y_too,
        swap(hold(over_y, base), 0, 1),
        swap(over_y_too, 0, 1),
    ]
    arrived = [arrived[k, 0] for k in range(1, dom_count)]
    hidden, hidden_flip = add_halo(me, base, halo, arrived, row_count)
    pre_first, pre_second, stats = linear(me, hidden, params, mask, cotangent, weights)
    mine, parts = exchange_stats(stats, dom_at, row_at, dom_count, row_count)
    near_flip = swap(hidden_flip[1], 0, 1)

    mine = hold(mine, near_flip)
    output, grads, near_pre, sums = None, [], [], []
    for part, preact in enumerate((pre_first, pre_second)):
        grad_pre, sum_part, output = backward(
            mine, params, mask, cotangent, preact, parts, part, output
        )
        grads.append(grad_pre)
        near_pre.append(swap(grad_pre, 0, 1))
        sums.append(sum_part)
    sums = jnp.concatenate(sums, axis=1)
    halved = far[2] + far[3]
    keep_a, send_a, keep_b, send_b = outers(me, hidden_flip, near_flip, grads, near_pre)
    grad_hidden, slots = hidden_grads(me, grads, weights, halo_flip, side, halved)

    returned = {}
    part_of = lambda order, n: [(k, n) for k in order]
    bit = lambda step: (dom_at // step) % 2
    blocks_back = lambda order, *turn: send_in_turn(lambda k: slots[k], order, returned, *turn)

    turn_flip = lambda j, *turn: swap(hold(flip[j * rows : (j + 1) * rows], *turn), 0, j)
    rounds = groups(dom_count, row_count)

    start, span = 0, rows
    for step in [1 << n for n in range(dom_count.bit_length() - 1)]:
        span //= 2
        start = start + bit(step) * span
    small_steps = sum(rounds, [])

    flips = [flip[:rows], turn_flip(1, send_a), None, None]
    turn = [swap(send_a, 0, 2), swap(send_b, 1, 0), flips[1], grad_hidden]
    kept_a, sent_a, kept_b, sent_b = first_sums(me, keep_a, turn[0], keep_b, turn[1])
    near_grad = swap(hold(grad_hidden, *turn), 0, 1)
    flips[2] = turn_flip(2, *turn)
    turn = [
        swap(hold(sent_a, *turn), 1, 0),
        swap(hold(sent_b, *turn), 0, 2),
        blocks_back(whole(far[0]), *turn),
        near_grad,
        flips[2],
    ]
    kept, sent = joined(bit(2), kept_a, turn[0], kept_b, turn[1])
    steps = [1 << n for n in range(1, dom_count.bit_length() - 1)]
    quarter = rows // 4
    grad_parts, cross = [], []

    def over_y_back(*turn):
        n = len(grad_parts)
        grad_parts.append(
            swap(hold(grad_hidden[n * quarter : (n + 1) * quarter], *turn), 0, 2)
        )
        if n:
            cross.append(swap(hold(grad_parts[n - 1], *turn), 0, 1))
        return [grad_parts[n]] + cross[n - 1 : n]

    beside = [
        [part_of(far[2], 0), whole(light[0])],
        [part_of(far[2], 1), whole(light[1])],
        [part_of(far[3], 0)],
        [part_of(far[3], 1)],
    ]
    for n, step in enumerate(steps):
        came = swap(hold(sent, *turn), step, 0)
        more = []
        if n < 2:
            more = [blocks_back(order, *turn) for order in beside[n]] + over_y_back(*turn)
        turn = [came] + more
        if step < dom_count // 2:
            kept, sent = halved_sums(bit(2 * step), kept, came)
    weight_grad, totals = piece_totals(
        start, kept, came, sums, weight, weight_first, weight_second
    )
    for n, step in enumerate(reversed(steps)):
        came = swap(hold(weight_grad, *turn), step, 0)
        more = []
        if n < 2:
            more = [blocks_back(order, *turn) for order in beside[2 + n]] + over_y_back(*turn)
            for flip_bits in small_steps[:3] if n == 0 else small_steps[3:]:
                totals = pair_sum(totals, [flip_bits], *turn)
            more.append(totals)
        weight_grad = by_bit(bit(step), weight_grad, came)
        turn = [came] + more
    came = swap(hold(weight_grad, *turn), 1, 0)
    blocks_back(whole(far[1]), *turn)
    blocks_back(whole(light[2]), *turn)
    cross.append(swap(hold(grad_parts[-1], *turn), 0, 1))
    flips[3] = turn_flip(3, *turn)
    bias_grad = totals[0:1]
    weight_norms = jnp.sqrt(jnp.sum(totals[1:3], axis=1))
    base = near_back(flips, [grad_hidden, near_grad] + grad_parts + cross)
    weight_grad = by_bit(bit(1), weight_grad, hold(came, base)).astype(jnp.float32)
    returned = [returned[key] for key in sorted(returned)]
    weight_first_new, weight_second_new, weight_update = lamb_step(
        weight, weight_grad, weight_first, weight_second, WEIGHT_DECAY
    )
    weight_new = (
        weight - LEARN_RATE * (weight_norms[0] / (weight_norms[1] + TRUST_EPS)) * weight_update
    )

    grad_features = give_back(chooser, hold(base, weight_new), returned)
    param_grads = jnp.concatenate([bias_grad, sums[1:3]], axis=0)
    params_first_new, params_second_new, param_update = lamb_step(
        params, param_grads, params_first, params_second, 0.0
    )
    param_norms = jnp.sqrt(jnp.sum(params * params, axis=1, keepdims=True))
    update_norms = jnp.sqrt(jnp.sum(param_update * param_update, axis=1, keepdims=True))
    params_new = params - LEARN_RATE * (param_norms / (update_norms + TRUST_EPS)) * param_update
    norms = jnp.concatenate(
        [weight_norms[None, :], jnp.concatenate([param_norms, update_norms], axis=1)], axis=0
    )
    return (
        output,
        grad_features,
        weight_new,
        weight_new.astype(jnp.bfloat16),
        weight_first_new,
        weight_second_new,
        params_new,
        params_first_new,
        params_second_new,
        norms,
    )


def solution(mesh):
    in_specs = (
        P(("dom", "row"), None),
        P(("dom", "row"), None),
        P(("dom", "row"), None, None),
        P(("dom", "row")),
        P(("dom", "row")),
        P(("dom", "row")),
        P(("dom", "row"), None),
        P(("dom", "row")),
        P("row", None),
        P(),
        P("row", None),
        P("row", None),
        P(),
        P(),
        P(("dom", "row"), None),
    )
    out_specs = (
        P(("dom", "row"), None),
        P(("dom", "row"), None),
        P("row", None),
        P("row", None),
        P("row", None),
        P("row", None),
        P(),
        P(),
        P(),
        P(),
    )
    return jax.shard_map(
        on_device, mesh=mesh, in_specs=in_specs, out_specs=out_specs, check_vma=False
    )
```

time: 993 us -> 395 us (0.40)
  matrix products: 284 us -> 0 us
  blocking collectives: 284 us -> 0 us
  local copies, waits for them, and re-layouts: 170 us -> 20.4 us
  Pallas kernels: 0 us -> 90 us
  starting transfers between devices: 12.8 us -> 66.3 us
  other arithmetic: 58.6 us -> 16.5 us
  waiting for transfers between devices: 159 us -> 194 us
  between operations: 16.2 us -> 3.67 us
    psum x5 -> x0, blocking collectives: 284 us -> none  [the longest x1 158 us: on_device(): lax.psum((weight_local, bias_local), ('dom', 'row'))]
    dot_general x13 -> x0, matrix products: 284 us -> none  [the longest x1 59 us: on_device(): jnp.einsum('tij,tjf->tif', tile_values, picked, preferred_element_type=jn...]
    ppermute x0 -> x62, waiting for transfers between devices: none -> 194 us  [swap(): return lax.ppermute(value, AXES, pairs)]
    dot_general x4 -> x0, local copies, waits for them, and re-layouts: 152 us -> none  [the longest x1 72 us: on_device(): jnp.einsum('tij,tif->tjf', tile_values, hidden_rows, preferred_element_ty...]
    pallas_call x0 -> x17, Pallas kernels: none -> 90 us  [the longest x1 15.3 us: hidden_grads(): call(kernel, flops=0, vmem_mb=56, in_specs=[SMEM] + [ANY] * len(inputs),...]
    all_to_all x2 -> x0, waiting for transfers between devices: 81.6 us -> none  [the longest x1 81.6 us: on_device(): lax.all_to_all(outgoing.reshape(peer_count * block_rows, feat_width), 'do...]
    reduce_scatter x1 -> x0, waiting for transfers between devices: 76.8 us -> none  [on_device(): lax.psum_scatter(jnp.einsum('rp,rf->pf', columns, grad_hidden, preferred_...]
    ppermute x0 -> x62, starting transfers between devices: none -> 66.3 us  [swap(): return lax.ppermute(value, AXES, pairs)]
  transfers between devices with their start and end apart: 6 -> 62, of which waited for: 2 -> 28; matrix products, arithmetic and copies ran while one was open for 47% -> 5% of each run, Pallas kernels for 0% -> 16%
where the time goes in v2:
time: 395 us; the launch traced here: 391 us
  waiting for transfers between devices  194 us (49%)
  Pallas kernels  90 us (23%)
  starting transfers between devices  66.3 us (17%)
  local copies, waits for them, and re-layouts  20.4 us (5%)
  other arithmetic  16.5 us (4%)
    ppermute x62, waiting for transfers between devices, swap(): return lax.ppermute(value, AXES, pairs)  194 us
    ppermute x62, starting transfers between devices, swap(): return lax.ppermute(value, AXES, pairs)  66.3 us
    unnamed x135, local copies, waits for them, and re-layouts  15.8 us
    pallas_call x1, Pallas kernels, hidden_grads(): call(kernel, flops=0, vmem_mb=56, in_specs=[SMEM] + [ANY] * len(inputs),...  15.3 us
    pallas_call x1, Pallas kernels, near_back(): call(kernel, flops=2 * rows * rows * len(flips) * width, vmem_mb=56, in_s...  12.8 us
    pallas_call x2, Pallas kernels, backward(): call(kernel, flops=50 * rows * span, vmem_mb=56, in_specs=[SMEM, VMEM, VM...  12.3 us
    convert_element_type x1, other arithmetic, on_device(): weight_new.astype(jnp.bfloat16)  9.53 us
    pallas_call x1, Pallas kernels, outers(): call(outers_kernel, flops=0, vmem_mb=56, in_specs=[SMEM] + [ANY] * 6, out...  8.99 us
  transfers between devices with their start and end apart: 62, of which 28 were waited for; matrix products, arithmetic and copies ran while one was open for 5% of the time, Pallas kernels for 16%

profile of v2, /device:TPU:0, one launch (start us, length us, event | category | flops | bytes accessed | tf_op | source)
XLA Modules:
  0.0 391.2 jit_solution(2403421799017040885)
XLA Ops:
  11.1 22.1 %collective-permute-done.2.refs_6_ = bf16[128,2048]{1,0:T(8,128)(2,1)S(1)} collective-permute-done((bf16[128,2048]{1,0:T(8,128)(2,1)S(1)}, bf16[128,2048]{1,0:T(8,128)(2,1)S(1)}, u32[]{:S(2)}, u32[]{:S(2)}) %collective-permute-start.2) | collective-permute-done | bytes 524320 | tf_op jit(solution)/shard_map/ppermute | solution.py:50
  41.5 8.4 %collective-permute-done.7.refs_5_ = bf16[128,2048]{1,0:T(8,128)(2,1)S(1)} collective-permute-done((bf16[128,2048]{1,0:T(8,128)(2,1)S(1)}, bf16[128,2048]{1,0:T(8,128)(2,1)S(1)}, u32[]{:S(2)}, u32[]{:S(2)}) %collective-permute-start.7) | collective-permute-done | bytes 524320 | tf_op jit(solution)/shard_map/ppermute | solution.py:50
  49.9 12.3 %collective-permute-done.6.refs_8_ = bf16[128,2048]{1,0:T(8,128)(2,1)S(1)} collective-permute-done((bf16[128,2048]{1,0:T(8,128)(2,1)S(1)}, bf16[128,2048]{1,0:T(8,128)(2,1)S(1)}, u32[]{:S(2)}, u32[]{:S(2)}) %collective-permute-start.6) | collective-permute-done | bytes 524320 | tf_op jit(solution)/shard_map/ppermute | solution.py:50
  68.3 23.2 %collective-permute-done.10.refs_7_ = bf16[128,2048]{1,0:T(8,128)(2,1)S(1)} collective-permute-done((bf16[128,2048]{1,0:T(8,128)(2,1)S(1)}, bf16[128,2048]{1,0:T(8,128)(2,1)S(1)}, u32[]{:S(2)}, u32[]{:S(2)}) %collective-permute-start.10) | collective-permute-done | bytes 524320 | tf_op jit(solution)/shard_map/ppermute | solution.py:50
  105.5 10.5 %collective-permute-done.15.refs_3_.refs_6_ = bf16[256,2048]{1,0:T(8,128)(2,1)S(1)} collective-permute-done((bf16[256,2048]{1,0:T(8,128)(2,1)S(1)}, bf16[256,2048]{1,0:T(8,128)(2,1)S(1)}, u32[]{:S(2)}, u32[]{:S(2)}) %collective-permute-start.15) | collective-permute-done | bytes 1048608 | tf_op jit(solution)/shard_map/ppermute | solution.py:50
  121.3 8.3 %linear.1 = (f32[512,1024]{1,0:T(8,128)S(1)}, f32[512,1024]{1,0:T(8,128)S(1)}, f32[8,2048]{1,0:T(8,128)S(1)}) custom-call(s32[3]{0:T(128)S(1)} %pad_add_fusion.me.refs_0_, bf16[512,2048]{1,0:T(8,128)(2,1)S(1)} %get-tuple-element.130.hidden, f32[3,2048]{1,0:T(4,128)S(1)} %copy-done.20, f32[512,128]{1,0:T(8,128)S(1)} %broadcast_in_dim.132.mask_ref.refs_2_, ...), custom_call_target="tpu_custom_call" | custom-call | flops 4294967296 | tf_op jit(solution)/shard_map/linear/pallas_call | solution.py:288
  152.2 6.1 %backward.2 = (bf16[512,1024]{1,0:T(8,128)(2,1)}, f32[8,1024]{1,0:T(8,128)}, bf16[512,2048]{1,0:T(8,128)(2,1)}) custom-call(s32[1]{0:T(128)} %bitcast.5.refs_0_, f32[3,2048]{1,0:T(4,128)} %refs_1_.3, f32[512,128]{1,0:T(8,128)} %copy-done.3, bf16[512,2048]{1,0:T(8,128)(2,1)} %refs_3_.3, f32[512,1024]{1,0:T(8,128)} %copy-done.4, f32[8,2048]{1,0:T(8,128)} %copy-done.19, ...), custom_call_target="tpu_custom_call" | custom-call | flops 26214400 | tf_op jit(solution)/shard_map/backward/pallas_call | solution.py:432
  158.3 6.2 %backward.3 = (bf16[512,1024]{1,0:T(8,128)(2,1)}, f32[8,1024]{1,0:T(8,128)}, bf16[512,2048]{1,0:T(8,128)(2,1)}) custom-call(s32[1]{0:T(128)} %bitcast.5.refs_0_, f32[3,2048]{1,0:T(4,128)} %refs_1_.3, f32[512,128]{1,0:T(8,128)} %copy-done.3, bf16[512,2048]{1,0:T(8,128)(2,1)} %refs_3_.3, f32[512,1024]{1,0:T(8,128)} %copy-done.11, ...), custom_call_target="tpu_custom_call", output_to_operand_aliasing={{2}: (9, {})} | custom-call | flops 26214400 | tf_op jit(solution)/shard_map/backward/pallas_call | solution.py:432
  170.1 9.0 %outers.1 = (bf16[512,1024]{1,0:T(8,128)(2,1)}, bf16[512,1024]{1,0:T(8,128)(2,1)}, bf16[512,1024]{1,0:T(8,128)(2,1)}, bf16[512,1024]{1,0:T(8,128)(2,1)}) custom-call(s32[3]{0:T(128)} %copy-done.22, bf16[2,1024,512]{2,1,0:T(8,128)(2,1)} %copy-done.2, bf16[1024,512]{1,0:T(8,128)(2,1)} %copy-done.34, bf16[512,1024]{1,0:T(8,128)(2,1)} %get-tuple-element.140.refs_2_.refs_1_, ...), custom_call_target="tpu_custom_call" | custom-call | tf_op jit(solution)/shard_map/outers/pallas_call | solution.py:503
  182.4 15.3 %hidden_grads.1 = (bf16[512,2048]{1,0:T(8,128)(2,1)}, bf16[128,2048]{1,0:T(8,128)(2,1)}, bf16[128,2048]{1,0:T(8,128)(2,1)}, bf16[128,2048]{1,0:T(8,128)(2,1)}, b...) custom-call(s32[3]{0:T(128)} %copy-done.22, ...), custom_call_target="tpu_custom_call" | custom-call | tf_op jit(solution)/shard_map/hidden_grads/pallas_call | solution.py:595
  197.7 6.8 %collective-permute-done.28.came_a = bf16[512,1024]{1,0:T(8,128)(2,1)S(1)} collective-permute-done((bf16[512,1024]{1,0:T(8,128)(2,1)}, bf16[512,1024]{1,0:T(8,128)(2,1)S(1)}, u32[]{:S(2)}, u32[]{:S(2)}) %collective-permute-start.28) | collective-permute-done | bytes 1048608 | tf_op jit(solution)/shard_map/ppermute | solution.py:50
  215.9 9.4 %collective-permute-done.32.came_b = bf16[256,1024]{1,0:T(8,128)(2,1)S(1)} collective-permute-done((bf16[256,1024]{1,0:T(8,128)(2,1)}, bf16[256,1024]{1,0:T(8,128)(2,1)S(1)}, u32[]{:S(2)}, u32[]{:S(2)}) %collective-permute-start.32) | collective-permute-done | bytes 524320 | tf_op jit(solution)/shard_map/ppermute | solution.py:50
  229.5 8.1 %collective-permute-done.33.refs_3_ = bf16[128,2048]{1,0:T(8,128)(2,1)} collective-permute-done((bf16[128,2048]{1,0:T(8,128)(2,1)}, bf16[128,2048]{1,0:T(8,128)(2,1)}, u32[]{:S(2)}, u32[]{:S(2)}) %collective-permute-start.33) | collective-permute-done | bytes 524320 | tf_op jit(solution)/shard_map/ppermute | solution.py:50
  242.4 13.5 %collective-permute-done.36.refs_4_ = bf16[64,2048]{1,0:T(8,128)(2,1)S(1)} collective-permute-done((bf16[64,2048]{1,0:T(8,128)(2,1)}, bf16[64,2048]{1,0:T(8,128)(2,1)S(1)}, u32[]{:S(2)}, u32[]{:S(2)}) %collective-permute-start.36) | collective-permute-done | bytes 262176 | tf_op jit(solution)/shard_map/ppermute | solution.py:50
  267.1 13.3 %collective-permute-done.40.refs_5_ = bf16[64,2048]{1,0:T(8,128)(2,1)S(1)} collective-permute-done((bf16[64,2048]{1,0:T(8,128)(2,1)}, bf16[64,2048]{1,0:T(8,128)(2,1)S(1)}, u32[]{:S(2)}, u32[]{:S(2)}) %collective-permute-start.40) | collective-permute-done | bytes 262176 | tf_op jit(solution)/shard_map/ppermute | solution.py:50
  280.4 7.6 %collective-permute-done.39.came = bf16[64,2048]{1,0:T(8,128)(2,1)S(1)} collective-permute-done((bf16[64,2048]{1,0:T(8,128)(2,1)}, bf16[64,2048]{1,0:T(8,128)(2,1)S(1)}, u32[]{:S(2)}, u32[]{:S(2)}) %collective-permute-start.39) | collective-permute-done | bytes 262176 | tf_op jit(solution)/shard_map/ppermute | solution.py:50
  298.5 5.4 %collective-permute-done.49 = f32[8,2048]{1,0:T(8,128)S(1)} collective-permute-done((f32[8,2048]{1,0:T(8,128)S(1)}, f32[8,2048]{1,0:T(8,128)S(1)}, u32[]{:S(2)}, u32[]{:S(2)}) %collective-permute-start.49) | collective-permute-done | bytes 65568 | tf_op jit(solution)/shard_map/ppermute | solution.py:50
  308.3 10.7 %collective-permute-done.44 = bf16[64,2048]{1,0:T(8,128)(2,1)S(1)} collective-permute-done((bf16[64,2048]{1,0:T(8,128)(2,1)}, bf16[64,2048]{1,0:T(8,128)(2,1)S(1)}, u32[]{:S(2)}, u32[]{:S(2)}) %collective-permute-start.44) | collective-permute-done | bytes 262176 | tf_op jit(solution)/shard_map/ppermute | solution.py:50
  328.2 8.9 %collective-permute-done.56 = f32[8,2048]{1,0:T(8,128)S(1)} collective-permute-done((f32[8,2048]{1,0:T(8,128)S(1)}, f32[8,2048]{1,0:T(8,128)S(1)}, u32[]{:S(2)}, u32[]{:S(2)}) %collective-permute-start.56) | collective-permute-done | bytes 65568 | tf_op jit(solution)/shard_map/ppermute | solution.py:50
  338.2 7.2 %collective-permute-done.52.refs_8_ = bf16[64,2048]{1,0:T(8,128)(2,1)S(1)} collective-permute-done((bf16[64,2048]{1,0:T(8,128)(2,1)}, bf16[64,2048]{1,0:T(8,128)(2,1)S(1)}, u32[]{:S(2)}, u32[]{:S(2)}) %collective-permute-start.52) | collective-permute-done | bytes 262176 | tf_op jit(solution)/shard_map/ppermute | solution.py:50
  352.5 8.1 %collective-permute-done.57.refs_3_ = bf16[512,512]{1,0:T(8,128)(2,1)} collective-permute-done((bf16[512,512]{1,0:T(8,128)(2,1)S(1)}, bf16[512,512]{1,0:T(8,128)(2,1)}, u32[]{:S(2)}, u32[]{:S(2)}) %collective-permute-start.57) | collective-permute-done | bytes 524320 | tf_op jit(solution)/shard_map/ppermute | solution.py:50
  360.7 12.8 %near_back.1.base = f32[512,2048]{1,0:T(8,128)} custom-call(bf16[512,512]{1,0:T(8,128)(2,1)} %get-tuple-element.219.refs_0_, bf16[512,512]{1,0:T(8,128)(2,1)} %copy-done.60, bf16[512,512]{1,0:T(8,128)(2,1)} %collective-permute-done.30.refs_2_, bf16[512,512]{1,0:T(8,128)(2,1)} %collective-permute-done.57.refs_3_, ...), custom_call_target="tpu_custom_call" | custom-call | flops 4294967296 | tf_op jit(solution)/shard_map/near_back/pallas_call | solution.py:638
  373.5 9.5 %fusion.4 = (bf16[512,2048]{1,0:T(8,128)(2,1)}, f32[512,2048]{1,0:T(8,128)}, f32[512,2048]{1,0:T(8,128)}, f32[512,2048]{1,0:T(8,128)}) fusion(f32[512,2048]{1,0:T(8,128)S(1)} %copy-done.29, f32[]{:T(128)} %bitcast.13, bf16[256,2048]{1,0:T(8,128)(2,1)S(1)} %collective-permute-done.59, bf16[256,2048]{1,0:T(8,128)(2,1)S(1)} %bitcast_select_fusion.1, ...), kind=kLoop, calls=%fused_computation.30 | loop fusion | flops 17825792 | bytes 29360644 | tf_op jit(solution)/shard_map/convert_element_type | solution.py:993
  383.9 7.1 %give_back.1 = bf16[512,2048]{1,0:T(8,128)(2,1)} custom-call(bf16[512,896]{1,0:T(8,128)(2,1)} %copy-done.18, f32[512,2048]{1,0:T(8,128)} %near_back.1.base, bf16[128,2048]{1,0:T(8,128)(2,1)} %copy-done.43, bf16[128,2048]{1,0:T(8,128)(2,1)} %collective-permute-done.60.refs_1_, bf16[128,2048]{1,0:T(8,128)(2,1)} %copy-done.44, ...), custom_call_target="tpu_custom_call" | custom-call | flops 1879048192 | tf_op jit(solution)/shard_map/give_back/pallas_call | solution.py:661
  (287 shorter events, 137.4 us)
Async XLA Ops:
  0.6 32.6 %collective-permute-start = (bf16[512,2048]{1,0:T(8,128)(2,1)}, bf16[512,2048]{1,0:T(8,128)(2,1)S(1)}, u32[]{:S(2)}, u32[]{:S(2)}) collective-permute-start(bf16[512,2048]{1,0:T(8,128)(2,1)} %refs_0_.1), channel_id=1, source_target_pairs={{0,1},{1,0},{2,3},{3,2},{4,5},{5,4},{6,7},{7,6},{8,9},{9,8},{10,11... | collective-permute-start | bytes 6291464 | tf_op jit(solution)/shard_map/ppermute | solution.py:50
  4.4 28.8 %collective-permute-start.1 = (bf16[256,2048]{1,0:T(8,128)(2,1)S(1)}, bf16[256,2048]{1,0:T(8,128)(2,1)S(1)}, u32[]{:S(2)}, u32[]{:S(2)}) collective-permute-start(bf16[256,2048]{1,0:T(8,128)(2,1)S(1)} %get-tuple-element.108), channel_id=1, source_target_pairs={{0,2},{1,3},{2,0},{3,1},{4,6},{5,7},{6,4},{7,5},{8,10},{9,11},{10,... | collective-permute-start | bytes 3145736 | tf_op jit(solution)/shard_map/ppermute | solution.py:50
  7.0 26.2 %collective-permute-start.2 = (bf16[128,2048]{1,0:T(8,128)(2,1)S(1)}, bf16[128,2048]{1,0:T(8,128)(2,1)S(1)}, u32[]{:S(2)}, u32[]{:S(2)}) collective-permute-start(bf16[128,2048]{1,0:T(8,128)(2,1)S(1)} %get-tuple-element.110), channel_id=1, source_target_pairs={{0,16},{1,17},{2,18},{3,19},{4,20},{5,21},{6,22},{7,23},{8,24},{9,... | collective-permute-start | bytes 1572872 | tf_op jit(solution)/shard_map/ppermute | solution.py:50
  34.5 27.7 %collective-permute-start.5 = (bf16[256,2048]{1,0:T(8,128)(2,1)S(1)}, bf16[256,2048]{1,0:T(8,128)(2,1)S(1)}, u32[]{:S(2)}, u32[]{:S(2)}) collective-permute-start(bf16[256,2048]{1,0:T(8,128)(2,1)S(1)} %collective-permute-done.1.refs_2_), channel_id=1, source_target_pairs={{0,1},{1,0},{2,3},{3,2},{4,5},{5,4},{6,7},{7,6},{8,9},{9,8},{10,11... | collective-permute-start | bytes 3145736 | tf_op jit(solution)/shard_map/ppermute | solution.py:50
  34.5 27.7 %collective-permute-start.4 = (bf16[256,2048]{1,0:T(8,128)(2,1)S(1)}, bf16[256,2048]{1,0:T(8,128)(2,1)S(1)}, u32[]{:S(2)}, u32[]{:S(2)}) collective-permute-start(bf16[256,2048]{1,0:T(8,128)(2,1)S(1)} %get-tuple-element.112), channel_id=1, source_target_pairs={{0,2},{1,3},{2,0},{3,1},{4,6},{5,7},{6,4},{7,5},{8,10},{9,11},{10,... | collective-permute-start | bytes 3145736 | tf_op jit(solution)/shard_map/ppermute | solution.py:50
  36.7 25.6 %collective-permute-start.6 = (bf16[128,2048]{1,0:T(8,128)(2,1)S(1)}, bf16[128,2048]{1,0:T(8,128)(2,1)S(1)}, u32[]{:S(2)}, u32[]{:S(2)}) collective-permute-start(bf16[128,2048]{1,0:T(8,128)(2,1)S(1)} %get-tuple-element.115), channel_id=1, source_target_pairs={{0,24},{1,25},{2,26},{3,27},{4,28},{5,29},{6,30},{7,31},{8,16},{9,... | collective-permute-start | bytes 1572872 | tf_op jit(solution)/shard_map/ppermute | solution.py:50
  62.2 29.6 %collective-permute-start.12 = (bf16[512,2048]{1,0:T(8,128)(2,1)S(1)}, bf16[512,2048]{1,0:T(8,128)(2,1)S(1)}, u32[]{:S(2)}, u32[]{:S(2)}) collective-permute-start(bf16[512,2048]{1,0:T(8,128)(2,1)S(1)} %convert_element_type.29.refs_0_.refs_3_), channel_id=1, source_target_pairs={{0,1},{1,0},{2,3},{3,2},{4,5},{5,4},{6,7},{7,6},{8,9},{9,8},{10,11... | collective-permute-start | bytes 6291464 | tf_op jit(solution)/shard_map/ppermute | solution.py:50
  62.4 29.4 %collective-permute-start.11 = (bf16[256,2048]{1,0:T(8,128)(2,1)S(1)}, bf16[256,2048]{1,0:T(8,128)(2,1)S(1)}, u32[]{:S(2)}, u32[]{:S(2)}) collective-permute-start(bf16[256,2048]{1,0:T(8,128)(2,1)S(1)} %get-tuple-element.125), channel_id=1, source_target_pairs={{0,2},{1,3},{2,0},{3,1},{4,6},{5,7},{6,4},{7,5},{8,10},{9,11},{10,... | collective-permute-start | bytes 3145736 | tf_op jit(solution)/shard_map/ppermute | solution.py:50
  64.0 27.9 %collective-permute-start.8 = (bf16[256,2048]{1,0:T(8,128)(2,1)S(1)}, bf16[256,2048]{1,0:T(8,128)(2,1)S(1)}, u32[]{:S(2)}, u32[]{:S(2)}) collective-permute-start(bf16[256,2048]{1,0:T(8,128)(2,1)S(1)} %collective-permute-done.4.refs_3_), channel_id=1, source_target_pairs={{0,1},{1,0},{2,3},{3,2},{4,5},{5,4},{6,7},{7,6},{8,9},{9,8},{10,11... | collective-permute-start | bytes 3145736 | tf_op jit(solution)/shard_map/ppermute | solution.py:50
  64.2 27.3 %collective-permute-start.10 = (bf16[128,2048]{1,0:T(8,128)(2,1)S(1)}, bf16[128,2048]{1,0:T(8,128)(2,1)S(1)}, u32[]{:S(2)}, u32[]{:S(2)}) collective-permute-start(bf16[128,2048]{1,0:T(8,128)(2,1)S(1)} %get-tuple-element.123), channel_id=1, source_target_pairs={{0,20},{1,21},{2,22},{3,23},{4,16},{5,17},{6,18},{7,19},{8,28},{9,... | collective-permute-start | bytes 1572872 | tf_op jit(solution)/shard_map/ppermute | solution.py:50
  67.1 24.7 %collective-permute-start.9 = (bf16[128,2048]{1,0:T(8,128)(2,1)S(1)}, bf16[128,2048]{1,0:T(8,128)(2,1)S(1)}, u32[]{:S(2)}, u32[]{:S(2)}) collective-permute-start(bf16[128,2048]{1,0:T(8,128)(2,1)S(1)} %get-tuple-element.121), channel_id=1, source_target_pairs={{0,8},{1,9},{2,10},{3,11},{4,12},{5,13},{6,14},{7,15},{8,0},{9,1},... | collective-permute-start | bytes 1572872 | tf_op jit(solution)/shard_map/ppermute | solution.py:50
  120.5 26.9 %collective-permute-start.14 = (bf16[1024,512]{1,0:T(8,128)(2,1)S(1)}, bf16[1024,512]{1,0:T(8,128)(2,1)S(1)}, u32[]{:S(2)}, u32[]{:S(2)}) collective-permute-start(bf16[1024,512]{1,0:T(8,128)(2,1)S(1)} %slice_bitcast_fusion), channel_id=1, source_target_pairs={{0,1},{1,0},{2,3},{3,2},{4,5},{5,4},{6,7},{7,6},{8,9},{9,8},{10,11... | collective-permute-start | bytes 3145736 | tf_op jit(solution)/shard_map/ppermute | solution.py:50
  179.1 25.5 %collective-permute-start.28 = (bf16[512,1024]{1,0:T(8,128)(2,1)}, bf16[512,1024]{1,0:T(8,128)(2,1)S(1)}, u32[]{:S(2)}, u32[]{:S(2)}) collective-permute-start(bf16[512,1024]{1,0:T(8,128)(2,1)} %get-tuple-element.142), channel_id=1, source_target_pairs={{0,2},{1,3},{2,0},{3,1},{4,6},{5,7},{6,4},{7,5},{8,10},{9,11},{10,... | collective-permute-start | bytes 3145736 | tf_op jit(solution)/shard_map/ppermute | solution.py:50
  180.1 25.1 %collective-permute-start.29 = (bf16[512,1024]{1,0:T(8,128)(2,1)}, bf16[512,1024]{1,0:T(8,128)(2,1)S(1)}, u32[]{:S(2)}, u32[]{:S(2)}) collective-permute-start(bf16[512,1024]{1,0:T(8,128)(2,1)} %get-tuple-element.144), channel_id=1, source_target_pairs={{0,4},{1,5},{2,6},{3,7},{4,0},{5,1},{6,2},{7,3},{8,12},{9,13},{10,... | collective-permute-start | bytes 3145736 | tf_op jit(solution)/shard_map/ppermute | solution.py:50
  205.3 32.3 %collective-permute-start.34 = (bf16[512,2048]{1,0:T(8,128)(2,1)}, bf16[512,2048]{1,0:T(8,128)(2,1)}, u32[]{:S(2)}, u32[]{:S(2)}) collective-permute-start(bf16[512,2048]{1,0:T(8,128)(2,1)} %get-tuple-element.160.refs_4_), channel_id=1, source_target_pairs={{0,1},{1,0},{2,3},{3,2},{4,5},{5,4},{6,7},{7,6},{8,9},{9,8},{10,11... | collective-permute-start | bytes 6291464 | tf_op jit(solution)/shard_map/ppermute | solution.py:50
  212.3 25.3 %collective-permute-start.33 = (bf16[128,2048]{1,0:T(8,128)(2,1)}, bf16[128,2048]{1,0:T(8,128)(2,1)}, u32[]{:S(2)}, u32[]{:S(2)}) collective-permute-start(bf16[128,2048]{1,0:T(8,128)(2,1)} %get-tuple-element.159), channel_id=1, source_target_pairs={{0,16},{1,17},{2,18},{3,19},{4,20},{5,21},{6,22},{7,23},{8,24},{9,... | collective-permute-start | bytes 1572872 | tf_op jit(solution)/shard_map/ppermute | solution.py:50
  258.0 30.0 %collective-permute-start.43 = (bf16[128,2048]{1,0:T(8,128)(2,1)S(1)}, bf16[128,2048]{1,0:T(8,128)(2,1)S(1)}, u32[]{:S(2)}, u32[]{:S(2)}) collective-permute-start(bf16[128,2048]{1,0:T(8,128)(2,1)S(1)} %collective-permute-done.38.refs_6_), channel_id=1, source_target_pairs={{0,1},{1,0},{2,3},{3,2},{4,5},{5,4},{6,7},{7,6},{8,9},{9,8},{10,11... | collective-permute-start | bytes 1572872 | tf_op jit(solution)/shard_map/ppermute | solution.py:50
  258.0 30.0 %collective-permute-start.42 = (bf16[128,2048]{1,0:T(8,128)(2,1)}, bf16[128,2048]{1,0:T(8,128)(2,1)}, u32[]{:S(2)}, u32[]{:S(2)}) collective-permute-start(bf16[128,2048]{1,0:T(8,128)(2,1)} %get-tuple-element.177), channel_id=1, source_target_pairs={{0,2},{1,3},{2,0},{3,1},{4,6},{5,7},{6,4},{7,5},{8,10},{9,11},{10,... | collective-permute-start | bytes 1572872 | tf_op jit(solution)/shard_map/ppermute | solution.py:50
  259.1 28.9 %collective-permute-start.41 = (bf16[128,2048]{1,0:T(8,128)(2,1)}, bf16[128,2048]{1,0:T(8,128)(2,1)S(1)}, u32[]{:S(2)}, u32[]{:S(2)}) collective-permute-start(bf16[128,2048]{1,0:T(8,128)(2,1)} %get-tuple-element.176), channel_id=1, source_target_pairs={{0,12},{1,13},{2,14},{3,15},{4,8},{5,9},{6,10},{7,11},{8,4},{9,5},... | collective-permute-start | bytes 1572872 | tf_op jit(solution)/shard_map/ppermute | solution.py:50
  288.1 30.9 %collective-permute-start.47 = (bf16[128,2048]{1,0:T(8,128)(2,1)}, bf16[128,2048]{1,0:T(8,128)(2,1)S(1)}, u32[]{:S(2)}, u32[]{:S(2)}) collective-permute-start(bf16[128,2048]{1,0:T(8,128)(2,1)} %collective-permute-done.42.refs_7_), channel_id=1, source_target_pairs={{0,1},{1,0},{2,3},{3,2},{4,5},{5,4},{6,7},{7,6},{8,9},{9,8},{10,11... | collective-permute-start | bytes 1572872 | tf_op jit(solution)/shard_map/ppermute | solution.py:50
  288.1 30.9 %collective-permute-start.46 = (bf16[128,2048]{1,0:T(8,128)(2,1)S(1)}, bf16[128,2048]{1,0:T(8,128)(2,1)S(1)}, u32[]{:S(2)}, u32[]{:S(2)}) collective-permute-start(bf16[128,2048]{1,0:T(8,128)(2,1)S(1)} %copy-done.42), channel_id=1, source_target_pairs={{0,2},{1,3},{2,0},{3,1},{4,6},{5,7},{6,4},{7,5},{8,10},{9,11},{10,... | collective-permute-start | bytes 1572872 | tf_op jit(solution)/shard_map/ppermute | solution.py:50
  345.5 28.0 %collective-permute-start.59 = (bf16[256,2048]{1,0:T(8,128)(2,1)S(1)}, bf16[256,2048]{1,0:T(8,128)(2,1)S(1)}, u32[]{:S(2)}, u32[]{:S(2)}) collective-permute-start(bf16[256,2048]{1,0:T(8,128)(2,1)S(1)} %bitcast_select_fusion.1), channel_id=1, source_target_pairs={{0,4},{1,5},{2,6},{3,7},{4,0},{5,1},{6,2},{7,3},{8,12},{9,13},{10,... | collective-permute-start | bytes 3145736 | tf_op jit(solution)/shard_map/ppermute | solution.py:50
  347.9 35.2 %collective-permute-start.61 = (bf16[128,2048]{1,0:T(8,128)(2,1)}, bf16[128,2048]{1,0:T(8,128)(2,1)S(1)}, u32[]{:S(2)}, u32[]{:S(2)}) collective-permute-start(bf16[128,2048]{1,0:T(8,128)(2,1)} %get-tuple-element.203), channel_id=1, source_target_pairs={{0,24},{1,25},{2,26},{3,27},{4,28},{5,29},{6,30},{7,31},{8,16},{9,... | collective-permute-start | bytes 1572872 | tf_op jit(solution)/shard_map/ppermute | solution.py:50
  349.9 33.1 %collective-permute-start.60 = (bf16[128,2048]{1,0:T(8,128)(2,1)}, bf16[128,2048]{1,0:T(8,128)(2,1)}, u32[]{:S(2)}, u32[]{:S(2)}) collective-permute-start(bf16[128,2048]{1,0:T(8,128)(2,1)} %get-tuple-element.201), channel_id=1, source_target_pairs={{0,8},{1,9},{2,10},{3,11},{4,12},{5,13},{6,14},{7,15},{8,0},{9,1},... | collective-permute-start | bytes 1572872 | tf_op jit(solution)/shard_map/ppermute | solution.py:50
  (105 other events, 2029.5 us)

commit v3 on v2

--- a/solution.py
+++ b/solution.py
@@ -616,59 +616,76 @@
     return grad_hidden, slots
 
 
-def near_back_kernel(*refs, row_count):
-    flips, grads, out = refs[:row_count], refs[row_count:-1], refs[-1]
-    rows = flips[0].shape[0]
-    for c in range(out.shape[1] // COLS):
-        cs = slice(c * COLS, (c + 1) * COLS)
-        total, done = 0.0, 0
-        for grad in grads:
-            depth = grad.shape[0]
-            total += dot(flips[done // rows][:, done % rows : done % rows + depth], grad[:, cs])
-            done += depth
-        out[:, cs] = total
-
-
-def near_back(flips, grads):
+def pieces_of(chooser, numbers, side):
+    return [chooser[:, (k - 1) * side : k * side] for k in numbers]
+
+
+def near_back(flips, grads, chooser, returned):
     rows, width = grads[0].shape
+    numbers, blocks = sorted(returned), [returned[k] for k in sorted(returned)]
+    side = blocks[0].shape[0]
 
     def kernel(*refs):
-        near_back_kernel(*refs, row_count=len(flips))
-
+        flips_in, refs = refs[: len(flips)], refs[len(flips) :]
+        grads_in, refs = refs[: len(grads)], refs[len(grads) :]
+        chooser_ref, blocks_in, out = refs[0], refs[1:-1], refs[-1]
+        picked = jnp.concatenate(pieces_of(chooser_ref, numbers, side), axis=1)
+        for c in range(width // COLS):
+            cs = slice(c * COLS, (c + 1) * COLS)
+            total = dot(picked, jnp.concatenate([block[:, cs] for block in blocks_in], axis=0))
+            done = 0
+            for grad in grads_in:
+                depth = grad.shape[0]
+                flip = flips_in[done // rows]
+                total += dot(flip[:, done % rows : done % rows + depth], grad[:, cs])
+                done += depth
+            out[:, cs] = total
+
+    blocked = chooser.shape[1] > WHOLE_HALO
+    if blocked:
+        grid, block, whole = columns(width, True)
+        specs = [whole((rows, rows))] * len(flips) + [block(g.shape[0]) for g in grads]
+        specs += [whole(chooser.shape)] + [block(side)] * len(blocks)
+        width = COLS
+    else:
+        grid, specs = {}, [VMEM] * (len(flips) + len(grads) + 1 + len(blocks))
     return call(
         kernel,
-        flops=2 * rows * rows * len(flips) * width,
+        flops=0,
         vmem_mb=56,
-        in_specs=[VMEM] * (len(flips) + len(grads)),
-        out_specs=VMEM,
-        out_shape=SDS((rows, width), jnp.float32),
+        in_specs=specs,
+        out_specs=block(rows) if blocked else VMEM,
+        out_shape=SDS((rows, grads[0].shape[1]), jnp.float32),
         name="near_back",
-    )(*flips, *grads)
-
-
-def return_kernel(chooser, base, *refs):
-    returned, out = refs[:-1], refs[-1]
-    for c in range(out.shape[1] // COLS):
-        cs = slice(c * COLS, (c + 1) * COLS)
-        pieces = jnp.concatenate([ref[:, cs] for ref in returned], axis=0)
-        out[:, cs] = (base[:, cs] + dot(chooser[...], pieces)).astype(jnp.bfloat16)
+        **grid,
+    )(*flips, *grads, chooser, *blocks)
 
 
 def give_back(chooser, base, returned):
     rows, width = base.shape
+    numbers, blocks = sorted(returned), [returned[k] for k in sorted(returned)]
+    side = blocks[0].shape[0]
     blocked = chooser.shape[1] > WHOLE_HALO
     grid, block, whole = columns(width, blocked)
-    return call(
-        return_kernel,
-        flops=2 * rows * chooser.shape[1] * width,
+
+    def kernel(chooser_ref, base_ref, *refs):
+        blocks_in, out = refs[:-1], refs[-1]
+        picked = jnp.concatenate(pieces_of(chooser_ref, numbers, side), axis=1)
+        for c in range(out.shape[1] // COLS):
+            cs = slice(c * COLS, (c + 1) * COLS)
+            pieces = jnp.concatenate([block[:, cs] for block in blocks_in], axis=0)
+            out[:, cs] = (base_ref[:, cs] + dot(picked, pieces)).astype(jnp.bfloat16)
+
+    return call(
+        kernel,
+        flops=0,
         vmem_mb=56,
-        in_specs=[whole(chooser.shape), block(rows)]
-        + [block(r.shape[0]) for r in returned],
+        in_specs=[whole(chooser.shape), block(rows)] + [block(side)] * len(blocks),
         out_specs=block(rows),
         out_shape=SDS((rows, width), jnp.bfloat16),
         name="give_back",
         **grid,
-    )(chooser, base, *returned)
+    )(chooser, base, *blocks)
 
 
 def lamb_step(value, grad, first, second, decay):
@@ -683,112 +700,106 @@
     return (first_new, second_new, update)
 
 
-def first_sums_kernel(me, keep_a, came_a, keep_b, came_b, kept_a, sent_a, kept_b, sent_b):
-    half = kept_a.shape[0]
-    for flag, out in ((me[2], kept_a), (1 - me[2], sent_a)):
-        rows = pl.ds(pl.multiple_of(flag * half, half), half)
-        out[...] = (keep_a[rows, :].astype(jnp.float32) + came_a[rows, :].astype(jnp.float32)).astype(out.dtype)
-    for n, out in enumerate((kept_b, sent_b)):
-        rows = slice(n * half, (n + 1) * half)
-        out[...] = (keep_b[rows, :].astype(jnp.float32) + came_b[rows, :].astype(jnp.float32)).astype(out.dtype)
-
-
-def first_sums(me, keep_a, came_a, keep_b, came_b):
+def term_sum(terms):
+    return sum(term[...].astype(jnp.float32) for term in terms)
+
+
+def first_sends(side_bit, keep_a, came_a, keep_b, came_b):
     rows, span = keep_a.shape
-    kept, sent = SDS((rows // 2, span), jnp.float32), SDS((rows // 2, span), jnp.bfloat16)
-    return call(
-        first_sums_kernel,
+    half = rows // 2
+    block = lambda place: pl.BlockSpec((half, span), place)
+    other, second = block(lambda i, bit: (1 - bit[0], 0)), block(lambda i, bit: (1, 0))
+
+    def kernel(bit, *refs):
+        for n, out in enumerate(refs[4:]):
+            out[...] = term_sum(refs[2 * n : 2 * n + 2]).astype(out.dtype)
+
+    return call(
+        kernel,
         flops=0,
         vmem_mb=56,
-        in_specs=[SMEM] + [VMEM] * 4,
-        out_specs=[VMEM] * 4,
-        out_shape=[kept, sent, kept, sent],
-        name="first_sums",
-    )(me, keep_a, came_a, keep_b, came_b)
-
-
-def joined_kernel(flag, kept_a, came_a, kept_b, came_b, kept, sent):
-    half, span = kept.shape[0], kept_a.shape[1]
-    for n, (keep, came) in enumerate(((kept_a, came_a), (kept_b, came_b))):
-        cs = slice(n * span, (n + 1) * span)
-        for bit, out in ((flag[0], kept), (1 - flag[0], sent)):
-            rows = pl.ds(pl.multiple_of(bit * half, half), half)
-            out[:, cs] = (keep[rows, :] + came[rows, :].astype(jnp.float32)).astype(out.dtype)
-
-
-def joined(flag, kept_a, came_a, kept_b, came_b):
-    rows, span = kept_a.shape
-    return call(
-        joined_kernel,
+        grid_spec=pltpu.PrefetchScalarGridSpec(
+            num_scalar_prefetch=1,
+            grid=(1,),
+            in_specs=[other] * 2 + [second] * 2,
+            out_specs=[block(lambda i, bit: (0, 0))] * 2,
+        ),
+        out_shape=[SDS((half, span), jnp.bfloat16)] * 2,
+        name="first_sends",
+    )(side_bit[None], keep_a, came_a, keep_b, came_b)
+
+
+def rows_sum(start, rows, terms_a, terms_b, terms, extra=()):
+    span = terms_a[0][0].shape[1]
+    narrow = [*terms_a, *terms_b]
+    places = jnp.stack([(start - offset) // rows for _, offset in [*narrow, *terms]]).astype(jnp.int32)
+    at = lambda n, cols: pl.BlockSpec((rows, cols), lambda i, places: (places[n], 0))
+    specs = [at(n, span) for n in range(len(narrow))]
+    specs += [at(len(narrow) + n, 2 * span) for n in range(len(terms))]
+    return places, specs, [term for term, _ in [*narrow, *terms]], len(terms_a), len(narrow)
+
+
+def send_rows(start, rows, terms_a, terms_b, terms):
+    places, specs, arrays, cut, narrow = rows_sum(start, rows, terms_a, terms_b, terms)
+    span = arrays[0].shape[1]
+
+    def kernel(places, *refs):
+        out = refs[-1]
+        wide = term_sum(refs[narrow:-1])
+        for n, part in enumerate((refs[:cut], refs[cut:narrow])):
+            cs = slice(n * span, (n + 1) * span)
+            more = wide if isinstance(wide, int) else wide[:, cs]
+            out[:, cs] = (term_sum(part) + more).astype(out.dtype)
+
+    return call(
+        kernel,
         flops=0,
         vmem_mb=56,
-        in_specs=[SMEM] + [VMEM] * 4,
-        out_specs=[VMEM] * 2,
-        out_shape=[
-            SDS((rows // 2, 2 * span), jnp.float32),
-            SDS((rows // 2, 2 * span), jnp.bfloat16),
-        ],
-        name="joined",
-    )(flag[None], kept_a, came_a, kept_b, came_b)
-
-
-def halved_kernel(flag, keep, came, kept, sent):
-    half = kept.shape[0]
-    for bit, out in ((flag[0], kept), (1 - flag[0], sent)):
-        rows = pl.ds(pl.multiple_of(bit * half, half), half)
-        out[...] = (keep[rows, :] + came[rows, :].astype(jnp.float32)).astype(out.dtype)
-
-
-def halved_sums(flag, keep, came):
-    rows, width = keep.shape
-    return call(
-        halved_kernel,
+        grid_spec=pltpu.PrefetchScalarGridSpec(
+            num_scalar_prefetch=1,
+            grid=(1,),
+            in_specs=specs,
+            out_specs=pl.BlockSpec((rows, 2 * span), lambda i, places: (0, 0)),
+        ),
+        out_shape=SDS((rows, 2 * span), jnp.bfloat16),
+        name="send_rows",
+    )(places, *arrays)
+
+
+def piece_totals(start, rows, terms_a, terms_b, terms, sums, weight, first, second):
+    places, specs, arrays, cut, narrow = rows_sum(start, rows, terms_a, terms_b, terms)
+    span = arrays[0].shape[1]
+    own = pl.BlockSpec((rows, 2 * span), lambda i, places: (places[0], 0))
+    whole = lambda height: pl.BlockSpec((height, 2 * span), lambda i, places: (0, 0))
+
+    def kernel(places, *refs):
+        sums, value, first, second, piece, totals = refs[-6:]
+        wide = term_sum(refs[narrow:-6])
+        totals[0:1, :] = sums[0:1, :]
+        totals[3:8, :] = jnp.zeros((5, 2 * span), jnp.float32)
+        for n, part in enumerate((refs[:cut], refs[cut:narrow])):
+            cs = slice(n * span, (n + 1) * span)
+            low = (term_sum(part) + wide[:, cs]).astype(jnp.bfloat16)
+            piece[:, cs] = low
+            update = lamb_step(
+                value[:, cs], low.astype(jnp.float32), first[:, cs], second[:, cs], WEIGHT_DECAY
+            )[2]
+            totals[1:2, cs] = jnp.sum(value[:, cs] * value[:, cs], axis=0, keepdims=True)
+            totals[2:3, cs] = jnp.sum(update * update, axis=0, keepdims=True)
+
+    return call(
+        kernel,
         flops=0,
         vmem_mb=56,
-        in_specs=[SMEM] + [VMEM] * 2,
-        out_specs=[VMEM] * 2,
-        out_shape=[SDS((rows // 2, width), jnp.float32), SDS((rows // 2, width), jnp.bfloat16)],
-        name="halved_sums",
-    )(flag[None], keep, came)
-
-
-def piece_kernel(start, kept, came, sums, value_in, first_in, second_in, piece, totals, value, first, second, sems):
-    rows = piece.shape[0]
-    here = pl.ds(pl.multiple_of(start[0], rows), rows)
-    copies = [
-        pltpu.make_async_copy(source.at[here, :], target, sems.at[n])
-        for n, (source, target) in enumerate(
-            zip((value_in, first_in, second_in), (value, first, second))
-        )
-    ]
-    for copy in copies:
-        copy.start()
-    low = (kept[...] + came[...].astype(jnp.float32)).astype(jnp.bfloat16)
-    piece[...] = low
-    for copy in copies:
-        copy.wait()
-    update = lamb_step(
-        value[...], low.astype(jnp.float32), first[...], second[...], WEIGHT_DECAY
-    )[2]
-    totals[0:1, :] = sums[0:1, :]
-    totals[1:2, :] = jnp.sum(value[...] * value[...], axis=0, keepdims=True)
-    totals[2:3, :] = jnp.sum(update * update, axis=0, keepdims=True)
-    totals[3:8, :] = jnp.zeros((5, totals.shape[1]), jnp.float32)
-
-
-def piece_totals(start, kept, came, sums, weight, first, second):
-    rows, width = kept.shape
-    return call(
-        piece_kernel,
-        flops=0,
-        vmem_mb=56,
-        in_specs=[SMEM, VMEM, VMEM, VMEM, ANY, ANY, ANY],
-        out_specs=[VMEM, VMEM],
-        out_shape=[SDS((rows, width), jnp.bfloat16), SDS((STAT_ROWS, width), jnp.float32)],
-        scratch_shapes=[pltpu.VMEM((rows, width), jnp.float32)] * 3
-        + [pltpu.SemaphoreType.DMA((3,))],
+        grid_spec=pltpu.PrefetchScalarGridSpec(
+            num_scalar_prefetch=1,
+            grid=(1,),
+            in_specs=specs + [whole(STAT_ROWS)] + [own] * 3,
+            out_specs=[whole(rows), whole(STAT_ROWS)],
+        ),
+        out_shape=[SDS((rows, 2 * span), jnp.bfloat16), SDS((STAT_ROWS, 2 * span), jnp.float32)],
         name="piece_totals",
-    )(start[None], kept, came, sums, weight, first, second)
+    )(places, *arrays, sums, weight, first, second)
 
 
 def by_bit(flag, own, came):
@@ -887,7 +898,7 @@
         near_pre.append(swap(grad_pre, 0, 1))
         sums.append(sum_part)
     sums = jnp.concatenate(sums, axis=1)
-    halved = far[2] + far[3]
+    halved = []
     keep_a, send_a, keep_b, send_b = outers(me, hidden_flip, near_flip, grads, near_pre)
     grad_hidden, slots = hidden_grads(me, grads, weights, halo_flip, side, halved)
 
@@ -899,15 +910,12 @@
     turn_flip = lambda j, *turn: swap(hold(flip[j * rows : (j + 1) * rows], *turn), 0, j)
     rounds = groups(dom_count, row_count)
 
-    start, span = 0, rows
-    for step in [1 << n for n in range(dom_count.bit_length() - 1)]:
-        span //= 2
-        start = start + bit(step) * span
     small_steps = sum(rounds, [])
 
     flips = [flip[:rows], turn_flip(1, send_a), None, None]
     turn = [swap(send_a, 0, 2), swap(send_b, 1, 0), flips[1], grad_hidden]
-    kept_a, sent_a, kept_b, sent_b = first_sums(me, keep_a, turn[0], keep_b, turn[1])
+    sent_a, sent_b = first_sends(side_bit, keep_a, turn[0], keep_b, turn[1])
+    terms_a, terms_b, terms = [(keep_a, 0), (turn[0], 0)], [(keep_b, side_bit * half), (turn[1], side_bit * half)], []
     near_grad = swap(hold(grad_hidden, *turn), 0, 1)
     flips[2] = turn_flip(2, *turn)
     turn = [
@@ -917,7 +925,9 @@
         near_grad,
         flips[2],
     ]
-    kept, sent = joined(bit(2), kept_a, turn[0], kept_b, turn[1])
+    first, span = side_bit * half, half
+    terms_a.append((turn[0], first))
+    terms_b.append((turn[1], first))
     steps = [1 << n for n in range(1, dom_count.bit_length() - 1)]
     quarter = rows // 4
     grad_parts, cross = [], []
@@ -927,26 +937,33 @@
         grad_parts.append(
             swap(hold(grad_hidden[n * quarter : (n + 1) * quarter], *turn), 0, 2)
         )
-        if n:
-            cross.append(swap(hold(grad_parts[n - 1], *turn), 0, 1))
-        return [grad_parts[n]] + cross[n - 1 : n]
+        more = [grad_parts[n]]
+        if n > 1:
+            cross.append(swap(hold(grad_parts[n - 2], *turn), 0, 1))
+            more.append(cross[n - 2])
+        if n == 1:
+            flips[3] = turn_flip(3, *turn)
+            more.append(flips[3])
+        return more
 
     beside = [
-        [part_of(far[2], 0), whole(light[0])],
-        [part_of(far[2], 1), whole(light[1])],
-        [part_of(far[3], 0)],
-        [part_of(far[3], 1)],
+        [whole(far[2]), whole(light[0])],
+        [whole(light[1])],
+        [],
+        [whole(far[3])],
     ]
     for n, step in enumerate(steps):
+        span //= 2
+        sent = send_rows(first + (1 - bit(step)) * span, span, terms_a, terms_b, terms)
+        first = first + bit(step) * span
         came = swap(hold(sent, *turn), step, 0)
+        terms.append((came, first))
         more = []
         if n < 2:
             more = [blocks_back(order, *turn) for order in beside[n]] + over_y_back(*turn)
         turn = [came] + more
-        if step < dom_count // 2:
-            kept, sent = halved_sums(bit(2 * step), kept, came)
     weight_grad, totals = piece_totals(
-        start, kept, came, sums, weight, weight_first, weight_second
+        first, span, terms_a, terms_b, terms, sums, weight, weight_first, weight_second
     )
     for n, step in enumerate(reversed(steps)):
         came = swap(hold(weight_grad, *turn), step, 0)
@@ -961,13 +978,18 @@
     came = swap(hold(weight_grad, *turn), 1, 0)
     blocks_back(whole(far[1]), *turn)
     blocks_back(whole(light[2]), *turn)
-    cross.append(swap(hold(grad_parts[-1], *turn), 0, 1))
-    flips[3] = turn_flip(3, *turn)
+    cross += [swap(hold(part, *turn), 0, 1) for part in grad_parts[-2:]]
     bias_grad = totals[0:1]
     weight_norms = jnp.sqrt(jnp.sum(totals[1:3], axis=1))
-    base = near_back(flips, [grad_hidden, near_grad] + grad_parts + cross)
+    late = far[1] + light[2]
+    base = near_back(
+        flips,
+        [grad_hidden, near_grad] + grad_parts + cross,
+        chooser,
+        {key[0]: value for key, value in returned.items() if key[0] not in late},
+    )
     weight_grad = by_bit(bit(1), weight_grad, hold(came, base)).astype(jnp.float32)
-    returned = [returned[key] for key in sorted(returned)]
+    returned = {key[0]: value for key, value in returned.items() if key[0] in late}
     weight_first_new, weight_second_new, weight_update = lamb_step(
         weight, weight_grad, weight_first, weight_second, WEIGHT_DECAY
     )

time: 395 us -> 384 us (0.972)
  waiting for transfers between devices: 194 us -> 181 us
    ppermute x62 -> x60, waiting for transfers between devices: 194 us -> 181 us  [swap(): return lax.ppermute(value, AXES, pairs)]
    ppermute x62 -> x60, starting transfers between devices: 66.3 us -> 67.1 us  [swap(): return lax.ppermute(value, AXES, pairs)]
    unnamed x135 -> x127, local copies, waits for them, and re-layouts: 15.8 us -> 15.2 us
  transfers between devices with their start and end apart: 62 -> 60, of which waited for: 28 -> 30; matrix products, arithmetic and copies ran while one was open for 5% -> 6% of each run, Pallas kernels for 16% -> 17%
where the time goes in v3:
time: 384 us; the launch traced here: 381 us
  waiting for transfers between devices  181 us (47%)
  Pallas kernels  89 us (23%)
  starting transfers between devices  67.1 us (17%)
  local copies, waits for them, and re-layouts  21.7 us (6%)
  other arithmetic  17.6 us (5%)
    ppermute x60, waiting for transfers between devices, swap(): return lax.ppermute(value, AXES, pairs)  181 us
    ppermute x60, starting transfers between devices, swap(): return lax.ppermute(value, AXES, pairs)  67.1 us
    pallas_call x1, Pallas kernels, near_back(): call(kernel, flops=0, vmem_mb=56, in_specs=specs, out_specs=block(rows) i...  15.4 us
    pallas_call x1, Pallas kernels, hidden_grads(): call(kernel, flops=0, vmem_mb=56, in_specs=[SMEM] + [ANY] * len(inputs),...  15.3 us
    unnamed x127, local copies, waits for them, and re-layouts  15.2 us
    pallas_call x2, Pallas kernels, backward(): call(kernel, flops=50 * rows * span, vmem_mb=56, in_specs=[SMEM, VMEM, VM...  12.4 us
    convert_element_type x1, other arithmetic, on_device(): weight_new.astype(jnp.bfloat16)  9.53 us
    pallas_call x1, Pallas kernels, outers(): call(outers_kernel, flops=0, vmem_mb=56, in_specs=[SMEM] + [ANY] * 6, out...  8.94 us
  transfers between devices with their start and end apart: 60, of which 30 were waited for; matrix products, arithmetic and copies ran while one was open for 6% of the time, Pallas kernels for 17%

profile of v3, /device:TPU:0, one launch (start us, length us, event | category | flops | bytes accessed | tf_op | source)
XLA Modules:
  0.0 380.5 jit_solution(1676969063907966543)
XLA Ops:
  11.1 22.1 %collective-permute-done.2.refs_6_ = bf16[128,2048]{1,0:T(8,128)(2,1)S(1)} collective-permute-done((bf16[128,2048]{1,0:T(8,128)(2,1)S(1)}, bf16[128,2048]{1,0:T(8,128)(2,1)S(1)}, u32[]{:S(2)}, u32[]{:S(2)}) %collective-permute-start.2) | collective-permute-done | bytes 524320 | tf_op jit(solution)/shard_map/ppermute | solution.py:50
  41.5 8.4 %collective-permute-done.7.refs_5_ = bf16[128,2048]{1,0:T(8,128)(2,1)S(1)} collective-permute-done((bf16[128,2048]{1,0:T(8,128)(2,1)S(1)}, bf16[128,2048]{1,0:T(8,128)(2,1)S(1)}, u32[]{:S(2)}, u32[]{:S(2)}) %collective-permute-start.7) | collective-permute-done | bytes 524320 | tf_op jit(solution)/shard_map/ppermute | solution.py:50
  49.9 12.3 %collective-permute-done.6.refs_8_ = bf16[128,2048]{1,0:T(8,128)(2,1)S(1)} collective-permute-done((bf16[128,2048]{1,0:T(8,128)(2,1)S(1)}, bf16[128,2048]{1,0:T(8,128)(2,1)S(1)}, u32[]{:S(2)}, u32[]{:S(2)}) %collective-permute-start.6) | collective-permute-done | bytes 524320 | tf_op jit(solution)/shard_map/ppermute | solution.py:50
  68.3 23.2 %collective-permute-done.10.refs_7_ = bf16[128,2048]{1,0:T(8,128)(2,1)S(1)} collective-permute-done((bf16[128,2048]{1,0:T(8,128)(2,1)S(1)}, bf16[128,2048]{1,0:T(8,128)(2,1)S(1)}, u32[]{:S(2)}, u32[]{:S(2)}) %collective-permute-start.10) | collective-permute-done | bytes 524320 | tf_op jit(solution)/shard_map/ppermute | solution.py:50
  100.8 4.5 %near.1.refs_1_ = f32[512,2048]{1,0:T(8,128)S(1)} custom-call(bf16[512,2048]{1,0:T(8,128)(2,1)S(1)} %get-tuple-element.97.wide, bf16[512,2048]{1,0:T(8,128)(2,1)S(1)} %copy-done.9, bf16[512,2048]{1,0:T(8,128)(2,1)S(1)} %copy-done.28, bf16[256,2048]{1,0:T(8,128)(2,1)S(1)} %collective-permute-done.1.refs_2_, ...), custom_call_target="tpu_custom_call" | custom-call | flops 4294967296 | tf_op jit(solution)/shard_map/near/pallas_call | solution.py:195
  105.5 10.5 %collective-permute-done.15.refs_3_.refs_6_ = bf16[256,2048]{1,0:T(8,128)(2,1)S(1)} collective-permute-done((bf16[256,2048]{1,0:T(8,128)(2,1)S(1)}, bf16[256,2048]{1,0:T(8,128)(2,1)S(1)}, u32[]{:S(2)}, u32[]{:S(2)}) %collective-permute-start.15) | collective-permute-done | bytes 1048608 | tf_op jit(solution)/shard_map/ppermute | solution.py:50
  121.4 8.3 %linear.1 = (f32[512,1024]{1,0:T(8,128)S(1)}, f32[512,1024]{1,0:T(8,128)S(1)}, f32[8,2048]{1,0:T(8,128)S(1)}) custom-call(s32[3]{0:T(128)S(1)} %pad_add_fusion.me.refs_0_, bf16[512,2048]{1,0:T(8,128)(2,1)S(1)} %get-tuple-element.120.hidden, f32[3,2048]{1,0:T(4,128)S(1)} %copy-done.20, f32[512,128]{1,0:T(8,128)S(1)} %broadcast_in_dim.124.mask_ref.refs_2_, ...), custom_call_target="tpu_custom_call" | custom-call | flops 4294967296 | tf_op jit(solution)/shard_map/linear/pallas_call | solution.py:288
  147.5 4.1 %collective-permute-done.23.refs_7_ = f32[8,2048]{1,0:T(8,128)S(1)} collective-permute-done((f32[8,2048]{1,0:T(8,128)S(1)}, f32[8,2048]{1,0:T(8,128)S(1)}, u32[]{:S(2)}, u32[]{:S(2)}) %collective-permute-start.23) | collective-permute-done | bytes 65568 | tf_op jit(solution)/shard_map/ppermute | solution.py:50
  152.2 6.2 %backward.2 = (bf16[512,1024]{1,0:T(8,128)(2,1)}, f32[8,1024]{1,0:T(8,128)}, bf16[512,2048]{1,0:T(8,128)(2,1)}) custom-call(s32[1]{0:T(128)} %bitcast.5.refs_0_, f32[3,2048]{1,0:T(4,128)} %refs_1_.3, f32[512,128]{1,0:T(8,128)} %copy-done.4, bf16[512,2048]{1,0:T(8,128)(2,1)} %refs_3_.3, f32[512,1024]{1,0:T(8,128)} %copy-done.5, f32[8,2048]{1,0:T(8,128)} %copy-done.19, ...), custom_call_target="tpu_custom_call" | custom-call | flops 26214400 | tf_op jit(solution)/shard_map/backward/pallas_call | solution.py:432
  158.4 6.2 %backward.3 = (bf16[512,1024]{1,0:T(8,128)(2,1)}, f32[8,1024]{1,0:T(8,128)}, bf16[512,2048]{1,0:T(8,128)(2,1)}) custom-call(s32[1]{0:T(128)} %bitcast.5.refs_0_, f32[3,2048]{1,0:T(4,128)} %refs_1_.3, f32[512,128]{1,0:T(8,128)} %copy-done.4, bf16[512,2048]{1,0:T(8,128)(2,1)} %refs_3_.3, f32[512,1024]{1,0:T(8,128)} %copy-done.12, ...), custom_call_target="tpu_custom_call", output_to_operand_aliasing={{2}: (9, {})} | custom-call | flops 26214400 | tf_op jit(solution)/shard_map/backward/pallas_call | solution.py:432
  170.2 8.9 %outers.1 = (bf16[512,1024]{1,0:T(8,128)(2,1)}, bf16[512,1024]{1,0:T(8,128)(2,1)}, bf16[512,1024]{1,0:T(8,128)(2,1)}, bf16[512,1024]{1,0:T(8,128)(2,1)}) custom-call(s32[3]{0:T(128)} %copy-done.22, bf16[2,1024,512]{2,1,0:T(8,128)(2,1)} %copy-done.2, bf16[1024,512]{1,0:T(8,128)(2,1)} %copy-done.37, bf16[512,1024]{1,0:T(8,128)(2,1)} %get-tuple-element.130.refs_2_.refs_1_, ...), custom_call_target="tpu_custom_call" | custom-call | tf_op jit(solution)/shard_map/outers/pallas_call | solution.py:503
  182.5 15.3 %hidden_grads.1 = (bf16[512,2048]{1,0:T(8,128)(2,1)}, bf16[128,2048]{1,0:T(8,128)(2,1)}, bf16[128,2048]{1,0:T(8,128)(2,1)}, bf16[128,2048]{1,0:T(8,128)(2,1)}, b...) custom-call(s32[3]{0:T(128)} %copy-done.22, ...), custom_call_target="tpu_custom_call" | custom-call | tf_op jit(solution)/shard_map/hidden_grads/pallas_call | solution.py:595
  197.8 6.8 %collective-permute-done.28.refs_1_ = bf16[512,1024]{1,0:T(8,128)(2,1)S(1)} collective-permute-done((bf16[512,1024]{1,0:T(8,128)(2,1)}, bf16[512,1024]{1,0:T(8,128)(2,1)S(1)}, u32[]{:S(2)}, u32[]{:S(2)}) %collective-permute-start.28) | collective-permute-done | bytes 1048608 | tf_op jit(solution)/shard_map/ppermute | solution.py:50
  214.2 9.9 %collective-permute-done.32.refs_5_ = bf16[256,1024]{1,0:T(8,128)(2,1)S(1)} collective-permute-done((bf16[256,1024]{1,0:T(8,128)(2,1)}, bf16[256,1024]{1,0:T(8,128)(2,1)S(1)}, u32[]{:S(2)}, u32[]{:S(2)}) %collective-permute-start.32) | collective-permute-done | bytes 524320 | tf_op jit(solution)/shard_map/ppermute | solution.py:50
  228.8 3.4 collective-permute-done.33.refs_17_
  240.3 16.7 %collective-permute-done.35.refs_6_ = bf16[128,2048]{1,0:T(8,128)(2,1)S(1)} collective-permute-done((bf16[128,2048]{1,0:T(8,128)(2,1)}, bf16[128,2048]{1,0:T(8,128)(2,1)S(1)}, u32[]{:S(2)}, u32[]{:S(2)}) %collective-permute-start.35) | collective-permute-done | bytes 524320 | tf_op jit(solution)/shard_map/ppermute | solution.py:50
  259.3 3.8 %collective-permute-done.36.refs_18_ = bf16[128,2048]{1,0:T(8,128)(2,1)S(1)} collective-permute-done((bf16[128,2048]{1,0:T(8,128)(2,1)S(1)}, bf16[128,2048]{1,0:T(8,128)(2,1)S(1)}, u32[]{:S(2)}, u32[]{:S(2)}) %collective-permute-start.36) | collective-permute-done | bytes 524320 | tf_op jit(solution)/shard_map/ppermute | solution.py:50
  271.0 12.8 %collective-permute-done.41.refs_7_ = bf16[64,2048]{1,0:T(8,128)(2,1)S(1)} collective-permute-done((bf16[64,2048]{1,0:T(8,128)(2,1)}, bf16[64,2048]{1,0:T(8,128)(2,1)S(1)}, u32[]{:S(2)}, u32[]{:S(2)}) %collective-permute-start.41) | collective-permute-done | bytes 262176 | tf_op jit(solution)/shard_map/ppermute | solution.py:50
  287.9 3.8 %piece_totals.1 = (bf16[64,2048]{1,0:T(8,128)(2,1)}, f32[8,2048]{1,0:T(8,128)}) custom-call(s32[8]{0:T(128)} %stack.72.places, bf16[512,1024]{1,0:T(8,128)(2,1)} %get-tuple-element.138.refs_0_, bf16[512,1024]{1,0:T(8,128)(2,1)} %copy-done.30, bf16[256,1024]{1,0:T(8,128)(2,1)} %copy-done.34, bf16[512,1024]{1,0:T(8,128)(2,1)} %get-tuple-element.139.refs_2_.refs_3_, ...), custom_call_target="tpu_custom_call" | custom-call | tf_op jit(solution)/shard_map/piece_totals/pallas_call | solution.py:790
  297.6 3.4 collective-permute-done.47
  315.7 23.0 %collective-permute-done.54 = f32[8,2048]{1,0:T(8,128)S(1)} collective-permute-done((f32[8,2048]{1,0:T(8,128)S(1)}, f32[8,2048]{1,0:T(8,128)S(1)}, u32[]{:S(2)}, u32[]{:S(2)}) %collective-permute-start.54) | collective-permute-done | bytes 65568 | tf_op jit(solution)/shard_map/ppermute | solution.py:50
  349.9 15.4 %near_back.1.base_ref = f32[512,2048]{1,0:T(8,128)} custom-call(bf16[512,512]{1,0:T(8,128)(2,1)} %get-tuple-element.199.refs_0_, bf16[512,512]{1,0:T(8,128)(2,1)} %copy-done.40, bf16[512,512]{1,0:T(8,128)(2,1)} %collective-permute-done.30.refs_2_, bf16[512,512]{1,0:T(8,128)(2,1)} %collective-permute-done.39.refs_3_, ...), custom_call_target="tpu_custom_call" | custom-call | tf_op jit(solution)/shard_map/near_back/pallas_call | solution.py:652
  365.2 9.5 %fusion.4 = (bf16[512,2048]{1,0:T(8,128)(2,1)}, f32[512,2048]{1,0:T(8,128)}, f32[512,2048]{1,0:T(8,128)}, f32[512,2048]{1,0:T(8,128)}) fusion(f32[512,2048]{1,0:T(8,128)S(1)} %copy-done.29, f32[]{:T(128)} %bitcast.18, bf16[256,2048]{1,0:T(8,128)(2,1)S(1)} %collective-permute-done.57, bf16[256,2048]{1,0:T(8,128)(2,1)S(1)} %bitcast_select_fusion.1, ...), kind=kLoop, calls=%fused_computation.30 | loop fusion | flops 17825792 | bytes 29360644 | tf_op jit(solution)/shard_map/convert_element_type | solution.py:1015
  375.6 4.8 %give_back.1 = bf16[512,2048]{1,0:T(8,128)(2,1)} custom-call(bf16[512,896]{1,0:T(8,128)(2,1)} %copy-done.3, f32[512,2048]{1,0:T(8,128)} %near_back.1.base_ref, bf16[128,2048]{1,0:T(8,128)(2,1)} %collective-permute-done.58.refs_0_, bf16[128,2048]{1,0:T(8,128)(2,1)} %copy-done.48), custom_call_target="tpu_custom_call" | custom-call | tf_op jit(solution)/shard_map/give_back/pallas_call | solution.py:679
  (278 shorter events, 133.6 us)
Async XLA Ops:
  0.6 32.6 %collective-permute-start = (bf16[512,2048]{1,0:T(8,128)(2,1)}, bf16[512,2048]{1,0:T(8,128)(2,1)S(1)}, u32[]{:S(2)}, u32[]{:S(2)}) collective-permute-start(bf16[512,2048]{1,0:T(8,128)(2,1)} %refs_0_.1), channel_id=1, source_target_pairs={{0,1},{1,0},{2,3},{3,2},{4,5},{5,4},{6,7},{7,6},{8,9},{9,8},{10,11... | collective-permute-start | bytes 6291464 | tf_op jit(solution)/shard_map/ppermute | solution.py:50
  4.4 28.8 %collective-permute-start.1 = (bf16[256,2048]{1,0:T(8,128)(2,1)S(1)}, bf16[256,2048]{1,0:T(8,128)(2,1)S(1)}, u32[]{:S(2)}, u32[]{:S(2)}) collective-permute-start(bf16[256,2048]{1,0:T(8,128)(2,1)S(1)} %get-tuple-element.98), channel_id=1, source_target_pairs={{0,2},{1,3},{2,0},{3,1},{4,6},{5,7},{6,4},{7,5},{8,10},{9,11},{10,... | collective-permute-start | bytes 3145736 | tf_op jit(solution)/shard_map/ppermute | solution.py:50
  7.0 26.2 %collective-permute-start.2 = (bf16[128,2048]{1,0:T(8,128)(2,1)S(1)}, bf16[128,2048]{1,0:T(8,128)(2,1)S(1)}, u32[]{:S(2)}, u32[]{:S(2)}) collective-permute-start(bf16[128,2048]{1,0:T(8,128)(2,1)S(1)} %get-tuple-element.100), channel_id=1, source_target_pairs={{0,16},{1,17},{2,18},{3,19},{4,20},{5,21},{6,22},{7,23},{8,24},{9,... | collective-permute-start | bytes 1572872 | tf_op jit(solution)/shard_map/ppermute | solution.py:50
  34.5 27.7 %collective-permute-start.5 = (bf16[256,2048]{1,0:T(8,128)(2,1)S(1)}, bf16[256,2048]{1,0:T(8,128)(2,1)S(1)}, u32[]{:S(2)}, u32[]{:S(2)}) collective-permute-start(bf16[256,2048]{1,0:T(8,128)(2,1)S(1)} %collective-permute-done.1.refs_2_), channel_id=1, source_target_pairs={{0,1},{1,0},{2,3},{3,2},{4,5},{5,4},{6,7},{7,6},{8,9},{9,8},{10,11... | collective-permute-start | bytes 3145736 | tf_op jit(solution)/shard_map/ppermute | solution.py:50
  34.5 27.7 %collective-permute-start.4 = (bf16[256,2048]{1,0:T(8,128)(2,1)S(1)}, bf16[256,2048]{1,0:T(8,128)(2,1)S(1)}, u32[]{:S(2)}, u32[]{:S(2)}) collective-permute-start(bf16[256,2048]{1,0:T(8,128)(2,1)S(1)} %get-tuple-element.102), channel_id=1, source_target_pairs={{0,2},{1,3},{2,0},{3,1},{4,6},{5,7},{6,4},{7,5},{8,10},{9,11},{10,... | collective-permute-start | bytes 3145736 | tf_op jit(solution)/shard_map/ppermute | solution.py:50
  36.7 25.6 %collective-permute-start.6 = (bf16[128,2048]{1,0:T(8,128)(2,1)S(1)}, bf16[128,2048]{1,0:T(8,128)(2,1)S(1)}, u32[]{:S(2)}, u32[]{:S(2)}) collective-permute-start(bf16[128,2048]{1,0:T(8,128)(2,1)S(1)} %get-tuple-element.105), channel_id=1, source_target_pairs={{0,24},{1,25},{2,26},{3,27},{4,28},{5,29},{6,30},{7,31},{8,16},{9,... | collective-permute-start | bytes 1572872 | tf_op jit(solution)/shard_map/ppermute | solution.py:50
  62.2 29.6 %collective-permute-start.12 = (bf16[512,2048]{1,0:T(8,128)(2,1)S(1)}, bf16[512,2048]{1,0:T(8,128)(2,1)S(1)}, u32[]{:S(2)}, u32[]{:S(2)}) collective-permute-start(bf16[512,2048]{1,0:T(8,128)(2,1)S(1)} %convert_element_type.29.refs_0_.refs_3_), channel_id=1, source_target_pairs={{0,1},{1,0},{2,3},{3,2},{4,5},{5,4},{6,7},{7,6},{8,9},{9,8},{10,11... | collective-permute-start | bytes 6291464 | tf_op jit(solution)/shard_map/ppermute | solution.py:50
  62.4 29.4 %collective-permute-start.11 = (bf16[256,2048]{1,0:T(8,128)(2,1)S(1)}, bf16[256,2048]{1,0:T(8,128)(2,1)S(1)}, u32[]{:S(2)}, u32[]{:S(2)}) collective-permute-start(bf16[256,2048]{1,0:T(8,128)(2,1)S(1)} %get-tuple-element.115), channel_id=1, source_target_pairs={{0,2},{1,3},{2,0},{3,1},{4,6},{5,7},{6,4},{7,5},{8,10},{9,11},{10,... | collective-permute-start | bytes 3145736 | tf_op jit(solution)/shard_map/ppermute | solution.py:50
  64.0 27.9 %collective-permute-start.8 = (bf16[256,2048]{1,0:T(8,128)(2,1)S(1)}, bf16[256,2048]{1,0:T(8,128)(2,1)S(1)}, u32[]{:S(2)}, u32[]{:S(2)}) collective-permute-start(bf16[256,2048]{1,0:T(8,128)(2,1)S(1)} %collective-permute-done.4.refs_3_), channel_id=1, source_target_pairs={{0,1},{1,0},{2,3},{3,2},{4,5},{5,4},{6,7},{7,6},{8,9},{9,8},{10,11... | collective-permute-start | bytes 3145736 | tf_op jit(solution)/shard_map/ppermute | solution.py:50
  64.2 27.3 %collective-permute-start.10 = (bf16[128,2048]{1,0:T(8,128)(2,1)S(1)}, bf16[128,2048]{1,0:T(8,128)(2,1)S(1)}, u32[]{:S(2)}, u32[]{:S(2)}) collective-permute-start(bf16[128,2048]{1,0:T(8,128)(2,1)S(1)} %get-tuple-element.113), channel_id=1, source_target_pairs={{0,20},{1,21},{2,22},{3,23},{4,16},{5,17},{6,18},{7,19},{8,28},{9,... | collective-permute-start | bytes 1572872 | tf_op jit(solution)/shard_map/ppermute | solution.py:50
  67.1 24.7 %collective-permute-start.9 = (bf16[128,2048]{1,0:T(8,128)(2,1)S(1)}, bf16[128,2048]{1,0:T(8,128)(2,1)S(1)}, u32[]{:S(2)}, u32[]{:S(2)}) collective-permute-start(bf16[128,2048]{1,0:T(8,128)(2,1)S(1)} %get-tuple-element.111), channel_id=1, source_target_pairs={{0,8},{1,9},{2,10},{3,11},{4,12},{5,13},{6,14},{7,15},{8,0},{9,1},... | collective-permute-start | bytes 1572872 | tf_op jit(solution)/shard_map/ppermute | solution.py:50
  120.6 26.9 %collective-permute-start.14 = (bf16[1024,512]{1,0:T(8,128)(2,1)S(1)}, bf16[1024,512]{1,0:T(8,128)(2,1)S(1)}, u32[]{:S(2)}, u32[]{:S(2)}) collective-permute-start(bf16[1024,512]{1,0:T(8,128)(2,1)S(1)} %slice_bitcast_fusion), channel_id=1, source_target_pairs={{0,1},{1,0},{2,3},{3,2},{4,5},{5,4},{6,7},{7,6},{8,9},{9,8},{10,11... | collective-permute-start | bytes 3145736 | tf_op jit(solution)/shard_map/ppermute | solution.py:50
  179.1 25.5 %collective-permute-start.28 = (bf16[512,1024]{1,0:T(8,128)(2,1)}, bf16[512,1024]{1,0:T(8,128)(2,1)S(1)}, u32[]{:S(2)}, u32[]{:S(2)}) collective-permute-start(bf16[512,1024]{1,0:T(8,128)(2,1)} %get-tuple-element.132), channel_id=1, source_target_pairs={{0,2},{1,3},{2,0},{3,1},{4,6},{5,7},{6,4},{7,5},{8,10},{9,11},{10,... | collective-permute-start | bytes 3145736 | tf_op jit(solution)/shard_map/ppermute | solution.py:50
  180.2 25.1 %collective-permute-start.29 = (bf16[512,1024]{1,0:T(8,128)(2,1)}, bf16[512,1024]{1,0:T(8,128)(2,1)S(1)}, u32[]{:S(2)}, u32[]{:S(2)}) collective-permute-start(bf16[512,1024]{1,0:T(8,128)(2,1)} %get-tuple-element.134), channel_id=1, source_target_pairs={{0,4},{1,5},{2,6},{3,7},{4,0},{5,1},{6,2},{7,3},{8,12},{9,13},{10,... | collective-permute-start | bytes 3145736 | tf_op jit(solution)/shard_map/ppermute | solution.py:50
  205.3 29.5 %collective-permute-start.34 = (bf16[512,2048]{1,0:T(8,128)(2,1)}, bf16[512,2048]{1,0:T(8,128)(2,1)}, u32[]{:S(2)}, u32[]{:S(2)}) collective-permute-start(bf16[512,2048]{1,0:T(8,128)(2,1)} %get-tuple-element.146.refs_4_), channel_id=1, source_target_pairs={{0,1},{1,0},{2,3},{3,2},{4,5},{5,4},{6,7},{7,6},{8,9},{9,8},{10,11... | collective-permute-start | bytes 6291464 | tf_op jit(solution)/shard_map/ppermute | solution.py:50
  205.3 26.8 %collective-permute-start.33 = (bf16[128,2048]{1,0:T(8,128)(2,1)}, bf16[128,2048]{1,0:T(8,128)(2,1)}, u32[]{:S(2)}, u32[]{:S(2)}) collective-permute-start(bf16[128,2048]{1,0:T(8,128)(2,1)} %get-tuple-element.145), channel_id=1, source_target_pairs={{0,16},{1,17},{2,18},{3,19},{4,20},{5,21},{6,22},{7,23},{8,24},{9,... | collective-permute-start | bytes 1572872 | tf_op jit(solution)/shard_map/ppermute | solution.py:50
  237.7 25.5 %collective-permute-start.36 = (bf16[128,2048]{1,0:T(8,128)(2,1)S(1)}, bf16[128,2048]{1,0:T(8,128)(2,1)S(1)}, u32[]{:S(2)}, u32[]{:S(2)}) collective-permute-start(bf16[128,2048]{1,0:T(8,128)(2,1)S(1)} %copy-done.61), channel_id=1, source_target_pairs={{0,20},{1,21},{2,22},{3,23},{4,16},{5,17},{6,18},{7,19},{8,28},{9,... | collective-permute-start | bytes 1572872 | tf_op jit(solution)/shard_map/ppermute | solution.py:50
  309.8 30.3 %collective-permute-start.52 = (bf16[128,2048]{1,0:T(8,128)(2,1)}, bf16[128,2048]{1,0:T(8,128)(2,1)S(1)}, u32[]{:S(2)}, u32[]{:S(2)}) collective-permute-start(bf16[128,2048]{1,0:T(8,128)(2,1)} %get-tuple-element.172), channel_id=1, source_target_pairs={{0,28},{1,29},{2,30},{3,31},{4,24},{5,25},{6,26},{7,27},{8,20},{9,... | collective-permute-start | bytes 1572872 | tf_op jit(solution)/shard_map/ppermute | solution.py:50
  312.0 26.9 %collective-permute-start.51 = (bf16[128,2048]{1,0:T(8,128)(2,1)S(1)}, bf16[128,2048]{1,0:T(8,128)(2,1)}, u32[]{:S(2)}, u32[]{:S(2)}) collective-permute-start(bf16[128,2048]{1,0:T(8,128)(2,1)S(1)} %bitcast_select_fusion.2), channel_id=1, source_target_pairs={{0,8},{1,9},{2,10},{3,11},{4,12},{5,13},{6,14},{7,15},{8,0},{9,1},... | collective-permute-start | bytes 1572872 | tf_op jit(solution)/shard_map/ppermute | solution.py:50
  312.2 27.9 %collective-permute-start.50 = (bf16[128,2048]{1,0:T(8,128)(2,1)S(1)}, bf16[128,2048]{1,0:T(8,128)(2,1)S(1)}, u32[]{:S(2)}, u32[]{:S(2)}) collective-permute-start(bf16[128,2048]{1,0:T(8,128)(2,1)S(1)} %collective-permute-done.40.refs_7_), channel_id=1, source_target_pairs={{0,1},{1,0},{2,3},{3,2},{4,5},{5,4},{6,7},{7,6},{8,9},{9,8},{10,11... | collective-permute-start | bytes 1572872 | tf_op jit(solution)/shard_map/ppermute | solution.py:50
  312.2 27.9 %collective-permute-start.49 = (bf16[128,2048]{1,0:T(8,128)(2,1)}, bf16[128,2048]{1,0:T(8,128)(2,1)}, u32[]{:S(2)}, u32[]{:S(2)}) collective-permute-start(bf16[128,2048]{1,0:T(8,128)(2,1)} %get-tuple-element.168), channel_id=1, source_target_pairs={{0,2},{1,3},{2,0},{3,1},{4,6},{5,7},{6,4},{7,5},{8,10},{9,11},{10,... | collective-permute-start | bytes 1572872 | tf_op jit(solution)/shard_map/ppermute | solution.py:50
  340.1 25.1 %collective-permute-start.57 = (bf16[256,2048]{1,0:T(8,128)(2,1)S(1)}, bf16[256,2048]{1,0:T(8,128)(2,1)S(1)}, u32[]{:S(2)}, u32[]{:S(2)}) collective-permute-start(bf16[256,2048]{1,0:T(8,128)(2,1)S(1)} %bitcast_select_fusion.1), channel_id=1, source_target_pairs={{0,4},{1,5},{2,6},{3,7},{4,0},{5,1},{6,2},{7,3},{8,12},{9,13},{10,... | collective-permute-start | bytes 3145736 | tf_op jit(solution)/shard_map/ppermute | solution.py:50
  343.6 31.2 %collective-permute-start.59 = (bf16[128,2048]{1,0:T(8,128)(2,1)}, bf16[128,2048]{1,0:T(8,128)(2,1)S(1)}, u32[]{:S(2)}, u32[]{:S(2)}) collective-permute-start(bf16[128,2048]{1,0:T(8,128)(2,1)} %get-tuple-element.183), channel_id=1, source_target_pairs={{0,24},{1,25},{2,26},{3,27},{4,28},{5,29},{6,30},{7,31},{8,16},{9,... | collective-permute-start | bytes 1572872 | tf_op jit(solution)/shard_map/ppermute | solution.py:50
  346.2 28.6 %collective-permute-start.58 = (bf16[128,2048]{1,0:T(8,128)(2,1)}, bf16[128,2048]{1,0:T(8,128)(2,1)}, u32[]{:S(2)}, u32[]{:S(2)}) collective-permute-start(bf16[128,2048]{1,0:T(8,128)(2,1)} %get-tuple-element.181), channel_id=1, source_target_pairs={{0,8},{1,9},{2,10},{3,11},{4,12},{5,13},{6,14},{7,15},{8,0},{9,1},... | collective-permute-start | bytes 1572872 | tf_op jit(solution)/shard_map/ppermute | solution.py:50
  (99 other events, 1795.7 us)

commit v4 on v3

--- a/solution.py
+++ b/solution.py
@@ -74,7 +74,7 @@
 
 def turns(dom_count):
     half = dom_count // 2
-    far = sorted(range(half, dom_count), key=lambda k: (k % 2, k))
+    far = sorted(range(half, dom_count), key=lambda k: (k % 2, k if k % 2 else -k))
     near = sorted(range(1, half), key=lambda k: (k % 2 == 0, k))
     cut = lambda order, n, of: order[n * len(order) // of : (n + 1) * len(order) // of]
     return [cut(far, n, 4) for n in range(4)], [cut(near, n, 3) for n in range(3)]
@@ -432,7 +432,7 @@
     return call(
         kernel,
         flops=50 * rows * span,
-        vmem_mb=56,
+        vmem_mb=62,
         in_specs=[SMEM, VMEM, VMEM, ANY, ANY] + [VMEM] * len(parts) + [ANY] * len(before),
         out_specs=[VMEM, VMEM, ANY],
         out_shape=[
@@ -461,7 +461,7 @@
         pltpu.make_async_copy(source, buffer, sems.at[n])
         for n, (source, buffer) in enumerate(zip(inputs, buffers))
     ]
-    for copy in copies:
+    for copy in copies[:4]:
         copy.start()
     own_flip, near_flip = buffers[:2]
     rows, span = buffers[2].shape
@@ -470,6 +470,9 @@
     for part in range(2):
         for n in ((0, 1, 2, 3), (4, 5))[part]:
             copies[n].wait()
+        if part == 0:
+            for copy in copies[4:]:
+                copy.start()
         grad, near_grad = buffers[2 + 2 * part : 4 + 2 * part]
         for c in range(span // COLS):
             cs = slice(c * COLS, (c + 1) * COLS)
@@ -639,7 +642,7 @@
                 flip = flips_in[done // rows]
                 total += dot(flip[:, done % rows : done % rows + depth], grad[:, cs])
                 done += depth
-            out[:, cs] = total
+            out[:, cs] = total.astype(out.dtype)
 
     blocked = chooser.shape[1] > WHOLE_HALO
     if blocked:
@@ -655,7 +658,7 @@
         vmem_mb=56,
         in_specs=specs,
         out_specs=block(rows) if blocked else VMEM,
-        out_shape=SDS((rows, grads[0].shape[1]), jnp.float32),
+        out_shape=SDS((rows, grads[0].shape[1]), jnp.bfloat16),
         name="near_back",
         **grid,
     )(*flips, *grads, chooser, *blocks)
@@ -674,7 +677,7 @@
         for c in range(out.shape[1] // COLS):
             cs = slice(c * COLS, (c + 1) * COLS)
             pieces = jnp.concatenate([block[:, cs] for block in blocks_in], axis=0)
-            out[:, cs] = (base_ref[:, cs] + dot(picked, pieces)).astype(jnp.bfloat16)
+            out[:, cs] = (base_ref[:, cs].astype(jnp.float32) + dot(picked, pieces)).astype(jnp.bfloat16)
 
     return call(
         kernel,

time: 384 us -> 381 us (level)
  waiting for transfers between devices: 181 us -> 187 us
  starting transfers between devices: 67.1 us -> 62.4 us
    ppermute x60, waiting for transfers between devices: 181 us -> 187 us  [swap(): return lax.ppermute(value, AXES, pairs)]
    ppermute x60, starting transfers between devices: 67.1 us -> 62.4 us  [swap(): return lax.ppermute(value, AXES, pairs)]
  transfers between devices with their start and end apart: 60 -> 60, of which waited for: 30 -> 32; matrix products, arithmetic and copies ran while one was open for 6% -> 6% of each run, Pallas kernels for 17% -> 17%
where the time goes in v4:
time: 381 us; the launch traced here: 378 us
  waiting for transfers between devices  187 us (49%)
  Pallas kernels  87.8 us (23%)
  starting transfers between devices  62.4 us (16%)
  local copies, waits for them, and re-layouts  18.7 us (5%)
  other arithmetic  17.6 us (5%)
    ppermute x60, waiting for transfers between devices, swap(): return lax.ppermute(value, AXES, pairs)  187 us
    ppermute x60, starting transfers between devices, swap(): return lax.ppermute(value, AXES, pairs)  62.4 us
    pallas_call x1, Pallas kernels, hidden_grads(): call(kernel, flops=0, vmem_mb=56, in_specs=[SMEM] + [ANY] * len(inputs),...  15.3 us
    pallas_call x1, Pallas kernels, near_back(): call(kernel, flops=0, vmem_mb=56, in_specs=specs, out_specs=block(rows) i...  14.8 us
    pallas_call x2, Pallas kernels, backward(): call(kernel, flops=50 * rows * span, vmem_mb=62, in_specs=[SMEM, VMEM, VM...  12.4 us
    unnamed x127, local copies, waits for them, and re-layouts  12.2 us
    convert_element_type x1, other arithmetic, on_device(): weight_new.astype(jnp.bfloat16)  9.53 us
    pallas_call x1, Pallas kernels, outers(): call(outers_kernel, flops=0, vmem_mb=56, in_specs=[SMEM] + [ANY] * 6, out...  8.94 us
  transfers between devices with their start and end apart: 60, of which 32 were waited for; matrix products, arithmetic and copies ran while one was open for 6% of the time, Pallas kernels for 17%

profile of v4, /device:TPU:0, one launch (start us, length us, event | category | flops | bytes accessed | tf_op | source)
XLA Modules:
  0.0 377.5 jit_solution(3786709198498597885)
XLA Ops:
  7.0 3.6 collective-permute-start.2
  12.1 10.9 %collective-permute-done.2.refs_8_ = bf16[128,2048]{1,0:T(8,128)(2,1)S(1)} collective-permute-done((bf16[128,2048]{1,0:T(8,128)(2,1)S(1)}, bf16[128,2048]{1,0:T(8,128)(2,1)S(1)}, u32[]{:S(2)}, u32[]{:S(2)}) %collective-permute-start.2) | collective-permute-done | bytes 524320 | tf_op jit(solution)/shard_map/ppermute | solution.py:50
  24.4 6.5 %collective-permute-done.1.refs_2_ = bf16[256,2048]{1,0:T(8,128)(2,1)S(1)} collective-permute-done((bf16[256,2048]{1,0:T(8,128)(2,1)S(1)}, bf16[256,2048]{1,0:T(8,128)(2,1)S(1)}, u32[]{:S(2)}, u32[]{:S(2)}) %collective-permute-start.1) | collective-permute-done | bytes 1048608 | tf_op jit(solution)/shard_map/ppermute | solution.py:50
  40.4 18.4 %collective-permute-done.7.refs_5_ = bf16[128,2048]{1,0:T(8,128)(2,1)S(1)} collective-permute-done((bf16[128,2048]{1,0:T(8,128)(2,1)S(1)}, bf16[128,2048]{1,0:T(8,128)(2,1)S(1)}, u32[]{:S(2)}, u32[]{:S(2)}) %collective-permute-start.7) | collective-permute-done | bytes 524320 | tf_op jit(solution)/shard_map/ppermute | solution.py:50
  66.5 24.0 %collective-permute-done.10.refs_7_ = bf16[128,2048]{1,0:T(8,128)(2,1)S(1)} collective-permute-done((bf16[128,2048]{1,0:T(8,128)(2,1)S(1)}, bf16[128,2048]{1,0:T(8,128)(2,1)S(1)}, u32[]{:S(2)}, u32[]{:S(2)}) %collective-permute-start.10) | collective-permute-done | bytes 524320 | tf_op jit(solution)/shard_map/ppermute | solution.py:50
  96.3 4.5 %near.1.refs_1_ = f32[512,2048]{1,0:T(8,128)S(1)} custom-call(bf16[512,2048]{1,0:T(8,128)(2,1)S(1)} %get-tuple-element.97.wide, bf16[512,2048]{1,0:T(8,128)(2,1)S(1)} %copy-done.9, bf16[512,2048]{1,0:T(8,128)(2,1)S(1)} %copy-done.28, bf16[256,2048]{1,0:T(8,128)(2,1)S(1)} %collective-permute-done.1.refs_2_, ...), custom_call_target="tpu_custom_call" | custom-call | flops 4294967296 | tf_op jit(solution)/shard_map/near/pallas_call | solution.py:195
  101.0 14.7 %collective-permute-done.15.refs_3_.refs_6_ = bf16[256,2048]{1,0:T(8,128)(2,1)S(1)} collective-permute-done((bf16[256,2048]{1,0:T(8,128)(2,1)S(1)}, bf16[256,2048]{1,0:T(8,128)(2,1)S(1)}, u32[]{:S(2)}, u32[]{:S(2)}) %collective-permute-start.15) | collective-permute-done | bytes 1048608 | tf_op jit(solution)/shard_map/ppermute | solution.py:50
  121.0 8.3 %linear.1 = (f32[512,1024]{1,0:T(8,128)S(1)}, f32[512,1024]{1,0:T(8,128)S(1)}, f32[8,2048]{1,0:T(8,128)S(1)}) custom-call(s32[3]{0:T(128)S(1)} %pad_add_fusion.me.refs_0_, bf16[512,2048]{1,0:T(8,128)(2,1)S(1)} %get-tuple-element.120.hidden, f32[3,2048]{1,0:T(4,128)S(1)} %copy-done.20, f32[512,128]{1,0:T(8,128)S(1)} %broadcast_in_dim.124.mask_ref.refs_2_, ...), custom_call_target="tpu_custom_call" | custom-call | flops 4294967296 | tf_op jit(solution)/shard_map/linear/pallas_call | solution.py:288
  149.5 6.2 %backward.2 = (bf16[512,1024]{1,0:T(8,128)(2,1)}, f32[8,1024]{1,0:T(8,128)}, bf16[512,2048]{1,0:T(8,128)(2,1)}) custom-call(s32[1]{0:T(128)} %bitcast.5.refs_0_, f32[3,2048]{1,0:T(4,128)} %refs_1_.3, f32[512,128]{1,0:T(8,128)} %copy-done.4, bf16[512,2048]{1,0:T(8,128)(2,1)} %refs_3_.3, f32[512,1024]{1,0:T(8,128)} %copy-done.5, f32[8,2048]{1,0:T(8,128)} %copy-done.19, ...), custom_call_target="tpu_custom_call" | custom-call | flops 26214400 | tf_op jit(solution)/shard_map/backward/pallas_call | solution.py:432
  155.7 6.2 %backward.3 = (bf16[512,1024]{1,0:T(8,128)(2,1)}, f32[8,1024]{1,0:T(8,128)}, bf16[512,2048]{1,0:T(8,128)(2,1)}) custom-call(s32[1]{0:T(128)} %bitcast.5.refs_0_, f32[3,2048]{1,0:T(4,128)} %refs_1_.3, f32[512,128]{1,0:T(8,128)} %copy-done.4, bf16[512,2048]{1,0:T(8,128)(2,1)} %refs_3_.3, f32[512,1024]{1,0:T(8,128)} %copy-done.12, ...), custom_call_target="tpu_custom_call", output_to_operand_aliasing={{2}: (9, {})} | custom-call | flops 26214400 | tf_op jit(solution)/shard_map/backward/pallas_call | solution.py:432
  167.4 8.9 %outers.1 = (bf16[512,1024]{1,0:T(8,128)(2,1)}, bf16[512,1024]{1,0:T(8,128)(2,1)}, bf16[512,1024]{1,0:T(8,128)(2,1)}, bf16[512,1024]{1,0:T(8,128)(2,1)}) custom-call(s32[3]{0:T(128)} %copy-done.22, bf16[2,1024,512]{2,1,0:T(8,128)(2,1)} %copy-done.2, bf16[1024,512]{1,0:T(8,128)(2,1)} %copy-done.37, bf16[512,1024]{1,0:T(8,128)(2,1)} %get-tuple-element.130.refs_2_.refs_1_, ...), custom_call_target="tpu_custom_call" | custom-call | tf_op jit(solution)/shard_map/outers/pallas_call | solution.py:506
  180.0 15.3 %hidden_grads.1 = (bf16[512,2048]{1,0:T(8,128)(2,1)}, bf16[128,2048]{1,0:T(8,128)(2,1)}, bf16[128,2048]{1,0:T(8,128)(2,1)}, bf16[128,2048]{1,0:T(8,128)(2,1)}, b...) custom-call(s32[3]{0:T(128)} %copy-done.22, ...), custom_call_target="tpu_custom_call" | custom-call | tf_op jit(solution)/shard_map/hidden_grads/pallas_call | solution.py:598
  195.3 6.6 %collective-permute-done.28.refs_1_ = bf16[512,1024]{1,0:T(8,128)(2,1)S(1)} collective-permute-done((bf16[512,1024]{1,0:T(8,128)(2,1)}, bf16[512,1024]{1,0:T(8,128)(2,1)S(1)}, u32[]{:S(2)}, u32[]{:S(2)}) %collective-permute-start.28) | collective-permute-done | bytes 1048608 | tf_op jit(solution)/shard_map/ppermute | solution.py:50
  212.8 9.8 %collective-permute-done.32.refs_5_ = bf16[256,1024]{1,0:T(8,128)(2,1)S(1)} collective-permute-done((bf16[256,1024]{1,0:T(8,128)(2,1)}, bf16[256,1024]{1,0:T(8,128)(2,1)S(1)}, u32[]{:S(2)}, u32[]{:S(2)}) %collective-permute-start.32) | collective-permute-done | bytes 524320 | tf_op jit(solution)/shard_map/ppermute | solution.py:50
  227.2 6.0 %collective-permute-done.30.refs_2_ = bf16[512,512]{1,0:T(8,128)(2,1)} collective-permute-done((bf16[512,512]{1,0:T(8,128)(2,1)}, bf16[512,512]{1,0:T(8,128)(2,1)}, u32[]{:S(2)}, u32[]{:S(2)}) %collective-permute-start.30) | collective-permute-done | bytes 524320 | tf_op jit(solution)/shard_map/ppermute | solution.py:50
  237.7 17.3 %collective-permute-done.35.refs_6_ = bf16[128,2048]{1,0:T(8,128)(2,1)S(1)} collective-permute-done((bf16[128,2048]{1,0:T(8,128)(2,1)}, bf16[128,2048]{1,0:T(8,128)(2,1)S(1)}, u32[]{:S(2)}, u32[]{:S(2)}) %collective-permute-start.35) | collective-permute-done | bytes 524320 | tf_op jit(solution)/shard_map/ppermute | solution.py:50
  255.9 5.1 %collective-permute-done.36.refs_17_ = bf16[128,2048]{1,0:T(8,128)(2,1)S(1)} collective-permute-done((bf16[128,2048]{1,0:T(8,128)(2,1)S(1)}, bf16[128,2048]{1,0:T(8,128)(2,1)S(1)}, u32[]{:S(2)}, u32[]{:S(2)}) %collective-permute-start.36) | collective-permute-done | bytes 524320 | tf_op jit(solution)/shard_map/ppermute | solution.py:50
  268.0 13.5 %collective-permute-done.41.refs_7_ = bf16[64,2048]{1,0:T(8,128)(2,1)S(1)} collective-permute-done((bf16[64,2048]{1,0:T(8,128)(2,1)}, bf16[64,2048]{1,0:T(8,128)(2,1)S(1)}, u32[]{:S(2)}, u32[]{:S(2)}) %collective-permute-start.41) | collective-permute-done | bytes 262176 | tf_op jit(solution)/shard_map/ppermute | solution.py:50
  286.9 3.8 %piece_totals.1 = (bf16[64,2048]{1,0:T(8,128)(2,1)}, f32[8,2048]{1,0:T(8,128)}) custom-call(s32[8]{0:T(128)} %stack.72.places, bf16[512,1024]{1,0:T(8,128)(2,1)} %get-tuple-element.138.refs_0_, bf16[512,1024]{1,0:T(8,128)(2,1)} %copy-done.30, bf16[256,1024]{1,0:T(8,128)(2,1)} %copy-done.34, bf16[512,1024]{1,0:T(8,128)(2,1)} %get-tuple-element.139.refs_2_.refs_3_, ...), custom_call_target="tpu_custom_call" | custom-call | tf_op jit(solution)/shard_map/piece_totals/pallas_call | solution.py:793
  294.0 5.6 %collective-permute-done.47 = f32[8,2048]{1,0:T(8,128)S(1)} collective-permute-done((f32[8,2048]{1,0:T(8,128)S(1)}, f32[8,2048]{1,0:T(8,128)S(1)}, u32[]{:S(2)}, u32[]{:S(2)}) %collective-permute-start.47) | collective-permute-done | bytes 65568 | tf_op jit(solution)/shard_map/ppermute | solution.py:50
  314.7 21.7 %collective-permute-done.54 = f32[8,2048]{1,0:T(8,128)S(1)} collective-permute-done((f32[8,2048]{1,0:T(8,128)S(1)}, f32[8,2048]{1,0:T(8,128)S(1)}, u32[]{:S(2)}, u32[]{:S(2)}) %collective-permute-start.54) | collective-permute-done | bytes 65568 | tf_op jit(solution)/shard_map/ppermute | solution.py:50
  348.1 14.8 %near_back.1.base_ref = bf16[512,2048]{1,0:T(8,128)(2,1)} custom-call(bf16[512,512]{1,0:T(8,128)(2,1)} %get-tuple-element.199.refs_0_, bf16[512,512]{1,0:T(8,128)(2,1)} %copy-done.40, bf16[512,512]{1,0:T(8,128)(2,1)} %collective-permute-done.30.refs_2_, bf16[512,512]{1,0:T(8,128)(2,1)} %collective-permute-done.39.refs_3_, ...), custom_call_target="tpu_custom_call" | custom-call | tf_op jit(solution)/shard_map/near_back/pallas_call | solution.py:655
  362.9 9.5 %fusion.4 = (bf16[512,2048]{1,0:T(8,128)(2,1)}, f32[512,2048]{1,0:T(8,128)}, f32[512,2048]{1,0:T(8,128)}, f32[512,2048]{1,0:T(8,128)}) fusion(f32[512,2048]{1,0:T(8,128)S(1)} %copy-done.29, f32[]{:T(128)} %bitcast.18, bf16[256,2048]{1,0:T(8,128)(2,1)S(1)} %collective-permute-done.57, bf16[256,2048]{1,0:T(8,128)(2,1)S(1)} %bitcast_select_fusion.1, ...), kind=kLoop, calls=%fused_computation.30 | loop fusion | flops 17825792 | bytes 29360644 | tf_op jit(solution)/shard_map/convert_element_type | solution.py:1018
  373.2 4.1 %give_back.1 = bf16[512,2048]{1,0:T(8,128)(2,1)} custom-call(bf16[512,896]{1,0:T(8,128)(2,1)} %copy-done.3, bf16[512,2048]{1,0:T(8,128)(2,1)} %near_back.1.base_ref, bf16[128,2048]{1,0:T(8,128)(2,1)} %collective-permute-done.58.refs_0_, bf16[128,2048]{1,0:T(8,128)(2,1)} %copy-done.48), custom_call_target="tpu_custom_call" | custom-call | tf_op jit(solution)/shard_map/give_back/pallas_call | solution.py:682
  (278 shorter events, 128.5 us)
Async XLA Ops:
  0.6 30.2 %collective-permute-start = (bf16[512,2048]{1,0:T(8,128)(2,1)}, bf16[512,2048]{1,0:T(8,128)(2,1)S(1)}, u32[]{:S(2)}, u32[]{:S(2)}) collective-permute-start(bf16[512,2048]{1,0:T(8,128)(2,1)} %refs_0_.1), channel_id=1, source_target_pairs={{0,1},{1,0},{2,3},{3,2},{4,5},{5,4},{6,7},{7,6},{8,9},{9,8},{10,11... | collective-permute-start | bytes 6291464 | tf_op jit(solution)/shard_map/ppermute | solution.py:50
  4.4 26.4 %collective-permute-start.1 = (bf16[256,2048]{1,0:T(8,128)(2,1)S(1)}, bf16[256,2048]{1,0:T(8,128)(2,1)S(1)}, u32[]{:S(2)}, u32[]{:S(2)}) collective-permute-start(bf16[256,2048]{1,0:T(8,128)(2,1)S(1)} %get-tuple-element.98), channel_id=1, source_target_pairs={{0,2},{1,3},{2,0},{3,1},{4,6},{5,7},{6,4},{7,5},{8,10},{9,11},{10,... | collective-permute-start | bytes 3145736 | tf_op jit(solution)/shard_map/ppermute | solution.py:50
  30.8 30.6 %collective-permute-start.5 = (bf16[256,2048]{1,0:T(8,128)(2,1)S(1)}, bf16[256,2048]{1,0:T(8,128)(2,1)S(1)}, u32[]{:S(2)}, u32[]{:S(2)}) collective-permute-start(bf16[256,2048]{1,0:T(8,128)(2,1)S(1)} %collective-permute-done.1.refs_2_), channel_id=1, source_target_pairs={{0,1},{1,0},{2,3},{3,2},{4,5},{5,4},{6,7},{7,6},{8,9},{9,8},{10,11... | collective-permute-start | bytes 3145736 | tf_op jit(solution)/shard_map/ppermute | solution.py:50
  30.8 30.6 %collective-permute-start.4 = (bf16[256,2048]{1,0:T(8,128)(2,1)S(1)}, bf16[256,2048]{1,0:T(8,128)(2,1)S(1)}, u32[]{:S(2)}, u32[]{:S(2)}) collective-permute-start(bf16[256,2048]{1,0:T(8,128)(2,1)S(1)} %get-tuple-element.102), channel_id=1, source_target_pairs={{0,2},{1,3},{2,0},{3,1},{4,6},{5,7},{6,4},{7,5},{8,10},{9,11},{10,... | collective-permute-start | bytes 3145736 | tf_op jit(solution)/shard_map/ppermute | solution.py:50
  32.6 26.1 %collective-permute-start.7 = (bf16[128,2048]{1,0:T(8,128)(2,1)S(1)}, bf16[128,2048]{1,0:T(8,128)(2,1)S(1)}, u32[]{:S(2)}, u32[]{:S(2)}) collective-permute-start(bf16[128,2048]{1,0:T(8,128)(2,1)S(1)} %get-tuple-element.107), channel_id=1, source_target_pairs={{0,12},{1,13},{2,14},{3,15},{4,8},{5,9},{6,10},{7,11},{8,4},{9,5},... | collective-permute-start | bytes 1572872 | tf_op jit(solution)/shard_map/ppermute | solution.py:50
  35.5 26.0 %collective-permute-start.6 = (bf16[128,2048]{1,0:T(8,128)(2,1)S(1)}, bf16[128,2048]{1,0:T(8,128)(2,1)S(1)}, u32[]{:S(2)}, u32[]{:S(2)}) collective-permute-start(bf16[128,2048]{1,0:T(8,128)(2,1)S(1)} %get-tuple-element.105), channel_id=1, source_target_pairs={{0,16},{1,17},{2,18},{3,19},{4,20},{5,21},{6,22},{7,23},{8,24},{9,... | collective-permute-start | bytes 1572872 | tf_op jit(solution)/shard_map/ppermute | solution.py:50
  61.5 29.1 %collective-permute-start.12 = (bf16[512,2048]{1,0:T(8,128)(2,1)S(1)}, bf16[512,2048]{1,0:T(8,128)(2,1)S(1)}, u32[]{:S(2)}, u32[]{:S(2)}) collective-permute-start(bf16[512,2048]{1,0:T(8,128)(2,1)S(1)} %convert_element_type.29.refs_0_.refs_3_), channel_id=1, source_target_pairs={{0,1},{1,0},{2,3},{3,2},{4,5},{5,4},{6,7},{7,6},{8,9},{9,8},{10,11... | collective-permute-start | bytes 6291464 | tf_op jit(solution)/shard_map/ppermute | solution.py:50
  61.7 28.9 %collective-permute-start.11 = (bf16[256,2048]{1,0:T(8,128)(2,1)S(1)}, bf16[256,2048]{1,0:T(8,128)(2,1)S(1)}, u32[]{:S(2)}, u32[]{:S(2)}) collective-permute-start(bf16[256,2048]{1,0:T(8,128)(2,1)S(1)} %get-tuple-element.115), channel_id=1, source_target_pairs={{0,2},{1,3},{2,0},{3,1},{4,6},{5,7},{6,4},{7,5},{8,10},{9,11},{10,... | collective-permute-start | bytes 3145736 | tf_op jit(solution)/shard_map/ppermute | solution.py:50
  63.3 27.3 %collective-permute-start.8 = (bf16[256,2048]{1,0:T(8,128)(2,1)S(1)}, bf16[256,2048]{1,0:T(8,128)(2,1)S(1)}, u32[]{:S(2)}, u32[]{:S(2)}) collective-permute-start(bf16[256,2048]{1,0:T(8,128)(2,1)S(1)} %collective-permute-done.4.refs_3_), channel_id=1, source_target_pairs={{0,1},{1,0},{2,3},{3,2},{4,5},{5,4},{6,7},{7,6},{8,9},{9,8},{10,11... | collective-permute-start | bytes 3145736 | tf_op jit(solution)/shard_map/ppermute | solution.py:50
  63.5 27.1 %collective-permute-start.10 = (bf16[128,2048]{1,0:T(8,128)(2,1)S(1)}, bf16[128,2048]{1,0:T(8,128)(2,1)S(1)}, u32[]{:S(2)}, u32[]{:S(2)}) collective-permute-start(bf16[128,2048]{1,0:T(8,128)(2,1)S(1)} %get-tuple-element.113), channel_id=1, source_target_pairs={{0,20},{1,21},{2,22},{3,23},{4,16},{5,17},{6,18},{7,19},{8,28},{9,... | collective-permute-start | bytes 1572872 | tf_op jit(solution)/shard_map/ppermute | solution.py:50
  63.7 26.8 %collective-permute-start.9 = (bf16[128,2048]{1,0:T(8,128)(2,1)S(1)}, bf16[128,2048]{1,0:T(8,128)(2,1)S(1)}, u32[]{:S(2)}, u32[]{:S(2)}) collective-permute-start(bf16[128,2048]{1,0:T(8,128)(2,1)S(1)} %get-tuple-element.111), channel_id=1, source_target_pairs={{0,8},{1,9},{2,10},{3,11},{4,12},{5,13},{6,14},{7,15},{8,0},{9,1},... | collective-permute-start | bytes 1572872 | tf_op jit(solution)/shard_map/ppermute | solution.py:50
  90.6 25.1 %collective-permute-start.15 = (bf16[256,2048]{1,0:T(8,128)(2,1)S(1)}, bf16[256,2048]{1,0:T(8,128)(2,1)S(1)}, u32[]{:S(2)}, u32[]{:S(2)}) collective-permute-start(bf16[256,2048]{1,0:T(8,128)(2,1)S(1)} %get-tuple-element.121), channel_id=1, source_target_pairs={{0,2},{1,3},{2,0},{3,1},{4,6},{5,7},{6,4},{7,5},{8,10},{9,11},{10,... | collective-permute-start | bytes 3145736 | tf_op jit(solution)/shard_map/ppermute | solution.py:50
  120.2 24.8 %collective-permute-start.14 = (bf16[1024,512]{1,0:T(8,128)(2,1)S(1)}, bf16[1024,512]{1,0:T(8,128)(2,1)S(1)}, u32[]{:S(2)}, u32[]{:S(2)}) collective-permute-start(bf16[1024,512]{1,0:T(8,128)(2,1)S(1)} %slice_bitcast_fusion), channel_id=1, source_target_pairs={{0,1},{1,0},{2,3},{3,2},{4,5},{5,4},{6,7},{7,6},{8,9},{9,8},{10,11... | collective-permute-start | bytes 3145736 | tf_op jit(solution)/shard_map/ppermute | solution.py:50
  176.4 25.5 %collective-permute-start.28 = (bf16[512,1024]{1,0:T(8,128)(2,1)}, bf16[512,1024]{1,0:T(8,128)(2,1)S(1)}, u32[]{:S(2)}, u32[]{:S(2)}) collective-permute-start(bf16[512,1024]{1,0:T(8,128)(2,1)} %get-tuple-element.132), channel_id=1, source_target_pairs={{0,2},{1,3},{2,0},{3,1},{4,6},{5,7},{6,4},{7,5},{8,10},{9,11},{10,... | collective-permute-start | bytes 3145736 | tf_op jit(solution)/shard_map/ppermute | solution.py:50
  177.4 25.1 %collective-permute-start.29 = (bf16[512,1024]{1,0:T(8,128)(2,1)}, bf16[512,1024]{1,0:T(8,128)(2,1)S(1)}, u32[]{:S(2)}, u32[]{:S(2)}) collective-permute-start(bf16[512,1024]{1,0:T(8,128)(2,1)} %get-tuple-element.134), channel_id=1, source_target_pairs={{0,4},{1,5},{2,6},{3,7},{4,0},{5,1},{6,2},{7,3},{8,12},{9,13},{10,... | collective-permute-start | bytes 3145736 | tf_op jit(solution)/shard_map/ppermute | solution.py:50
  202.6 30.7 %collective-permute-start.34 = (bf16[512,2048]{1,0:T(8,128)(2,1)}, bf16[512,2048]{1,0:T(8,128)(2,1)}, u32[]{:S(2)}, u32[]{:S(2)}) collective-permute-start(bf16[512,2048]{1,0:T(8,128)(2,1)} %get-tuple-element.146.refs_4_), channel_id=1, source_target_pairs={{0,1},{1,0},{2,3},{3,2},{4,5},{5,4},{6,7},{7,6},{8,9},{9,8},{10,11... | collective-permute-start | bytes 6291464 | tf_op jit(solution)/shard_map/ppermute | solution.py:50
  235.2 25.8 %collective-permute-start.36 = (bf16[128,2048]{1,0:T(8,128)(2,1)S(1)}, bf16[128,2048]{1,0:T(8,128)(2,1)S(1)}, u32[]{:S(2)}, u32[]{:S(2)}) collective-permute-start(bf16[128,2048]{1,0:T(8,128)(2,1)S(1)} %copy-done.61), channel_id=1, source_target_pairs={{0,20},{1,21},{2,22},{3,23},{4,16},{5,17},{6,18},{7,19},{8,28},{9,... | collective-permute-start | bytes 1572872 | tf_op jit(solution)/shard_map/ppermute | solution.py:50
  307.5 30.2 %collective-permute-start.52 = (bf16[128,2048]{1,0:T(8,128)(2,1)}, bf16[128,2048]{1,0:T(8,128)(2,1)S(1)}, u32[]{:S(2)}, u32[]{:S(2)}) collective-permute-start(bf16[128,2048]{1,0:T(8,128)(2,1)} %get-tuple-element.172), channel_id=1, source_target_pairs={{0,28},{1,29},{2,30},{3,31},{4,24},{5,25},{6,26},{7,27},{8,20},{9,... | collective-permute-start | bytes 1572872 | tf_op jit(solution)/shard_map/ppermute | solution.py:50
  309.9 26.6 %collective-permute-start.51 = (bf16[128,2048]{1,0:T(8,128)(2,1)S(1)}, bf16[128,2048]{1,0:T(8,128)(2,1)}, u32[]{:S(2)}, u32[]{:S(2)}) collective-permute-start(bf16[128,2048]{1,0:T(8,128)(2,1)S(1)} %bitcast_select_fusion.2), channel_id=1, source_target_pairs={{0,8},{1,9},{2,10},{3,11},{4,12},{5,13},{6,14},{7,15},{8,0},{9,1},... | collective-permute-start | bytes 1572872 | tf_op jit(solution)/shard_map/ppermute | solution.py:50
  310.9 26.8 %collective-permute-start.50 = (bf16[128,2048]{1,0:T(8,128)(2,1)S(1)}, bf16[128,2048]{1,0:T(8,128)(2,1)S(1)}, u32[]{:S(2)}, u32[]{:S(2)}) collective-permute-start(bf16[128,2048]{1,0:T(8,128)(2,1)S(1)} %collective-permute-done.40.refs_7_), channel_id=1, source_target_pairs={{0,1},{1,0},{2,3},{3,2},{4,5},{5,4},{6,7},{7,6},{8,9},{9,8},{10,11... | collective-permute-start | bytes 1572872 | tf_op jit(solution)/shard_map/ppermute | solution.py:50
  310.9 26.8 %collective-permute-start.49 = (bf16[128,2048]{1,0:T(8,128)(2,1)}, bf16[128,2048]{1,0:T(8,128)(2,1)}, u32[]{:S(2)}, u32[]{:S(2)}) collective-permute-start(bf16[128,2048]{1,0:T(8,128)(2,1)} %get-tuple-element.168), channel_id=1, source_target_pairs={{0,2},{1,3},{2,0},{3,1},{4,6},{5,7},{6,4},{7,5},{8,10},{9,11},{10,... | collective-permute-start | bytes 1572872 | tf_op jit(solution)/shard_map/ppermute | solution.py:50
  337.8 25.1 %collective-permute-start.57 = (bf16[256,2048]{1,0:T(8,128)(2,1)S(1)}, bf16[256,2048]{1,0:T(8,128)(2,1)S(1)}, u32[]{:S(2)}, u32[]{:S(2)}) collective-permute-start(bf16[256,2048]{1,0:T(8,128)(2,1)S(1)} %bitcast_select_fusion.1), channel_id=1, source_target_pairs={{0,4},{1,5},{2,6},{3,7},{4,0},{5,1},{6,2},{7,3},{8,12},{9,13},{10,... | collective-permute-start | bytes 3145736 | tf_op jit(solution)/shard_map/ppermute | solution.py:50
  342.2 30.2 %collective-permute-start.59 = (bf16[128,2048]{1,0:T(8,128)(2,1)}, bf16[128,2048]{1,0:T(8,128)(2,1)S(1)}, u32[]{:S(2)}, u32[]{:S(2)}) collective-permute-start(bf16[128,2048]{1,0:T(8,128)(2,1)} %get-tuple-element.183), channel_id=1, source_target_pairs={{0,16},{1,17},{2,18},{3,19},{4,20},{5,21},{6,22},{7,23},{8,24},{9,... | collective-permute-start | bytes 1572872 | tf_op jit(solution)/shard_map/ppermute | solution.py:50
  342.4 30.0 %collective-permute-start.58 = (bf16[128,2048]{1,0:T(8,128)(2,1)}, bf16[128,2048]{1,0:T(8,128)(2,1)}, u32[]{:S(2)}, u32[]{:S(2)}) collective-permute-start(bf16[128,2048]{1,0:T(8,128)(2,1)} %get-tuple-element.181), channel_id=1, source_target_pairs={{0,8},{1,9},{2,10},{3,11},{4,12},{5,13},{6,14},{7,15},{8,0},{9,1},... | collective-permute-start | bytes 1572872 | tf_op jit(solution)/shard_map/ppermute | solution.py:50
  (99 other events, 1788.3 us)
